TPU v7x, 32 devices: a whole 2x2x4 slice. The times are simulated.
32 devices in a mesh: gx: 2 (over x), gy: 4 (over y, core), gz: 4 (over z).
Axes of the slice: x: 2, y: 2, z: 4, core: 2. Of those that a mesh axis runs over, the one named last changes fastest.
Arguments:
- features: bfloat16 [2, 4, 4, 512, 128], P('gx', 'gy', 'gz'), may hold values from -6 to 6
- positions: float32 [2, 4, 4, 3, 512], P('gx', 'gy', 'gz'), may hold values from 0 to 1
- counts: int32 [2, 4, 4], P('gx', 'gy', 'gz'), may hold values from 256 to 512, as said below
- pair_first: int32 [2, 4, 4, 128, 128], P('gx', 'gy', 'gz'), may hold values from 0 to 511, as said below
- pair_second: int32 [2, 4, 4, 128, 128], P('gx', 'gy', 'gz'), may hold values from 0 to 13823, as said below
- pair_mask: int32 [2, 4, 4, 128, 128], P('gx', 'gy', 'gz'), may hold values from 0 to 1, as said below
- w_centre: bfloat16 [128, 256], replicated, may hold values from -0.5 to 0.5
- w_neighbour: bfloat16 [128, 256], replicated, may hold values from -0.5 to 0.5
- w_charge: bfloat16 [128], replicated, may hold values from -0.5 to 0.5
- w_radial: float32 [8, 256], replicated, may hold values from -3.5 to 3.5
- w_hidden: bfloat16 [256, 256], replicated, may hold values from -0.375 to 0.375
- w_energy: float32 [256], replicated, may hold values from -0.375 to 0.375
Outputs:
- forces: float32 [2, 4, 4, 3, 512], P('gx', 'gy', 'gz')
- charge_grad: float32 [2, 4, 4, 512], P('gx', 'gy', 'gz')
Inputs may be any that keep to these rules, and one draw needn't show every extreme that they name: `counts`: every brick holds at least half of its slots; some brick is full and some holds exactly half; the atoms present fill the lowest slots. `pair_first`: every listed pair names a present atom of its own brick. `pair_second`: every listed pair names a present atom of the image brick of its slot s (entry s * 512 + a); within slot 13 it differs from the pair's first atom. `pair_mask`: on every brick the tiles that hold a valid pair come before those that hold none; tile 0 always holds valid pairs.
All inputs are finite; a program needn't handle non-finite values.
Results may differ from a plain program's by a relative error of at most 0.0032.
Values may be sent and summed in bfloat16 or wider, within the bound.
A program may use at most 64 MiB of HBM per device.

v0:
```python
import jax
import jax.numpy as jnp
from jax import lax
from jax.sharding import PartitionSpec as P

delta_sq = 0.04
spread = 0.3
coulomb = 0.2
root_pi = 1.7724538509055159
block_tiles = 8


def with_halo(block, sides, width):
    for axis, dim in sides:
        count = lax.axis_size(axis)
        forward = [(i, i + 1) for i in range(count - 1)]
        forward.append((count - 1, 0))
        backward = [(target, source) for source, target in forward]
        low = lax.ppermute(
            lax.slice_in_dim(block, block.shape[dim] - width, None, axis=dim), axis, forward
        )
        high = lax.ppermute(lax.slice_in_dim(block, 0, width, axis=dim), axis, backward)
        block = jnp.concatenate([low, block, high], axis=dim)
    return block


def silu_parts(value):
    logistic = jax.nn.sigmoid(value)
    return (value * logistic, logistic * (1.0 + value * (1.0 - logistic)))


def shifted_coords(neighbours):
    steps_axis = jnp.arange(3, dtype=jnp.float32) - 1.0
    zero_grid = jnp.zeros((3, 3, 3), jnp.float32)
    shift_grid = jnp.stack(
        [
            steps_axis[:, None, None] + zero_grid,
            steps_axis[None, :, None] + zero_grid,
            steps_axis[None, None, :] + zero_grid,
            zero_grid,
        ],
        axis=3,
    )
    moved_grid = neighbours + shift_grid[..., None]
    return jnp.moveaxis(moved_grid, 3, 0).reshape(4, -1)


def pair_block(
    centre_proj,
    image_proj,
    coords_own,
    coords_all,
    pick_first,
    pick_second,
    pick_mask,
    w_radial,
    w_hidden,
    w_energy,
):
    rows_i = pick_first.reshape(-1)
    rows_j = pick_second.reshape(-1)
    weight = pick_mask.reshape(-1).astype(jnp.float32)
    place_i = coords_own[:3][:, rows_i]
    place_j = coords_all[:3][:, rows_j]
    charge_i = coords_own[3][rows_i]
    charge_j = coords_all[3][rows_j]
    separation = place_j - place_i
    dist_sq = jnp.sum(separation * separation, axis=0) + delta_sq
    distance = jnp.sqrt(dist_sq)
    centres = 0.25 + 0.3 * jnp.arange(w_radial.shape[0], dtype=jnp.float32)
    offset = distance[None, :] - centres[:, None]
    radial_basis = jnp.exp(-(offset / spread) * (offset / spread))
    radial = lax.dot_general(
        radial_basis, w_radial, (((0,), (0,)), ((), ())), precision=lax.Precision.HIGHEST
    )
    pre_one = (
        centre_proj[rows_i].astype(jnp.float32) + image_proj[rows_j].astype(jnp.float32) + radial
    )
    act_one, slope_one = silu_parts(pre_one)
    hidden = act_one.astype(jnp.bfloat16)
    pre_two = jnp.dot(hidden, w_hidden, preferred_element_type=jnp.float32)
    act_two, slope_two = silu_parts(pre_two)
    envelope = jnp.exp(-0.5 * dist_sq)
    readout = jnp.dot(act_two, w_energy, precision=lax.Precision.HIGHEST)
    back_two = (envelope[:, None] * w_energy[None, :] * slope_two).astype(jnp.bfloat16)
    back_one = (
        lax.dot_general(
            back_two, w_hidden, (((1,), (1,)), ((), ())), preferred_element_type=jnp.float32
        )
        * slope_one
    )
    back_basis = lax.dot_general(
        w_radial, back_one, (((1,), (1,)), ((), ())), precision=lax.Precision.HIGHEST
    )
    slope_nn = (
        jnp.sum(back_basis * radial_basis * (-2.0 * offset / (spread * spread)), axis=0)
        - readout * distance * envelope
    )
    screened = lax.erfc(distance)
    coulomb_pot = screened / distance
    slope_coul = -(2.0 / root_pi) * jnp.exp(-dist_sq) / distance - screened / dist_sq
    slope_all = weight * (slope_nn + coulomb * charge_i * charge_j * slope_coul)
    push_pair = separation * (slope_all / distance)[None, :]
    term_i = jnp.concatenate(
        [push_pair, (weight * coulomb * charge_j * coulomb_pot)[None, :]], axis=0
    )
    term_j = jnp.concatenate(
        [-push_pair, (weight * coulomb * charge_i * coulomb_pot)[None, :]], axis=0
    )
    return (rows_i, term_i, rows_j, term_j)


def brick_sum(
    centre_proj,
    image_proj,
    coords_own,
    coords_all,
    pair_first,
    pair_second,
    pair_mask,
    w_radial,
    w_hidden,
    w_energy,
    block_count,
):
    atom_slots = centre_proj.shape[0]

    def advance(index, summed):
        begin_row = index * block_tiles
        rows_i, term_i, rows_j, term_j = pair_block(
            centre_proj,
            image_proj,
            coords_own,
            coords_all,
            lax.dynamic_slice_in_dim(pair_first, begin_row, block_tiles, 0),
            lax.dynamic_slice_in_dim(pair_second, begin_row, block_tiles, 0),
            lax.dynamic_slice_in_dim(pair_mask, begin_row, block_tiles, 0),
            w_radial,
            w_hidden,
            w_energy,
        )
        summed = summed.at[13, :, rows_i].add(term_i.T)
        summed = summed.at[rows_j // atom_slots, :, rows_j % atom_slots].add(term_j.T)
        return summed

    start_sum = jnp.zeros((27, 4, atom_slots), jnp.float32)
    return lax.fori_loop(0, block_count, advance, start_sum)


def local(
    features,
    positions,
    counts,
    pair_first,
    pair_second,
    pair_mask,
    w_centre,
    w_neighbour,
    w_charge,
    w_radial,
    w_hidden,
    w_energy,
):
    own_feat = features[0, 0, 0]
    atom_slots = own_feat.shape[0]
    raw_charge = jnp.dot(own_feat, w_charge, preferred_element_type=jnp.float32)
    filled = counts[0, 0, 0]
    alive_slot = jnp.arange(atom_slots, dtype=jnp.int32) < filled
    average = jnp.sum(jnp.where(alive_slot, raw_charge, 0.0)) / filled.astype(jnp.float32)
    charges = jnp.where(alive_slot, raw_charge - average, 0.0)
    coords_own = jnp.concatenate([positions[0, 0, 0], charges[None, :]], axis=0)
    centre_proj = jnp.dot(own_feat, w_centre, preferred_element_type=jnp.float32).astype(
        jnp.bfloat16
    )
    neighbours = with_halo(coords_own[None, None, None], (("gx", 0), ("gy", 1), ("gz", 2)), 1)
    nearby = with_halo(features, (("gx", 0), ("gy", 1), ("gz", 2)), 1)
    image_proj = jnp.dot(
        nearby.reshape(27 * atom_slots, own_feat.shape[1]),
        w_neighbour,
        preferred_element_type=jnp.float32,
    ).astype(jnp.bfloat16)
    coords_all = shifted_coords(neighbours)
    first_tab = pair_first[0, 0, 0]
    second_tab = pair_second[0, 0, 0]
    mask_tab = pair_mask[0, 0, 0]
    busy_tiles = jnp.sum(jnp.any(mask_tab != 0, axis=1).astype(jnp.int32))
    block_count = (busy_tiles + block_tiles - 1) // block_tiles
    partial_value = brick_sum(
        centre_proj,
        image_proj,
        coords_own,
        coords_all,
        first_tab,
        second_tab,
        mask_tab,
        w_radial,
        w_hidden,
        w_energy,
        block_count,
    ).reshape(3, 3, 3, 4, atom_slots)
    padded = with_halo(partial_value, (("gx", 0), ("gy", 1), ("gz", 2)), 1)
    summed = jnp.sum(padded[0::2, 0::2, 0::2], axis=(0, 1, 2))
    return (summed[:3][None, None, None], summed[3][None, None, None])


def solution(mesh):
    placed = (
        P("gx", "gy", "gz", None, None),
        P("gx", "gy", "gz", None, None),
        P("gx", "gy", "gz"),
        P("gx", "gy", "gz", None, None),
        P("gx", "gy", "gz", None, None),
        P("gx", "gy", "gz", None, None),
        P(),
        P(),
        P(),
        P(),
        P(),
        P(),
    )
    return jax.shard_map(
        local,
        mesh=mesh,
        in_specs=placed,
        out_specs=(P("gx", "gy", "gz", None, None), P("gx", "gy", "gz", None)),
        check_vma=False,
    )
```

profile of v0, /device:TPU:0, one launch (start us, length us, event | category | flops | bytes accessed | tf_op | source)
XLA Modules:
  0.0 1184.3 jit_solution(4014743142093834373)
XLA Ops:
  36.2 43.7 %collective-permute-done.4 = f32[3,3,1,4,512]{4,3,2,1,0:T(4,128)S(1)} collective-permute-done((f32[3,3,1,4,512]{4,3,2,1,0:T(4,128)S(1)}, f32[3,3,1,4,512]{4,3,2,1,0:T(4,128)S(1)}, u32[]{:S(2)}, u32[]{:S(2)}) %collective-permute-start.4) | collective-permute-done | bytes 73760 | tf_op jit(solution)/shard_map/ppermute | solution.py:19
  95.3 463.0 %while.12 = (s32[]{:T(128)}, f32[27,4,512]{1,2,0:T(8,128)}, s32[]{:T(128)}, s32[128,128]{1,0:T(8,128)}, f32[4,13824]{0,1:T(8,128)}, /*index=5*/s32[128,128]{1,0:...) while((s32[]{:T(128)}, f32[27,4,512]{1,2,0:T(8,128)}, ...), condition=%wide.region_8.9_spmd, body=%wide.region_3.8_spmd.sunk | while | flops 330377216 | bytes 33843600 | solution.py:147
  105.3 7.4 gather_fusion.4
  131.3 6.9 gather_fusion
  138.9 11.2 scatter_fusion
  150.3 11.2 scatter_fusion.1
  171.4 7.4 gather_fusion.4
  197.4 6.9 gather_fusion
  205.0 11.2 scatter_fusion
  216.5 11.2 scatter_fusion.1
  237.5 7.4 gather_fusion.4
  263.5 6.9 gather_fusion
  271.1 11.2 scatter_fusion
  282.6 11.2 scatter_fusion.1
  303.7 7.4 gather_fusion.4
  329.7 6.9 gather_fusion
  337.2 11.2 scatter_fusion
  348.7 11.2 scatter_fusion.1
  369.8 7.4 gather_fusion.4
  403.3 11.2 scatter_fusion
  414.8 11.2 scatter_fusion.1
  435.9 7.4 gather_fusion.4
  461.9 6.9 gather_fusion
  469.4 11.2 scatter_fusion
  480.9 11.2 scatter_fusion.1
  502.0 7.4 gather_fusion.4
  528.0 6.9 gather_fusion
  535.5 11.2 scatter_fusion
  547.0 11.2 scatter_fusion.1
  572.5 396.6 %collective-permute-start.15 = (f32[5,1,3,4,512]{4,3,2,1,0:T(4,128)S(1)}, f32[5,1,3,4,512]{4,3,2,1,0:T(4,128)S(1)}, u32[]{:S(2)}, u32[]{:S(2)}) collective-permute-start(f32[5,1,3,4,512]{4,3,2,1,0:T(4,128)S(1)} %get-tuple-element.281), channel_id=1, source_target_pairs={{4,0},{8,4},{12,8},{0,12},{5,1},{9,5},{13,9},{1,13},{6,2},{10,6},{... | collective-permute-start | bytes 368648 | tf_op jit(solution)/shard_map/ppermute | solution.py:22
  972.3 68.1 %collective-permute-start.16 = (f32[5,5,1,4,512]{4,3,2,1,0:T(4,128)S(1)}, f32[5,5,1,4,512]{4,3,2,1,0:T(4,128)S(1)}, u32[]{:S(2)}, u32[]{:S(2)}) collective-permute-start(f32[5,5,1,4,512]{4,3,2,1,0:T(4,128)S(1)} %get-tuple-element.278), channel_id=1, source_target_pairs={{0,1},{1,2},{2,3},{3,0},{4,5},{5,6},{6,7},{7,4},{8,9},{9,10},{10,1... | collective-permute-start | bytes 614408 | tf_op jit(solution)/shard_map/ppermute | solution.py:19
  1040.4 132.1 %collective-permute-start.17 = (f32[5,5,1,4,512]{4,3,2,1,0:T(4,128)S(1)}, f32[5,5,1,4,512]{4,3,2,1,0:T(4,128)S(1)}, u32[]{:S(2)}, u32[]{:S(2)}) collective-permute-start(f32[5,5,1,4,512]{4,3,2,1,0:T(4,128)S(1)} %get-tuple-element.279), channel_id=1, source_target_pairs={{1,0},{2,1},{3,2},{0,3},{5,4},{6,5},{7,6},{4,7},{9,8},{10,9},{11,1... | collective-permute-start | bytes 614408 | tf_op jit(solution)/shard_map/ppermute | solution.py:22
  (357 shorter events, 289.1 us)
Async XLA Ops:
  0.6 86.0 %copy-start = (bf16[128,256]{1,0:T(8,128)(2,1)S(1)}, bf16[128,256]{1,0:T(8,128)(2,1)}, u32[]{:S(2)}) copy-start(bf16[128,256]{1,0:T(8,128)(2,1)} %param.21) | copy-start | bytes 196612
  0.6 28.7 %copy-start.2 = (s32[1,1,1,128,128]{4,3,2,1,0:T(8,128)S(1)}, s32[1,1,1,128,128]{4,3,2,1,0:T(8,128)}, u32[]{:S(2)}) copy-start(s32[1,1,1,128,128]{4,3,2,1,0:T(8,128)} %param.19) | copy-start | bytes 196612
  0.7 7.5 collective-permute-start.6
  3.7 6.5 collective-permute-start.7
  10.2 9.3 collective-permute-start.8
  10.3 10.7 collective-permute-start.9
  13.3 14.2 %collective-permute-start = (f32[1,1,1,4,512]{4,3,2,1,0:T(4,128)S(1)}, f32[1,1,1,4,512]{4,3,2,1,0:T(4,128)S(1)}, u32[]{:S(2)}, u32[]{:S(2)}) collective-permute-start(f32[1,1,1,4,512]{4,3,2,1,0:T(4,128)S(1)} %maximum_bitcast_fusion.2), channel_id=1, source_target_pairs={{0,16},{16,0},{1,17},{17,1},{2,18},{18,2},{3,19},{19,3},{4,20},{20... | collective-permute-start | bytes 24584 | tf_op jit(solution)/shard_map/ppermute | solution.py:19
  15.1 12.4 %collective-permute-start.1 = (f32[1,1,1,4,512]{4,3,2,1,0:T(4,128)S(1)}, f32[1,1,1,4,512]{4,3,2,1,0:T(4,128)S(1)}, u32[]{:S(2)}, u32[]{:S(2)}) collective-permute-start(f32[1,1,1,4,512]{4,3,2,1,0:T(4,128)S(1)} %maximum_bitcast_fusion.2), channel_id=1, source_target_pairs={{16,0},{0,16},{17,1},{1,17},{18,2},{2,18},{19,3},{3,19},{20,4},{4,... | collective-permute-start | bytes 24584 | tf_op jit(solution)/shard_map/ppermute | solution.py:22
  22.1 63.0 %collective-permute-start.10 = (bf16[3,3,1,512,128]{4,3,2,1,0:T(8,128)(2,1)}, bf16[3,3,1,512,128]{4,3,2,1,0:T(8,128)(2,1)S(1)}, u32[]{:S(2)}, u32[]{:S(2)}) collective-permute-start(bf16[3,3,1,512,128]{4,3,2,1,0:T(8,128)(2,1)} %pad_maximum_fusion.1), channel_id=1, source_target_pairs={{0,1},{1,2},{2,3},{3,0},{4,5},{5,6},{6,7},{7,4},{8,9},{9,10},{10,1... | collective-permute-start | bytes 3538952 | tf_op jit(solution)/shard_map/ppermute | solution.py:19
  23.7 61.4 %collective-permute-start.11 = (bf16[3,3,1,512,128]{4,3,2,1,0:T(8,128)(2,1)}, bf16[3,3,1,512,128]{4,3,2,1,0:T(8,128)(2,1)}, u32[]{:S(2)}, u32[]{:S(2)}) collective-permute-start(bf16[3,3,1,512,128]{4,3,2,1,0:T(8,128)(2,1)} %pad_maximum_fusion.1), channel_id=1, source_target_pairs={{1,0},{2,1},{3,2},{0,3},{5,4},{6,5},{7,6},{4,7},{9,8},{10,9},{11,1... | collective-permute-start | bytes 3538952 | tf_op jit(solution)/shard_map/ppermute | solution.py:22
  27.5 3.3 collective-permute-start.2
  27.8 3.0 collective-permute-start.3
  30.8 49.1 %collective-permute-start.4 = (f32[3,3,1,4,512]{4,3,2,1,0:T(4,128)S(1)}, f32[3,3,1,4,512]{4,3,2,1,0:T(4,128)S(1)}, u32[]{:S(2)}, u32[]{:S(2)}) collective-permute-start(f32[3,3,1,4,512]{4,3,2,1,0:T(4,128)S(1)} %pad_maximum_fusion.11), channel_id=1, source_target_pairs={{0,1},{1,2},{2,3},{3,0},{4,5},{5,6},{6,7},{7,4},{8,9},{9,10},{10,1... | collective-permute-start | bytes 221192 | tf_op jit(solution)/shard_map/ppermute | solution.py:19
  30.9 49.8 %collective-permute-start.5 = (f32[3,3,1,4,512]{4,3,2,1,0:T(4,128)S(1)}, f32[3,3,1,4,512]{4,3,2,1,0:T(4,128)S(1)}, u32[]{:S(2)}, u32[]{:S(2)}) collective-permute-start(f32[3,3,1,4,512]{4,3,2,1,0:T(4,128)S(1)} %pad_maximum_fusion.11), channel_id=1, source_target_pairs={{1,0},{2,1},{3,2},{0,3},{5,4},{6,5},{7,6},{4,7},{9,8},{10,9},{11,1... | collective-permute-start | bytes 221192 | tf_op jit(solution)/shard_map/ppermute | solution.py:22
  91.6 3.6 copy-start.1
  91.6 3.6 copy-start.3
  91.6 3.6 copy-start.4
  91.6 3.6 copy-start.5
  91.6 3.6 copy-start.6
  118.2 3.1 slice-start.1
  184.3 3.1 slice-start.1
  250.4 3.1 slice-start.1
  316.6 3.1 slice-start.1
  382.7 3.1 slice-start.1
  448.8 3.1 slice-start.1
  514.9 3.1 slice-start.1
  564.8 7.5 collective-permute-start.12
  565.5 6.8 collective-permute-start.13
  572.4 399.8 %collective-permute-start.14 = (f32[5,1,3,4,512]{4,3,2,1,0:T(4,128)S(1)}, f32[5,1,3,4,512]{4,3,2,1,0:T(4,128)S(1)}, u32[]{:S(2)}, u32[]{:S(2)}) collective-permute-start(f32[5,1,3,4,512]{4,3,2,1,0:T(4,128)S(1)} %get-tuple-element.280), channel_id=1, source_target_pairs={{0,4},{4,8},{8,12},{12,0},{1,5},{5,9},{9,13},{13,1},{2,6},{6,10},{... | collective-permute-start | bytes 368648 | tf_op jit(solution)/shard_map/ppermute | solution.py:19
  572.5 399.8 %collective-permute-start.15 = (f32[5,1,3,4,512]{4,3,2,1,0:T(4,128)S(1)}, f32[5,1,3,4,512]{4,3,2,1,0:T(4,128)S(1)}, u32[]{:S(2)}, u32[]{:S(2)}) collective-permute-start(f32[5,1,3,4,512]{4,3,2,1,0:T(4,128)S(1)} %get-tuple-element.281), channel_id=1, source_target_pairs={{4,0},{8,4},{12,8},{0,12},{5,1},{9,5},{13,9},{1,13},{6,2},{10,6},{... | collective-permute-start | bytes 368648 | tf_op jit(solution)/shard_map/ppermute | solution.py:22
  972.3 203.9 %collective-permute-start.16 = (f32[5,5,1,4,512]{4,3,2,1,0:T(4,128)S(1)}, f32[5,5,1,4,512]{4,3,2,1,0:T(4,128)S(1)}, u32[]{:S(2)}, u32[]{:S(2)}) collective-permute-start(f32[5,5,1,4,512]{4,3,2,1,0:T(4,128)S(1)} %get-tuple-element.278), channel_id=1, source_target_pairs={{0,1},{1,2},{2,3},{3,0},{4,5},{5,6},{6,7},{7,4},{8,9},{9,10},{10,1... | collective-permute-start | bytes 614408 | tf_op jit(solution)/shard_map/ppermute | solution.py:19
  1040.4 142.1 %collective-permute-start.17 = (f32[5,5,1,4,512]{4,3,2,1,0:T(4,128)S(1)}, f32[5,5,1,4,512]{4,3,2,1,0:T(4,128)S(1)}, u32[]{:S(2)}, u32[]{:S(2)}) collective-permute-start(f32[5,5,1,4,512]{4,3,2,1,0:T(4,128)S(1)} %get-tuple-element.279), channel_id=1, source_target_pairs={{1,0},{2,1},{3,2},{0,3},{5,4},{6,5},{7,6},{4,7},{9,8},{10,9},{11,1... | collective-permute-start | bytes 614408 | tf_op jit(solution)/shard_map/ppermute | solution.py:22
  (7 other events, 21.2 us)
where the time goes:
time: 1190 us; the launch traced here: 1180 us
  starting transfers between devices  615 us (52%)
  local copies, waits for them, and re-layouts  292 us (25%)
  other arithmetic  166 us (14%)
  waiting for transfers between devices  67.9 us (6%)
  matrix products  38.8 us (3%)
    ppermute x9, starting transfers between devices, with_halo(): lax.ppermute(lax.slice_in_dim(block, 0, width, axis=dim), axis, backward)  540 us
    while x49, other arithmetic  159 us
    ppermute x9, starting transfers between devices, with_halo(): lax.ppermute(lax.slice_in_dim(block, block.shape[dim] - width, None, axis...  75 us
    ppermute x9, waiting for transfers between devices, with_halo(): lax.ppermute(lax.slice_in_dim(block, block.shape[dim] - width, None, axis...  58.4 us
    gather x7, local copies, waits for them, and re-layouts, pair_block(): image_proj[rows_j].astype(jnp.float32)  51.7 us
    gather x7, local copies, waits for them, and re-layouts, pair_block(): charge_i = coords_own[3][rows_i]  48.1 us
    gather x7, local copies, waits for them, and re-layouts, pair_block(): charge_j = coords_all[3][rows_j]  43.1 us
    gather x14, local copies, waits for them, and re-layouts, pair_block(): place_j = coords_all[:3][:, rows_j]  42 us
  transfers between devices with their start and end apart: 18, of which 10 were waited for; matrix products, arithmetic and copies ran while one was open for 1% of the time, Pallas kernels for 0%

commit v1 on v0

v1 whole, which is shorter than its diff:
```python
import functools

import jax
import jax.numpy as jnp
from jax import lax
from jax.experimental import pallas as pl
from jax.experimental.pallas import tpu as pltpu
from jax.sharding import PartitionSpec as P

delta_sq = 0.04
spread = 0.3
coulomb = 0.2
root_pi = 1.7724538509055159
part_rows = 16
erfc_terms = (
    0.17087277,
    -0.82215223,
    1.48851587,
    -1.13520398,
    0.27886807,
    -0.18628806,
    0.09678418,
    0.37409196,
    1.00002368,
    -1.26551223,
)


def ring(axis, step):
    count = lax.axis_size(axis)
    return [(i, (i + step) % count) for i in range(count)]


def widen(block, axis):
    parts = [block, lax.ppermute(block, axis, ring(axis, -1))]
    if lax.axis_size(axis) > 2:
        parts.append(lax.ppermute(block, axis, ring(axis, 1)))
    return parts


def fold(blocks, axis):
    total = blocks[0] + lax.ppermute(blocks[1], axis, ring(axis, 1))
    if len(blocks) > 2:
        total = total + lax.ppermute(blocks[2], axis, ring(axis, -1))
    return total


def rounded(value):
    return lax.reduce_precision(value, 8, 7)


def three_parts(value):
    high = rounded(value)
    middle = rounded(value - high)
    return [high, middle, rounded(value - high - middle)]


def lower(left, right):
    return jnp.dot(left, right, preferred_element_type=jnp.float32)


def pair_kernel(
    width,
    plan_ref,
    pairs_ref,
    *refs,
):
    (
        *table_refs,
        to_centre_ref,
        to_image_ref,
        radial_cat_ref,
        radial_two_ref,
        hidden_ref,
        hidden_t_ref,
        energy_ref,
        out_ref,
        centre_ref,
        image_ref,
        pre_ref,
        sum_i_ref,
        sum_j_ref,
    ) = refs
    atoms = centre_ref.shape[1]
    lanes = pairs_ref.shape[2]
    hid = hidden_ref.shape[0]
    cuts = atoms // width

    centre_ref[...] = lower(to_centre_ref[...], table_refs[0][0]).astype(jnp.bfloat16)
    begin = 0
    for table_ref in table_refs:
        def project(index, carry, table_ref=table_ref, begin=begin):
            image = lower(to_image_ref[...], table_ref[index]).astype(jnp.bfloat16)
            for cut in range(cuts):
                image_ref[(begin + index) * cuts + cut] = image[:, cut * width : (cut + 1) * width]
            return carry

        lax.fori_loop(0, table_ref.shape[0], project, 0)
        begin += table_ref.shape[0]
    sum_i_ref[...] = jnp.zeros_like(sum_i_ref)
    sum_j_ref[...] = jnp.zeros_like(sum_j_ref)

    def pick(rows, entries):
        spot = lax.broadcasted_iota(jnp.int32, (rows, lanes), 0)
        return jnp.where(spot == entries, 1.0, 0.0).astype(jnp.bfloat16)

    def step(block, carry):
        listed = pairs_ref[block]
        first = listed[0:1]
        second = listed[1:2]
        offset_x = listed[2:3].astype(jnp.float32)
        offset_y = listed[3:4].astype(jnp.float32)
        offset_z = listed[4:5].astype(jnp.float32)
        weight = listed[5:6].astype(jnp.float32)
        least = plan_ref[2 * block + 1]
        most = plan_ref[2 * block + 2]
        pick_i = pick(atoms, first)
        pre_ref[...] = lower(centre_ref[...], pick_i)

        def gather(window, carry):
            pre_ref[...] += lower(image_ref[window], pick(width, second - window * width))
            return carry

        lax.fori_loop(least, most + 1, gather, 0)
        extra = pre_ref[hid:, :]
        sep_x = (extra[0:1] + extra[3:4]) + extra[6:7] + offset_x
        sep_y = (extra[1:2] + extra[4:5]) + extra[7:8] + offset_y
        sep_z = (extra[2:3] + extra[5:6]) + extra[8:9] + offset_z
        charge_i = extra[9:10] + extra[10:11] + extra[11:12]
        charge_j = extra[12:13] + extra[13:14] + extra[14:15]
        dist_sq = sep_x * sep_x + sep_y * sep_y + sep_z * sep_z + delta_sq
        distance = jnp.sqrt(dist_sq)
        inverse = 1.0 / distance
        envelope = jnp.exp(-0.5 * dist_sq)
        basis_count = radial_two_ref.shape[0] // 2
        order = lax.broadcasted_iota(jnp.int32, (basis_count, lanes), 0).astype(jnp.float32)
        offset = distance - (0.25 + 0.3 * order)
        basis = jnp.exp(-(offset / spread) * (offset / spread))
        basis_high = basis.astype(jnp.bfloat16).astype(jnp.float32)
        basis_cat = jnp.concatenate(
            [basis_high, basis - basis_high, basis_high, jnp.zeros_like(basis)], axis=0
        ).astype(jnp.bfloat16)
        pre_one = pre_ref[:hid, :] + lower(radial_cat_ref[...], basis_cat)
        gate_one = 0.5 * jnp.tanh(0.5 * pre_one) + 0.5
        act_one = pre_one * gate_one
        slope_one = gate_one + act_one * (1.0 - gate_one)
        pre_two = lower(hidden_t_ref[...], act_one.astype(jnp.bfloat16))
        gate_two = 0.5 * jnp.tanh(0.5 * pre_two) + 0.5
        scaled = energy_ref[...] * gate_two
        scaled_act = pre_two * scaled
        readout = jnp.sum(scaled_act, axis=0, keepdims=True)
        back_two = (envelope * (scaled + scaled_act * (1.0 - gate_two))).astype(jnp.bfloat16)
        back_one = lower(hidden_ref[...], back_two) * slope_one
        back_high = back_one.astype(jnp.bfloat16)
        back_low = (back_one - back_high.astype(jnp.float32)).astype(jnp.bfloat16)
        from_high = lower(radial_two_ref[...], back_high)
        from_low = lower(radial_two_ref[...], back_low)
        back_basis = from_high[:basis_count] + from_high[basis_count:] + from_low[:basis_count]
        slope_nn = (
            jnp.sum(
                back_basis * basis * (offset * (-2.0 / (spread * spread))), axis=0, keepdims=True
            )
            - readout * distance * envelope
        )
        ratio = 1.0 / (1.0 + 0.5 * distance)
        series = jnp.full_like(ratio, erfc_terms[0])
        for term in erfc_terms[1:]:
            series = series * ratio + term
        screened = ratio * jnp.exp(series - distance * distance)
        potential = screened * inverse
        slope_coul = -(2.0 / root_pi) * jnp.exp(-dist_sq) * inverse - potential * inverse
        slope = weight * (slope_nn + coulomb * charge_i * charge_j * slope_coul) * inverse
        push_x = slope * sep_x
        push_y = slope * sep_y
        push_z = slope * sep_z
        shared = weight * coulomb * potential
        terms = jnp.concatenate(
            [
                push_x,
                push_y,
                push_z,
                shared * charge_j,
                -push_x,
                -push_y,
                -push_z,
                shared * charge_i,
            ],
            axis=0,
        )
        terms_high = terms.astype(jnp.bfloat16).astype(jnp.float32)
        both = jnp.concatenate([terms_high, terms - terms_high], axis=0).astype(jnp.bfloat16)
        across = (((1,), (1,)), ((), ()))
        sum_i_ref[...] += lax.dot_general(
            both, pick_i, across, preferred_element_type=jnp.float32
        )

        def scatter(window, carry):
            sum_j_ref[window] += lax.dot_general(
                both,
                pick(width, second - window * width),
                across,
                preferred_element_type=jnp.float32,
            )
            return carry

        lax.fori_loop(least, most + 1, scatter, 0)
        return carry

    lax.fori_loop(0, plan_ref[0], step, 0)

    def finish(index, carry):
        for cut in range(cuts):
            total = sum_j_ref[index * cuts + cut]
            out_ref[index, :, cut * width : (cut + 1) * width] = total[4:8] + total[12:16]
        return carry

    lax.fori_loop(0, out_ref.shape[0], finish, 0)
    out_ref[0] += sum_i_ref[0:4, :] + sum_i_ref[8:12, :]


def local(
    features,
    positions,
    counts,
    pair_first,
    pair_second,
    pair_mask,
    w_centre,
    w_neighbour,
    w_charge,
    w_radial,
    w_hidden,
    w_energy,
):
    own_feat = features[0, 0, 0]
    atoms, feat = own_feat.shape
    hid = w_hidden.shape[0]
    spans = [min(3, lax.axis_size(axis)) for axis in ("gx", "gy", "gz")]
    raw_charge = jnp.dot(own_feat, w_charge, preferred_element_type=jnp.float32)
    filled = counts[0, 0, 0]
    alive_slot = jnp.arange(atoms, dtype=jnp.int32) < filled
    average = jnp.sum(jnp.where(alive_slot, raw_charge, 0.0)) / filled.astype(jnp.float32)
    charges = jnp.where(alive_slot, raw_charge - average, 0.0)
    own = jnp.concatenate(
        three_parts(positions[0, 0, 0])
        + three_parts(charges[None, :])
        + [jnp.zeros((part_rows - 12, atoms), jnp.float32)],
        axis=0,
    ).astype(jnp.bfloat16)
    own = jnp.concatenate([own_feat.T, own], axis=0)

    column = jnp.stack(widen(own, "gz"))
    plane = jnp.concatenate(widen(column, "gx"))
    tables = widen(plane, "gy")

    entry = pair_second[0, 0, 0].reshape(-1)
    slot = entry // atoms
    steps = (slot // 9 - 1, slot // 3 % 3 - 1, slot % 3 - 1)
    place = [jnp.where(step < 0, span - 1, step) for step, span in zip(steps, spans)]
    brick = (place[1] * spans[0] + place[0]) * spans[2] + place[2]
    bricks = spans[0] * spans[1] * spans[2]
    sign = ((steps[0] + 1) * 3 + steps[1] + 1) * 3 + steps[2] + 1
    key = ((brick * atoms + entry % atoms) * atoms + pair_first[0, 0, 0].reshape(-1)) * 27 + sign
    mask = pair_mask[0, 0, 0].reshape(-1) != 0
    key = jnp.where(mask, key, bricks * atoms * atoms * 27)
    key = lax.sort(key, is_stable=False)
    valid = jnp.sum(mask.astype(jnp.int32))
    lanes = 512 if key.shape[0] % 512 == 0 else 128
    width = 256 if atoms % 256 == 0 else 128
    blocks = key.shape[0] // lanes
    key = key.reshape(blocks, lanes)
    sign = key % 27
    second = key // (27 * atoms)
    rows = [
        key // 27 % atoms,
        second,
        sign // 9 - 1,
        sign // 3 % 3 - 1,
        sign % 3 - 1,
        (second < bricks * atoms).astype(jnp.int32),
    ]
    rows = rows + [jnp.zeros_like(key)] * 2
    listed = jnp.stack(rows, axis=1)
    window = jnp.minimum(second // width, bricks * atoms // width - 1)
    live = (valid + lanes - 1) // lanes
    plan = jnp.concatenate(
        [live[None], jnp.stack([window[:, 0], jnp.max(window, axis=1)], axis=1).reshape(-1)]
    ).astype(jnp.int32)

    carry_j = [[0.0] * part_rows for _ in range(part_rows)]
    carry_i = [[0.0] * part_rows for _ in range(part_rows)]
    for part in range(9):
        carry_j[part][part] = 1.0
        carry_i[part][part] = -1.0
    for part in range(3):
        carry_i[9 + part][9 + part] = 1.0
        carry_j[12 + part][9 + part] = 1.0

    def with_parts(weight, carried):
        top = jnp.concatenate([weight.T, jnp.zeros((hid, part_rows), jnp.bfloat16)], axis=1)
        bottom = jnp.concatenate(
            [jnp.zeros((part_rows, feat), jnp.bfloat16), jnp.array(carried, jnp.bfloat16)], axis=1
        )
        return jnp.concatenate([top, bottom], axis=0)

    radial_high = rounded(w_radial)
    radial_low = w_radial - radial_high
    radial_cat = jnp.concatenate(
        [radial_high, radial_high, radial_low, jnp.zeros_like(w_radial)], axis=0
    ).T.astype(jnp.bfloat16)
    radial_two = jnp.concatenate([radial_high, radial_low], axis=0).astype(jnp.bfloat16)

    vmem = pl.BlockSpec(memory_space=pltpu.VMEM)
    operands = [listed, *tables]
    operands += [with_parts(w_centre, carry_i), with_parts(w_neighbour, carry_j)]
    operands += [radial_cat, radial_two, w_hidden, w_hidden.T, w_energy[:, None]]
    windows = bricks * atoms // width
    partial = pl.pallas_call(
        functools.partial(pair_kernel, width),
        out_shape=jax.ShapeDtypeStruct((bricks, 4, atoms), jnp.float32),
        in_specs=[pl.BlockSpec(memory_space=pltpu.SMEM)] + [vmem] * len(operands),
        out_specs=vmem,
        scratch_shapes=[
            pltpu.VMEM((hid + part_rows, atoms), jnp.bfloat16),
            pltpu.VMEM((windows, hid + part_rows, width), jnp.bfloat16),
            pltpu.VMEM((hid + part_rows, lanes), jnp.float32),
            pltpu.VMEM((16, atoms), jnp.float32),
            pltpu.VMEM((windows, 16, width), jnp.float32),
        ],
        compiler_params=pltpu.CompilerParams(vmem_limit_bytes=48 * 1024 * 1024),
        name="pairs",
    )(plan, *operands)
    partial = partial.reshape(spans[1], spans[0], spans[2], 4, atoms)
    partial = fold(partial, "gy")
    partial = fold(partial, "gx")
    summed = fold(partial, "gz")
    return (summed[:3][None, None, None], summed[3][None, None, None])


def solution(mesh):
    placed = (
        P("gx", "gy", "gz", None, None),
        P("gx", "gy", "gz", None, None),
        P("gx", "gy", "gz"),
        P("gx", "gy", "gz", None, None),
        P("gx", "gy", "gz", None, None),
        P("gx", "gy", "gz", None, None),
        P(),
        P(),
        P(),
        P(),
        P(),
        P(),
    )
    return jax.shard_map(
        local,
        mesh=mesh,
        in_specs=placed,
        out_specs=(P("gx", "gy", "gz", None, None), P("gx", "gy", "gz", None)),
        check_vma=False,
    )
```

time: 1190 us -> 143 us (0.12)
  starting transfers between devices: 615 us -> 61.5 us
  local copies, waits for them, and re-layouts: 292 us -> 10.4 us
  other arithmetic: 166 us -> 13.8 us
  waiting for transfers between devices: 67.9 us -> 24.5 us
  matrix products: 38.8 us -> 0.13 us
  Pallas kernels: 0 us -> 29.9 us
    ppermute x18 -> x10, starting transfers between devices: 615 us -> 61.5 us  [the longest x2 51 us: fold(): total = total + lax.ppermute(blocks[2], axis, ring(axis, -1))]
    gather x56 -> x0, local copies, waits for them, and re-layouts: 233 us -> none  [the longest x7 51.7 us: pair_block(): image_proj[rows_j].astype(jnp.float32)]
    while x49 -> x0, other arithmetic: 159 us -> none
    ppermute x18 -> x10, waiting for transfers between devices: 67.9 us -> 24.5 us  [the longest x3 10 us: widen(): parts = [block, lax.ppermute(block, axis, ring(axis, -1))]]
    dot_general x37 -> x0, matrix products: 37.7 us -> none  [the longest x7 8.4 us: pair_block(): readout = jnp.dot(act_two, w_energy, precision=lax.Precision.HIGHEST)]
    slice x10 -> x2, local copies, waits for them, and re-layouts: 34.1 us -> 0.02 us  [the longest x1 0.01 us: fold(): total = blocks[0] + lax.ppermute(blocks[1], axis, ring(axis, 1))]
    pallas_call x0 -> x1, Pallas kernels: none -> 29.9 us  [local(): pl.pallas_call(functools.partial(pair_kernel, width), out_shape=jax.Shape...]
  transfers between devices with their start and end apart: 18 -> 10, of which waited for: 10 -> 7; matrix products, arithmetic and copies ran while one was open for 1% -> 13% of each run, Pallas kernels for 0% -> 0%
where the time goes in v1:
time: 143 us
  starting transfers between devices  61.5 us (43%)
  Pallas kernels  29.9 us (21%)
  waiting for transfers between devices  24.5 us (17%)
  other arithmetic  13.8 us (10%)
  local copies, waits for them, and re-layouts  10.4 us (7%)
  between operations  2.97 us (2%)
    ppermute x2, starting transfers between devices, fold(): total = total + lax.ppermute(blocks[2], axis, ring(axis, -1))  51 us
    pallas_call x1, Pallas kernels, local(): pl.pallas_call(functools.partial(pair_kernel, width), out_shape=jax.Shape...  29.9 us
    ppermute x3, waiting for transfers between devices, widen(): parts = [block, lax.ppermute(block, axis, ring(axis, -1))]  10 us
    ppermute x2, waiting for transfers between devices, widen(): parts.append(lax.ppermute(block, axis, ring(axis, 1)))  7.14 us
    sort x1, other arithmetic, local(): key = lax.sort(key, is_stable=False)  6.29 us
    unnamed x36, local copies, waits for them, and re-layouts  6.09 us
    ppermute x3, waiting for transfers between devices, fold(): total = blocks[0] + lax.ppermute(blocks[1], axis, ring(axis, 1))  5.58 us
    ppermute x3, starting transfers between devices, widen(): parts = [block, lax.ppermute(block, axis, ring(axis, -1))]  5.54 us
  transfers between devices with their start and end apart: 10, of which 7 were waited for; matrix products, arithmetic and copies ran while one was open for 13% of the time, Pallas kernels for 0%

profile of v1, /device:TPU:0, one launch (start us, length us, event | category | flops | bytes accessed | tf_op | source)
XLA Modules:
  0.0 143.2 jit_solution(13448964387207248129)
XLA Ops:
  1.3 1.1 copy.47
  2.5 0.6 select_reduce_fusion
  3.9 0.6 copy-done.14
  4.7 3.1 %collective-permute-start.1 = (bf16[144,512]{1,0:T(8,128)(2,1)S(1)}, bf16[144,512]{1,0:T(8,128)(2,1)S(1)}, u32[]{:S(2)}, u32[]{:S(2)}) collective-permute-start(bf16[144,512]{1,0:T(8,128)(2,1)S(1)} %concatenate.40), channel_id=1, source_target_pairs={{0,1},{1,2},{2,3},{3,0},{4,5},{5,6},{6,7},{7,4},{8,9},{9,10},{10,1... | collective-permute-start | bytes 442376 | tf_op jit(solution)/shard_map/ppermute | solution.py:37
  7.8 2.1 %collective-permute-start = (bf16[144,512]{1,0:T(8,128)(2,1)S(1)}, bf16[144,512]{1,0:T(8,128)(2,1)S(1)}, u32[]{:S(2)}, u32[]{:S(2)}) collective-permute-start(bf16[144,512]{1,0:T(8,128)(2,1)S(1)} %concatenate.40), channel_id=1, source_target_pairs={{0,3},{1,0},{2,1},{3,2},{4,7},{5,4},{6,5},{7,6},{8,11},{9,8},{10,9... | collective-permute-start | bytes 442376 | tf_op jit(solution)/shard_map/ppermute | solution.py:35
  9.9 0.6 convert_reduce_fusion
  10.8 6.3 %sort.7 = s32[16384]{0:T(1024)S(1)} sort(s32[16384]{0:T(1024)S(1)} %fusion.14), dimensions={0}, to_apply=%region_1.2 | sort | flops 229376 | bytes 131072 | tf_op jit(solution)/shard_map/sort | solution.py:266
  17.2 0.7 broadcast_remainder_fusion
  19.0 1.7 %collective-permute-start.2 = (bf16[3,144,512]{2,1,0:T(8,128)(2,1)S(1)}, bf16[3,144,512]{2,1,0:T(8,128)(2,1)S(1)}, u32[]{:S(2)}, u32[]{:S(2)}) collective-permute-start(bf16[3,144,512]{2,1,0:T(8,128)(2,1)S(1)} %pad_maximum_fusion.1), channel_id=1, source_target_pairs={{0,16},{16,0},{1,17},{17,1},{2,18},{18,2},{3,19},{19,3},{4,20},{20... | collective-permute-start | bytes 1327112 | tf_op jit(solution)/shard_map/ppermute | solution.py:35
  20.8 0.8 compare_convert_fusion
  21.7 9.1 %collective-permute-done.2 = bf16[3,144,512]{2,1,0:T(8,128)(2,1)S(1)} collective-permute-done((bf16[3,144,512]{2,1,0:T(8,128)(2,1)S(1)}, bf16[3,144,512]{2,1,0:T(8,128)(2,1)S(1)}, u32[]{:S(2)}, u32[]{:S(2)}) %collective-permute-start.2) | collective-permute-done | bytes 442400 | tf_op jit(solution)/shard_map/ppermute | solution.py:35
  30.9 1.7 %collective-permute-start.3 = (bf16[6,144,512]{2,1,0:T(8,128)(2,1)S(1)}, bf16[6,144,512]{2,1,0:T(8,128)(2,1)S(1)}, u32[]{:S(2)}, u32[]{:S(2)}) collective-permute-start(bf16[6,144,512]{2,1,0:T(8,128)(2,1)S(1)} %pad_maximum_fusion.refs_0_), channel_id=1, source_target_pairs={{0,12},{4,0},{8,4},{12,8},{1,13},{5,1},{9,5},{13,9},{2,14},{6,2},{... | collective-permute-start | bytes 2654216 | tf_op jit(solution)/shard_map/ppermute | solution.py:35
  33.5 0.7 copy.48
  34.4 0.7 copy.49
  35.1 0.7 copy-done.15
  36.0 0.8 copy.50
  36.8 1.3 fusion.23
  38.2 1.6 %fusion.22 = (s32[32,1,512]{2,1,0:T(1,128)}, s32[32,1,512]{2,1,0:T(1,128)}) fusion(s32[32,1,512]{2,1,0:T(1,128)S(1)} %get-tuple-element.5), kind=kLoop, calls=%fused_computation.53 | loop fusion | flops 360448 | bytes 196608 | tf_op jit(solution)/shard_map/sub | solution.py:278
  39.8 0.7 stack.32
  40.4 1.6 %stack.33.pairs_ref = s32[32,8,512]{2,1,0:T(8,128)S(1)} concatenate(s32[32,1,512]{2,1,0:T(1,128)} %get-tuple-element.18, s32[32,1,512]{2,1,0:T(1,128)} %get-tuple-element.3, s32[32,1,512]{2,1,0:T(1,128)} %get-tuple-element.17, s32[32,1,512]{2,1,0:T(1,128)} %get-tuple-element.16, s32[32,1,512]{2,1,0:T(1,128)} %get-tuple-element.4, s32[32,1,512]{2,1,0:T(1,128)} %get-tuple-element.2, ...), dimensions={1} | concatenate | bytes 1048576 | tf_op jit(solution)/shard_map/stack | solution.py:283
  42.2 0.7 copy-done.12
  42.9 0.9 fusion.2
  43.8 7.1 %collective-permute-done.4.refs_2_ = bf16[6,144,512]{2,1,0:T(8,128)(2,1)S(1)} collective-permute-done((bf16[6,144,512]{2,1,0:T(8,128)(2,1)S(1)}, bf16[6,144,512]{2,1,0:T(8,128)(2,1)S(1)}, u32[]{:S(2)}, u32[]{:S(2)}) %collective-permute-start.4) | collective-permute-done | bytes 884768 | tf_op jit(solution)/shard_map/ppermute | solution.py:37
  51.0 0.9 collective-permute-done.3.refs_1_
  51.9 29.9 %pairs.1 = f32[18,4,512]{2,1,0:T(4,128)S(1)} custom-call(s32[65]{0:T(128)S(1)} %pad_add_fusion.1.plan_ref, s32[32,8,512]{2,1,0:T(8,128)S(1)} %stack.33.pairs_ref, bf16[6,144,512]{2,1,0:T(8,128)(2,1)S(1)} %pad_maximum_fusion.refs_0_, bf16[6,144,512]{2,1,0:T(8,128)(2,1)S(1)} %collective-permute-done.3.refs_1_, ...), custom_call_target="tpu_custom_call" | custom-call | tf_op jit(solution)/shard_map/pairs/pallas_call | solution.py:318
  81.8 47.2 %collective-permute-start.6 = (f32[2,3,4,512]{3,2,1,0:T(4,128)S(1)}, f32[2,3,4,512]{3,2,1,0:T(4,128)S(1)}, u32[]{:S(2)}, u32[]{:S(2)}) collective-permute-start(f32[2,3,4,512]{3,2,1,0:T(4,128)S(1)} %bitcast.94), channel_id=1, source_target_pairs={{0,12},{4,0},{8,4},{12,8},{1,13},{5,1},{9,5},{13,9},{2,14},{6,2},{... | collective-permute-start | bytes 147464 | tf_op jit(solution)/shard_map/ppermute | solution.py:44
  129.0 1.7 %collective-permute-done.6 = f32[2,3,4,512]{3,2,1,0:T(4,128)S(1)} collective-permute-done((f32[2,3,4,512]{3,2,1,0:T(4,128)S(1)}, f32[2,3,4,512]{3,2,1,0:T(4,128)S(1)}, u32[]{:S(2)}, u32[]{:S(2)}) %collective-permute-start.6) | collective-permute-done | bytes 49184 | tf_op jit(solution)/shard_map/ppermute | solution.py:44
  130.7 1.8 %collective-permute-done.5 = f32[2,3,4,512]{3,2,1,0:T(4,128)S(1)} collective-permute-done((f32[2,3,4,512]{3,2,1,0:T(4,128)S(1)}, f32[2,3,4,512]{3,2,1,0:T(4,128)S(1)}, u32[]{:S(2)}, u32[]{:S(2)}) %collective-permute-start.5) | collective-permute-done | bytes 49184 | tf_op jit(solution)/shard_map/ppermute | solution.py:42
  132.5 1.7 %collective-permute-start.7 = (f32[3,4,512]{2,1,0:T(4,128)S(1)}, f32[3,4,512]{2,1,0:T(4,128)S(1)}, u32[]{:S(2)}, u32[]{:S(2)}) collective-permute-start(f32[3,4,512]{2,1,0:T(4,128)S(1)} %slice_bitcast_fusion), channel_id=1, source_target_pairs={{0,16},{16,0},{1,17},{17,1},{2,18},{18,2},{3,19},{19,3},{4,20},{20... | collective-permute-start | bytes 73736 | tf_op jit(solution)/shard_map/ppermute | solution.py:42
  134.2 2.2 %collective-permute-done.7 = f32[3,4,512]{2,1,0:T(4,128)S(1)} collective-permute-done((f32[3,4,512]{2,1,0:T(4,128)S(1)}, f32[3,4,512]{2,1,0:T(4,128)S(1)}, u32[]{:S(2)}, u32[]{:S(2)}) %collective-permute-start.7) | collective-permute-done | bytes 24608 | tf_op jit(solution)/shard_map/ppermute | solution.py:42
  136.5 3.8 %collective-permute-start.9 = (f32[4,512]{1,0:T(4,128)S(1)}, f32[4,512]{1,0:T(4,128)S(1)}, u32[]{:S(2)}, u32[]{:S(2)}) collective-permute-start(f32[4,512]{1,0:T(4,128)S(1)} %get-tuple-element.23), channel_id=1, source_target_pairs={{0,3},{1,0},{2,1},{3,2},{4,7},{5,4},{6,5},{7,6},{8,11},{9,8},{10,9... | collective-permute-start | bytes 24584 | tf_op jit(solution)/shard_map/ppermute | solution.py:44
  140.3 1.6 %collective-permute-done.8 = f32[4,512]{1,0:T(4,128)S(1)} collective-permute-done((f32[4,512]{1,0:T(4,128)S(1)}, f32[4,512]{1,0:T(4,128)S(1)}, u32[]{:S(2)}, u32[]{:S(2)}) %collective-permute-start.8) | collective-permute-done | bytes 8224 | tf_op jit(solution)/shard_map/ppermute | solution.py:42
  (72 shorter events, 4.0 us)
Async XLA Ops:
  0.6 1.8 %copy-start = (bf16[128]{0:T(256)(128)(2,1)S(1)}, bf16[128]{0:T(256)(128)(2,1)}, u32[]{:S(2)}) copy-start(bf16[128]{0:T(256)(128)(2,1)} %param.22) | copy-start | bytes 772
  1.3 1.1 copy-start.3
  3.8 0.7 copy-start.14
  4.6 5.4 %copy-start.6 = (s32[1,1,1,128,128]{4,3,2,1,0:T(8,128)S(1)}, s32[1,1,1,128,128]{4,3,2,1,0:T(8,128)}, u32[]{:S(2)}) copy-start(s32[1,1,1,128,128]{4,3,2,1,0:T(8,128)} %param.19) | copy-start | bytes 196612
  4.6 6.0 %copy-start.8 = (s32[1,1,1,128,128]{4,3,2,1,0:T(8,128)S(1)}, s32[1,1,1,128,128]{4,3,2,1,0:T(8,128)}, u32[]{:S(2)}) copy-start(s32[1,1,1,128,128]{4,3,2,1,0:T(8,128)} %param.18) | copy-start | bytes 196612
  4.7 5.8 %copy-start.7 = (s32[1,1,1,128,128]{4,3,2,1,0:T(8,128)S(1)}, s32[1,1,1,128,128]{4,3,2,1,0:T(8,128)}, u32[]{:S(2)}) copy-start(s32[1,1,1,128,128]{4,3,2,1,0:T(8,128)} %param.17) | copy-start | bytes 196612
  4.7 14.2 %collective-permute-start.1 = (bf16[144,512]{1,0:T(8,128)(2,1)S(1)}, bf16[144,512]{1,0:T(8,128)(2,1)S(1)}, u32[]{:S(2)}, u32[]{:S(2)}) collective-permute-start(bf16[144,512]{1,0:T(8,128)(2,1)S(1)} %concatenate.40), channel_id=1, source_target_pairs={{0,1},{1,2},{2,3},{3,0},{4,5},{5,6},{6,7},{7,4},{8,9},{9,10},{10,1... | collective-permute-start | bytes 442376 | tf_op jit(solution)/shard_map/ppermute | solution.py:37
  7.8 11.2 %collective-permute-start = (bf16[144,512]{1,0:T(8,128)(2,1)S(1)}, bf16[144,512]{1,0:T(8,128)(2,1)S(1)}, u32[]{:S(2)}, u32[]{:S(2)}) collective-permute-start(bf16[144,512]{1,0:T(8,128)(2,1)S(1)} %concatenate.40), channel_id=1, source_target_pairs={{0,3},{1,0},{2,1},{3,2},{4,7},{5,4},{6,5},{7,6},{8,11},{9,8},{10,9... | collective-permute-start | bytes 442376 | tf_op jit(solution)/shard_map/ppermute | solution.py:35
  18.3 0.7 copy-start.11
  19.0 11.7 %collective-permute-start.2 = (bf16[3,144,512]{2,1,0:T(8,128)(2,1)S(1)}, bf16[3,144,512]{2,1,0:T(8,128)(2,1)S(1)}, u32[]{:S(2)}, u32[]{:S(2)}) collective-permute-start(bf16[3,144,512]{2,1,0:T(8,128)(2,1)S(1)} %pad_maximum_fusion.1), channel_id=1, source_target_pairs={{0,16},{16,0},{1,17},{17,1},{2,18},{18,2},{3,19},{19,3},{4,20},{20... | collective-permute-start | bytes 1327112 | tf_op jit(solution)/shard_map/ppermute | solution.py:35
  30.8 20.1 %collective-permute-start.4 = (bf16[6,144,512]{2,1,0:T(8,128)(2,1)S(1)}, bf16[6,144,512]{2,1,0:T(8,128)(2,1)S(1)}, u32[]{:S(2)}, u32[]{:S(2)}) collective-permute-start(bf16[6,144,512]{2,1,0:T(8,128)(2,1)S(1)} %pad_maximum_fusion.refs_0_), channel_id=1, source_target_pairs={{0,4},{4,8},{8,12},{12,0},{1,5},{5,9},{9,13},{13,1},{2,6},{6,10},{... | collective-permute-start | bytes 2654216 | tf_op jit(solution)/shard_map/ppermute | solution.py:37
  30.9 21.0 %collective-permute-start.3 = (bf16[6,144,512]{2,1,0:T(8,128)(2,1)S(1)}, bf16[6,144,512]{2,1,0:T(8,128)(2,1)S(1)}, u32[]{:S(2)}, u32[]{:S(2)}) collective-permute-start(bf16[6,144,512]{2,1,0:T(8,128)(2,1)S(1)} %pad_maximum_fusion.refs_0_), channel_id=1, source_target_pairs={{0,12},{4,0},{8,4},{12,8},{1,13},{5,1},{9,5},{13,9},{2,14},{6,2},{... | collective-permute-start | bytes 2654216 | tf_op jit(solution)/shard_map/ppermute | solution.py:35
  32.7 0.8 copy-start.9
  33.5 0.8 copy-start.10
  34.4 1.5 %copy-start.1 = (bf16[256,256]{1,0:T(8,128)(2,1)S(1)}, bf16[256,256]{1,0:T(8,128)(2,1)}, u32[]{:S(2)}) copy-start(bf16[256,256]{1,0:T(8,128)(2,1)} %refs_7_.1) | copy-start | bytes 393220
  35.1 0.7 copy-start.15
  35.9 0.9 copy-start.4
  35.9 0.9 copy-start.5
  42.2 0.7 copy-start.12
  42.2 0.7 copy-start.13
  42.9 9.0 %copy-start.2 = (bf16[256,256]{0,1:T(8,128)(2,1)S(1)}, bf16[256,256]{0,1:T(8,128)(2,1)}, u32[]{:S(2)}) copy-start(bf16[256,256]{0,1:T(8,128)(2,1)} %copy.50) | copy-start | bytes 393220
  81.8 49.0 %collective-permute-start.6 = (f32[2,3,4,512]{3,2,1,0:T(4,128)S(1)}, f32[2,3,4,512]{3,2,1,0:T(4,128)S(1)}, u32[]{:S(2)}, u32[]{:S(2)}) collective-permute-start(f32[2,3,4,512]{3,2,1,0:T(4,128)S(1)} %bitcast.94), channel_id=1, source_target_pairs={{0,12},{4,0},{8,4},{12,8},{1,13},{5,1},{9,5},{13,9},{2,14},{6,2},{... | collective-permute-start | bytes 147464 | tf_op jit(solution)/shard_map/ppermute | solution.py:44
  129.0 3.5 %collective-permute-start.5 = (f32[2,3,4,512]{3,2,1,0:T(4,128)S(1)}, f32[2,3,4,512]{3,2,1,0:T(4,128)S(1)}, u32[]{:S(2)}, u32[]{:S(2)}) collective-permute-start(f32[2,3,4,512]{3,2,1,0:T(4,128)S(1)} %bitcast.93), channel_id=1, source_target_pairs={{0,4},{4,8},{8,12},{12,0},{1,5},{5,9},{9,13},{13,1},{2,6},{6,10},{... | collective-permute-start | bytes 147464 | tf_op jit(solution)/shard_map/ppermute | solution.py:42
  132.5 3.9 %collective-permute-start.7 = (f32[3,4,512]{2,1,0:T(4,128)S(1)}, f32[3,4,512]{2,1,0:T(4,128)S(1)}, u32[]{:S(2)}, u32[]{:S(2)}) collective-permute-start(f32[3,4,512]{2,1,0:T(4,128)S(1)} %slice_bitcast_fusion), channel_id=1, source_target_pairs={{0,16},{16,0},{1,17},{17,1},{2,18},{18,2},{3,19},{19,3},{4,20},{20... | collective-permute-start | bytes 73736 | tf_op jit(solution)/shard_map/ppermute | solution.py:42
  136.5 5.5 %collective-permute-start.8 = (f32[4,512]{1,0:T(4,128)S(1)}, f32[4,512]{1,0:T(4,128)S(1)}, u32[]{:S(2)}, u32[]{:S(2)}) collective-permute-start(f32[4,512]{1,0:T(4,128)S(1)} %get-tuple-element.22), channel_id=1, source_target_pairs={{0,1},{1,2},{2,3},{3,0},{4,5},{5,6},{6,7},{7,4},{8,9},{9,10},{10,1... | collective-permute-start | bytes 24584 | tf_op jit(solution)/shard_map/ppermute | solution.py:42
  136.5 5.4 %collective-permute-start.9 = (f32[4,512]{1,0:T(4,128)S(1)}, f32[4,512]{1,0:T(4,128)S(1)}, u32[]{:S(2)}, u32[]{:S(2)}) collective-permute-start(f32[4,512]{1,0:T(4,128)S(1)} %get-tuple-element.23), channel_id=1, source_target_pairs={{0,3},{1,0},{2,1},{3,2},{4,7},{5,4},{6,5},{7,6},{8,11},{9,8},{10,9... | collective-permute-start | bytes 24584 | tf_op jit(solution)/shard_map/ppermute | solution.py:44

commit v2 on v1

--- a/solution.py
+++ b/solution.py
@@ -12,6 +12,7 @@
 coulomb = 0.2
 root_pi = 1.7724538509055159
 part_rows = 16
+subs = 2
 erfc_terms = (
     0.17087277,
     -0.82215223,
@@ -80,7 +81,11 @@
         pre_ref,
         sum_i_ref,
         sum_j_ref,
+        pick_i_ref,
+        pick_j_ref,
+        terms_ref,
     ) = refs
+    basis_count = radial_two_ref.shape[0] // 2
     atoms = centre_ref.shape[1]
     lanes = pairs_ref.shape[2]
     hid = hidden_ref.shape[0]
@@ -100,39 +105,45 @@
     sum_i_ref[...] = jnp.zeros_like(sum_i_ref)
     sum_j_ref[...] = jnp.zeros_like(sum_j_ref)
 
+    chunk = 16
+    ladder = lax.broadcasted_iota(jnp.int32, (chunk, lanes), 0).astype(jnp.int16)
+
     def pick(rows, entries):
-        spot = lax.broadcasted_iota(jnp.int32, (rows, lanes), 0)
-        return jnp.where(spot == entries, 1.0, 0.0).astype(jnp.bfloat16)
-
-    def step(block, carry):
-        listed = pairs_ref[block]
-        first = listed[0:1]
-        second = listed[1:2]
-        offset_x = listed[2:3].astype(jnp.float32)
-        offset_y = listed[3:4].astype(jnp.float32)
-        offset_z = listed[4:5].astype(jnp.float32)
-        weight = listed[5:6].astype(jnp.float32)
-        least = plan_ref[2 * block + 1]
-        most = plan_ref[2 * block + 2]
-        pick_i = pick(atoms, first)
-        pre_ref[...] = lower(centre_ref[...], pick_i)
-
-        def gather(window, carry):
-            pre_ref[...] += lower(image_ref[window], pick(width, second - window * width))
-            return carry
-
-        lax.fori_loop(least, most + 1, gather, 0)
-        extra = pre_ref[hid:, :]
-        sep_x = (extra[0:1] + extra[3:4]) + extra[6:7] + offset_x
-        sep_y = (extra[1:2] + extra[4:5]) + extra[7:8] + offset_y
-        sep_z = (extra[2:3] + extra[5:6]) + extra[8:9] + offset_z
-        charge_i = extra[9:10] + extra[10:11] + extra[11:12]
-        charge_j = extra[12:13] + extra[13:14] + extra[14:15]
+        spread_out = jnp.broadcast_to(entries, (chunk, lanes)).astype(jnp.int16)
+        one = jnp.ones((chunk, lanes), jnp.bfloat16)
+        zero = jnp.zeros((chunk, lanes), jnp.bfloat16)
+        return jnp.concatenate(
+            [
+                jnp.where(spread_out == ladder + jnp.int16(base), one, zero)
+                for base in range(0, rows, chunk)
+            ],
+            axis=0,
+        )
+
+    across = (((1,), (1,)), ((), ()))
+
+    def spill(terms, picked):
+        return lax.dot_general(terms, picked, across, preferred_element_type=jnp.float32)
+
+    def begin_part(part):
+        listed = pairs_ref[part]
+        least = plan_ref[2 * part + 1]
+        after = jnp.minimum(least + 1, image_ref.shape[0] - 1)
+        pick_i = pick(atoms, listed[0:1])
+        pick_j = pick(2 * width, listed[1:2] - least * width)
+        pre = lower(centre_ref[...], pick_i)
+        pre += lower(image_ref[least], pick_j[:width])
+        pre += lower(image_ref[after], pick_j[width:])
+        return pre, pick_i, pick_j
+
+    def geometry(part, lane):
+        listed = pairs_ref[part]
+        extra = pre_ref[lane, hid:, :]
+        sep_x = (extra[0:1] + extra[3:4]) + extra[6:7] + listed[2:3].astype(jnp.float32)
+        sep_y = (extra[1:2] + extra[4:5]) + extra[7:8] + listed[3:4].astype(jnp.float32)
+        sep_z = (extra[2:3] + extra[5:6]) + extra[8:9] + listed[4:5].astype(jnp.float32)
         dist_sq = sep_x * sep_x + sep_y * sep_y + sep_z * sep_z + delta_sq
         distance = jnp.sqrt(dist_sq)
-        inverse = 1.0 / distance
-        envelope = jnp.exp(-0.5 * dist_sq)
-        basis_count = radial_two_ref.shape[0] // 2
         order = lax.broadcasted_iota(jnp.int32, (basis_count, lanes), 0).astype(jnp.float32)
         offset = distance - (0.25 + 0.3 * order)
         basis = jnp.exp(-(offset / spread) * (offset / spread))
@@ -140,27 +151,35 @@
         basis_cat = jnp.concatenate(
             [basis_high, basis - basis_high, basis_high, jnp.zeros_like(basis)], axis=0
         ).astype(jnp.bfloat16)
-        pre_one = pre_ref[:hid, :] + lower(radial_cat_ref[...], basis_cat)
-        gate_one = 0.5 * jnp.tanh(0.5 * pre_one) + 0.5
-        act_one = pre_one * gate_one
-        slope_one = gate_one + act_one * (1.0 - gate_one)
-        pre_two = lower(hidden_t_ref[...], act_one.astype(jnp.bfloat16))
-        gate_two = 0.5 * jnp.tanh(0.5 * pre_two) + 0.5
-        scaled = energy_ref[...] * gate_two
+        pre_one = pre_ref[lane, :hid, :] + lower(radial_cat_ref[...], basis_cat)
+        return (sep_x, sep_y, sep_z), dist_sq, distance, offset, basis, pre_one
+
+    def first_layer(pre_one):
+        gate = 0.5 * jnp.tanh(0.5 * pre_one) + 0.5
+        act = pre_one * gate
+        return act.astype(jnp.bfloat16), gate + act * (1.0 - gate)
+
+    def second_layer(pre_two, dist_sq):
+        gate = 0.5 * jnp.tanh(0.5 * pre_two) + 0.5
+        scaled = energy_ref[...] * gate
         scaled_act = pre_two * scaled
         readout = jnp.sum(scaled_act, axis=0, keepdims=True)
-        back_two = (envelope * (scaled + scaled_act * (1.0 - gate_two))).astype(jnp.bfloat16)
-        back_one = lower(hidden_ref[...], back_two) * slope_one
-        back_high = back_one.astype(jnp.bfloat16)
-        back_low = (back_one - back_high.astype(jnp.float32)).astype(jnp.bfloat16)
-        from_high = lower(radial_two_ref[...], back_high)
-        from_low = lower(radial_two_ref[...], back_low)
-        back_basis = from_high[:basis_count] + from_high[basis_count:] + from_low[:basis_count]
+        envelope = jnp.exp(-0.5 * dist_sq)
+        back = (envelope * (scaled + scaled_act * (1.0 - gate))).astype(jnp.bfloat16)
+        return back, readout * envelope
+
+    def pair_terms(part, lane, shape, back_basis, readout):
+        (sep_x, sep_y, sep_z), dist_sq, distance, offset, basis, _ = shape
+        weight = pairs_ref[part][5:6].astype(jnp.float32)
+        extra = pre_ref[lane, hid:, :]
+        charge_i = extra[9:10] + extra[10:11] + extra[11:12]
+        charge_j = extra[12:13] + extra[13:14] + extra[14:15]
+        inverse = 1.0 / distance
         slope_nn = (
             jnp.sum(
                 back_basis * basis * (offset * (-2.0 / (spread * spread))), axis=0, keepdims=True
             )
-            - readout * distance * envelope
+            - readout * distance
         )
         ratio = 1.0 / (1.0 + 0.5 * distance)
         series = jnp.full_like(ratio, erfc_terms[0])
@@ -188,22 +207,51 @@
             axis=0,
         )
         terms_high = terms.astype(jnp.bfloat16).astype(jnp.float32)
-        both = jnp.concatenate([terms_high, terms - terms_high], axis=0).astype(jnp.bfloat16)
-        across = (((1,), (1,)), ((), ()))
-        sum_i_ref[...] += lax.dot_general(
-            both, pick_i, across, preferred_element_type=jnp.float32
-        )
-
-        def scatter(window, carry):
-            sum_j_ref[window] += lax.dot_general(
-                both,
-                pick(width, second - window * width),
-                across,
-                preferred_element_type=jnp.float32,
-            )
-            return carry
-
-        lax.fori_loop(least, most + 1, scatter, 0)
+        return jnp.concatenate([terms_high, terms - terms_high], axis=0).astype(jnp.bfloat16)
+
+    def step(block, carry):
+        parts = [block * subs + lane for lane in range(subs)]
+        for lane, part in enumerate(parts):
+            pre, pick_i, pick_j = begin_part(part)
+            pre_ref[lane] = pre
+            pick_i_ref[lane] = pick_i
+            pick_j_ref[lane] = pick_j
+
+        for lane, part in enumerate(parts):
+            def gather(window, carry, lane=lane, part=part):
+                entries = pairs_ref[part][1:2] - window * width
+                pre_ref[lane] += lower(image_ref[window], pick(width, entries))
+                return carry
+
+            lax.fori_loop(plan_ref[2 * part + 1] + 2, plan_ref[2 * part + 2] + 1, gather, 0)
+
+        shapes = [geometry(part, lane) for lane, part in enumerate(parts)]
+        ones = [first_layer(shape[-1]) for shape in shapes]
+        twos = [lower(hidden_t_ref[...], one[0]) for one in ones]
+        backs = [second_layer(two, shape[1]) for two, shape in zip(twos, shapes)]
+        grads = [
+            (lower(hidden_ref[...], back[0]) * one[1]).astype(jnp.bfloat16)
+            for back, one in zip(backs, ones)
+        ]
+        for lane, part in enumerate(parts):
+            from_grad = lower(radial_two_ref[...], grads[lane])
+            back_basis = from_grad[:basis_count] + from_grad[basis_count:]
+            terms_ref[lane] = pair_terms(part, lane, shapes[lane], back_basis, backs[lane][1])
+        for lane, part in enumerate(parts):
+            least = plan_ref[2 * part + 1]
+            after = jnp.minimum(least + 1, image_ref.shape[0] - 1)
+            terms = terms_ref[lane]
+            sum_i_ref[...] += spill(terms, pick_i_ref[lane])
+            sum_j_ref[least] += spill(terms, pick_j_ref[lane, :width])
+            sum_j_ref[after] += spill(terms, pick_j_ref[lane, width:])
+
+        for lane, part in enumerate(parts):
+            def scatter(window, carry, lane=lane, part=part):
+                entries = pairs_ref[part][1:2] - window * width
+                sum_j_ref[window] += spill(terms_ref[lane], pick(width, entries))
+                return carry
+
+            lax.fori_loop(plan_ref[2 * part + 1] + 2, plan_ref[2 * part + 2] + 1, scatter, 0)
         return carry
 
     lax.fori_loop(0, plan_ref[0], step, 0)
@@ -265,7 +313,7 @@
     key = jnp.where(mask, key, bricks * atoms * atoms * 27)
     key = lax.sort(key, is_stable=False)
     valid = jnp.sum(mask.astype(jnp.int32))
-    lanes = 512 if key.shape[0] % 512 == 0 else 128
+    lanes = 256 if key.shape[0] % (256 * subs) == 0 else 128
     width = 256 if atoms % 256 == 0 else 128
     blocks = key.shape[0] // lanes
     key = key.reshape(blocks, lanes)
@@ -282,7 +330,7 @@
     rows = rows + [jnp.zeros_like(key)] * 2
     listed = jnp.stack(rows, axis=1)
     window = jnp.minimum(second // width, bricks * atoms // width - 1)
-    live = (valid + lanes - 1) // lanes
+    live = (valid + subs * lanes - 1) // (subs * lanes)
     plan = jnp.concatenate(
         [live[None], jnp.stack([window[:, 0], jnp.max(window, axis=1)], axis=1).reshape(-1)]
     ).astype(jnp.int32)
@@ -323,9 +371,12 @@
         scratch_shapes=[
             pltpu.VMEM((hid + part_rows, atoms), jnp.bfloat16),
             pltpu.VMEM((windows, hid + part_rows, width), jnp.bfloat16),
-            pltpu.VMEM((hid + part_rows, lanes), jnp.float32),
+            pltpu.VMEM((subs, hid + part_rows, lanes), jnp.float32),
             pltpu.VMEM((16, atoms), jnp.float32),
             pltpu.VMEM((windows, 16, width), jnp.float32),
+            pltpu.VMEM((subs, atoms, lanes), jnp.bfloat16),
+            pltpu.VMEM((subs, 2 * width, lanes), jnp.bfloat16),
+            pltpu.VMEM((subs, 16, lanes), jnp.bfloat16),
         ],
         compiler_params=pltpu.CompilerParams(vmem_limit_bytes=48 * 1024 * 1024),
         name="pairs",

time: 143 us -> 125 us (0.87)
  starting transfers between devices: 61.5 us -> 39.8 us
  Pallas kernels: 29.9 us -> 35.7 us
  waiting for transfers between devices: 24.5 us -> 21.4 us
    ppermute x2, starting transfers between devices: 51 us -> 3.87 us  [fold(): total = total + lax.ppermute(blocks[2], axis, ring(axis, -1))]
    ppermute x3, starting transfers between devices: 1.76 us -> 27.3 us  [fold(): total = blocks[0] + lax.ppermute(blocks[1], axis, ring(axis, 1))]
    pallas_call x1, Pallas kernels: 29.9 us -> 35.7 us  [local(): pl.pallas_call(functools.partial(pair_kernel, width), out_shape=jax.Shape...]
    ppermute x3, waiting for transfers between devices: 5.58 us -> 3.65 us  [fold(): total = blocks[0] + lax.ppermute(blocks[1], axis, ring(axis, 1))]
  transfers between devices with their start and end apart: 10 -> 10, of which waited for: 7 -> 7; matrix products, arithmetic and copies ran while one was open for 13% -> 15% of each run, Pallas kernels for 0% -> 0%
where the time goes in v2:
time: 125 us; the launch traced here: 124 us
  starting transfers between devices  39.8 us (32%)
  Pallas kernels  35.7 us (29%)
  waiting for transfers between devices  21.4 us (17%)
  other arithmetic  13.8 us (11%)
  local copies, waits for them, and re-layouts  10.5 us (8%)
  between operations  2.99 us (2%)
    pallas_call x1, Pallas kernels, local(): pl.pallas_call(functools.partial(pair_kernel, width), out_shape=jax.Shape...  35.7 us
    ppermute x3, starting transfers between devices, fold(): total = blocks[0] + lax.ppermute(blocks[1], axis, ring(axis, 1))  27.3 us
    ppermute x3, waiting for transfers between devices, widen(): parts = [block, lax.ppermute(block, axis, ring(axis, -1))]  10 us
    ppermute x2, waiting for transfers between devices, widen(): parts.append(lax.ppermute(block, axis, ring(axis, 1)))  7.1 us
    sort x1, other arithmetic, local(): key = lax.sort(key, is_stable=False)  6.29 us
    unnamed x36, local copies, waits for them, and re-layouts  6.09 us
    ppermute x3, starting transfers between devices, widen(): parts = [block, lax.ppermute(block, axis, ring(axis, -1))]  5.54 us
    ppermute x2, starting transfers between devices, fold(): total = total + lax.ppermute(blocks[2], axis, ring(axis, -1))  3.87 us
  transfers between devices with their start and end apart: 10, of which 7 were waited for; matrix products, arithmetic and copies ran while one was open for 15% of the time, Pallas kernels for 0%

profile of v2, /device:TPU:0, one launch (start us, length us, event | category | flops | bytes accessed | tf_op | source)
XLA Modules:
  0.0 124.3 jit_solution(6536247035120026720)
XLA Ops:
  1.3 1.1 copy.47
  2.5 0.6 select_reduce_fusion
  3.9 0.6 copy-done.14
  4.7 3.1 %collective-permute-start.1 = (bf16[144,512]{1,0:T(8,128)(2,1)S(1)}, bf16[144,512]{1,0:T(8,128)(2,1)S(1)}, u32[]{:S(2)}, u32[]{:S(2)}) collective-permute-start(bf16[144,512]{1,0:T(8,128)(2,1)S(1)} %concatenate.40), channel_id=1, source_target_pairs={{0,1},{1,2},{2,3},{3,0},{4,5},{5,6},{6,7},{7,4},{8,9},{9,10},{10,1... | collective-permute-start | bytes 442376 | tf_op jit(solution)/shard_map/ppermute | solution.py:38
  7.8 2.1 %collective-permute-start = (bf16[144,512]{1,0:T(8,128)(2,1)S(1)}, bf16[144,512]{1,0:T(8,128)(2,1)S(1)}, u32[]{:S(2)}, u32[]{:S(2)}) collective-permute-start(bf16[144,512]{1,0:T(8,128)(2,1)S(1)} %concatenate.40), channel_id=1, source_target_pairs={{0,3},{1,0},{2,1},{3,2},{4,7},{5,4},{6,5},{7,6},{8,11},{9,8},{10,9... | collective-permute-start | bytes 442376 | tf_op jit(solution)/shard_map/ppermute | solution.py:36
  9.9 0.6 convert_reduce_fusion
  10.8 6.3 %sort.7 = s32[16384]{0:T(1024)S(1)} sort(s32[16384]{0:T(1024)S(1)} %fusion.14), dimensions={0}, to_apply=%region_1.2 | sort | flops 229376 | bytes 131072 | tf_op jit(solution)/shard_map/sort | solution.py:314
  17.2 0.7 broadcast_remainder_fusion
  18.4 0.6 copy-done.11
  19.0 1.7 %collective-permute-start.2 = (bf16[3,144,512]{2,1,0:T(8,128)(2,1)S(1)}, bf16[3,144,512]{2,1,0:T(8,128)(2,1)S(1)}, u32[]{:S(2)}, u32[]{:S(2)}) collective-permute-start(bf16[3,144,512]{2,1,0:T(8,128)(2,1)S(1)} %pad_maximum_fusion.1), channel_id=1, source_target_pairs={{0,16},{16,0},{1,17},{17,1},{2,18},{18,2},{3,19},{19,3},{4,20},{20... | collective-permute-start | bytes 1327112 | tf_op jit(solution)/shard_map/ppermute | solution.py:36
  20.8 0.8 compare_convert_fusion
  21.6 9.1 %collective-permute-done.2 = bf16[3,144,512]{2,1,0:T(8,128)(2,1)S(1)} collective-permute-done((bf16[3,144,512]{2,1,0:T(8,128)(2,1)S(1)}, bf16[3,144,512]{2,1,0:T(8,128)(2,1)S(1)}, u32[]{:S(2)}, u32[]{:S(2)}) %collective-permute-start.2) | collective-permute-done | bytes 442400 | tf_op jit(solution)/shard_map/ppermute | solution.py:36
  30.9 1.7 %collective-permute-start.3 = (bf16[6,144,512]{2,1,0:T(8,128)(2,1)S(1)}, bf16[6,144,512]{2,1,0:T(8,128)(2,1)S(1)}, u32[]{:S(2)}, u32[]{:S(2)}) collective-permute-start(bf16[6,144,512]{2,1,0:T(8,128)(2,1)S(1)} %pad_maximum_fusion.refs_0_), channel_id=1, source_target_pairs={{0,12},{4,0},{8,4},{12,8},{1,13},{5,1},{9,5},{13,9},{2,14},{6,2},{... | collective-permute-start | bytes 2654216 | tf_op jit(solution)/shard_map/ppermute | solution.py:36
  33.5 0.7 copy.48
  34.4 0.7 copy.49
  35.1 0.7 copy-done.15
  36.0 0.8 copy.50
  36.9 1.3 %fusion.23 = (s32[64,1,256]{2,1,0:T(1,128)}, s32[64,1,256]{2,1,0:T(1,128)S(1)}, s32[64,1,256]{2,1,0:T(1,128)}) fusion(s32[64,1,256]{2,1,0:T(1,128)S(1)} %bitcast.90, s32[64,1,256]{2,1,0:T(1,128)S(1)} %bitcast.91, pred[64,1,256]{2,1,0:T(4,128)(4,1)S(1)} %ne.284), kind=kLoop, calls=%fused_computation.54 | loop fusion | flops 425984 | bytes 344064 | tf_op jit(solution)/shard_map/sub | solution.py:327
  38.2 1.6 %fusion.22 = (s32[64,1,256]{2,1,0:T(1,128)}, s32[64,1,256]{2,1,0:T(1,128)}) fusion(s32[64,1,256]{2,1,0:T(1,128)S(1)} %get-tuple-element.5), kind=kLoop, calls=%fused_computation.53 | loop fusion | flops 360448 | bytes 196608 | tf_op jit(solution)/shard_map/sub | solution.py:326
  39.8 0.7 stack.32
  40.5 1.6 %stack.33.pairs_ref = s32[64,8,256]{2,1,0:T(8,128)S(1)} concatenate(s32[64,1,256]{2,1,0:T(1,128)} %get-tuple-element.18, s32[64,1,256]{2,1,0:T(1,128)} %get-tuple-element.3, s32[64,1,256]{2,1,0:T(1,128)} %get-tuple-element.17, s32[64,1,256]{2,1,0:T(1,128)} %get-tuple-element.16, s32[64,1,256]{2,1,0:T(1,128)} %get-tuple-element.4, s32[64,1,256]{2,1,0:T(1,128)} %get-tuple-element.2, ...), dimensions={1} | concatenate | bytes 1048576 | tf_op jit(solution)/shard_map/stack | solution.py:331
  42.2 0.7 copy-done.12
  42.9 0.9 fusion.2
  43.8 7.1 %collective-permute-done.4.refs_2_ = bf16[6,144,512]{2,1,0:T(8,128)(2,1)S(1)} collective-permute-done((bf16[6,144,512]{2,1,0:T(8,128)(2,1)S(1)}, bf16[6,144,512]{2,1,0:T(8,128)(2,1)S(1)}, u32[]{:S(2)}, u32[]{:S(2)}) %collective-permute-start.4) | collective-permute-done | bytes 884768 | tf_op jit(solution)/shard_map/ppermute | solution.py:38
  50.9 0.9 collective-permute-done.3.refs_1_
  51.9 35.7 %pairs.1 = f32[18,4,512]{2,1,0:T(4,128)S(1)} custom-call(s32[129]{0:T(256)S(1)} %pad_add_fusion.1.plan_ref, s32[64,8,256]{2,1,0:T(8,128)S(1)} %stack.33.pairs_ref, bf16[6,144,512]{2,1,0:T(8,128)(2,1)S(1)} %pad_maximum_fusion.refs_0_, bf16[6,144,512]{2,1,0:T(8,128)(2,1)S(1)} %collective-permute-done.3.refs_1_, ...), custom_call_target="tpu_custom_call" | custom-call | tf_op jit(solution)/shard_map/pairs/pallas_call | solution.py:366
  87.7 18.4 %collective-permute-start.5 = (f32[2,3,4,512]{3,2,1,0:T(4,128)S(1)}, f32[2,3,4,512]{3,2,1,0:T(4,128)S(1)}, u32[]{:S(2)}, u32[]{:S(2)}) collective-permute-start(f32[2,3,4,512]{3,2,1,0:T(4,128)S(1)} %bitcast.93), channel_id=1, source_target_pairs={{0,4},{4,8},{8,12},{12,0},{1,5},{5,9},{9,13},{13,1},{2,6},{6,10},{... | collective-permute-start | bytes 147464 | tf_op jit(solution)/shard_map/ppermute | solution.py:43
  106.1 0.7 collective-permute-done.6
  107.0 8.8 %collective-permute-start.7 = (f32[3,4,512]{2,1,0:T(4,128)S(1)}, f32[3,4,512]{2,1,0:T(4,128)S(1)}, u32[]{:S(2)}, u32[]{:S(2)}) collective-permute-start(f32[3,4,512]{2,1,0:T(4,128)S(1)} %slice_bitcast_fusion), channel_id=1, source_target_pairs={{0,16},{16,0},{1,17},{17,1},{2,18},{18,2},{3,19},{19,3},{4,20},{20... | collective-permute-start | bytes 73736 | tf_op jit(solution)/shard_map/ppermute | solution.py:43
  115.8 1.8 %collective-permute-done.7 = f32[3,4,512]{2,1,0:T(4,128)S(1)} collective-permute-done((f32[3,4,512]{2,1,0:T(4,128)S(1)}, f32[3,4,512]{2,1,0:T(4,128)S(1)}, u32[]{:S(2)}, u32[]{:S(2)}) %collective-permute-start.7) | collective-permute-done | bytes 24608 | tf_op jit(solution)/shard_map/ppermute | solution.py:43
  117.7 3.8 %collective-permute-start.9 = (f32[4,512]{1,0:T(4,128)S(1)}, f32[4,512]{1,0:T(4,128)S(1)}, u32[]{:S(2)}, u32[]{:S(2)}) collective-permute-start(f32[4,512]{1,0:T(4,128)S(1)} %get-tuple-element.23), channel_id=1, source_target_pairs={{0,3},{1,0},{2,1},{3,2},{4,7},{5,4},{6,5},{7,6},{8,11},{9,8},{10,9... | collective-permute-start | bytes 24584 | tf_op jit(solution)/shard_map/ppermute | solution.py:45
  121.5 1.6 %collective-permute-done.8 = f32[4,512]{1,0:T(4,128)S(1)} collective-permute-done((f32[4,512]{1,0:T(4,128)S(1)}, f32[4,512]{1,0:T(4,128)S(1)}, u32[]{:S(2)}, u32[]{:S(2)}) %collective-permute-start.8) | collective-permute-done | bytes 8224 | tf_op jit(solution)/shard_map/ppermute | solution.py:43
  (72 shorter events, 3.7 us)
Async XLA Ops:
  0.6 1.8 %copy-start = (bf16[128]{0:T(256)(128)(2,1)S(1)}, bf16[128]{0:T(256)(128)(2,1)}, u32[]{:S(2)}) copy-start(bf16[128]{0:T(256)(128)(2,1)} %param.22) | copy-start | bytes 772
  1.3 1.1 copy-start.3
  3.8 0.7 copy-start.14
  4.6 5.4 %copy-start.6 = (s32[1,1,1,128,128]{4,3,2,1,0:T(8,128)S(1)}, s32[1,1,1,128,128]{4,3,2,1,0:T(8,128)}, u32[]{:S(2)}) copy-start(s32[1,1,1,128,128]{4,3,2,1,0:T(8,128)} %param.19) | copy-start | bytes 196612
  4.6 6.0 %copy-start.8 = (s32[1,1,1,128,128]{4,3,2,1,0:T(8,128)S(1)}, s32[1,1,1,128,128]{4,3,2,1,0:T(8,128)}, u32[]{:S(2)}) copy-start(s32[1,1,1,128,128]{4,3,2,1,0:T(8,128)} %param.18) | copy-start | bytes 196612
  4.7 5.8 %copy-start.7 = (s32[1,1,1,128,128]{4,3,2,1,0:T(8,128)S(1)}, s32[1,1,1,128,128]{4,3,2,1,0:T(8,128)}, u32[]{:S(2)}) copy-start(s32[1,1,1,128,128]{4,3,2,1,0:T(8,128)} %param.17) | copy-start | bytes 196612
  4.7 14.2 %collective-permute-start.1 = (bf16[144,512]{1,0:T(8,128)(2,1)S(1)}, bf16[144,512]{1,0:T(8,128)(2,1)S(1)}, u32[]{:S(2)}, u32[]{:S(2)}) collective-permute-start(bf16[144,512]{1,0:T(8,128)(2,1)S(1)} %concatenate.40), channel_id=1, source_target_pairs={{0,1},{1,2},{2,3},{3,0},{4,5},{5,6},{6,7},{7,4},{8,9},{9,10},{10,1... | collective-permute-start | bytes 442376 | tf_op jit(solution)/shard_map/ppermute | solution.py:38
  7.8 11.1 %collective-permute-start = (bf16[144,512]{1,0:T(8,128)(2,1)S(1)}, bf16[144,512]{1,0:T(8,128)(2,1)S(1)}, u32[]{:S(2)}, u32[]{:S(2)}) collective-permute-start(bf16[144,512]{1,0:T(8,128)(2,1)S(1)} %concatenate.40), channel_id=1, source_target_pairs={{0,3},{1,0},{2,1},{3,2},{4,7},{5,4},{6,5},{7,6},{8,11},{9,8},{10,9... | collective-permute-start | bytes 442376 | tf_op jit(solution)/shard_map/ppermute | solution.py:36
  18.3 0.7 copy-start.11
  19.0 11.7 %collective-permute-start.2 = (bf16[3,144,512]{2,1,0:T(8,128)(2,1)S(1)}, bf16[3,144,512]{2,1,0:T(8,128)(2,1)S(1)}, u32[]{:S(2)}, u32[]{:S(2)}) collective-permute-start(bf16[3,144,512]{2,1,0:T(8,128)(2,1)S(1)} %pad_maximum_fusion.1), channel_id=1, source_target_pairs={{0,16},{16,0},{1,17},{17,1},{2,18},{18,2},{3,19},{19,3},{4,20},{20... | collective-permute-start | bytes 1327112 | tf_op jit(solution)/shard_map/ppermute | solution.py:36
  30.8 20.1 %collective-permute-start.4 = (bf16[6,144,512]{2,1,0:T(8,128)(2,1)S(1)}, bf16[6,144,512]{2,1,0:T(8,128)(2,1)S(1)}, u32[]{:S(2)}, u32[]{:S(2)}) collective-permute-start(bf16[6,144,512]{2,1,0:T(8,128)(2,1)S(1)} %pad_maximum_fusion.refs_0_), channel_id=1, source_target_pairs={{0,4},{4,8},{8,12},{12,0},{1,5},{5,9},{9,13},{13,1},{2,6},{6,10},{... | collective-permute-start | bytes 2654216 | tf_op jit(solution)/shard_map/ppermute | solution.py:38
  30.9 21.0 %collective-permute-start.3 = (bf16[6,144,512]{2,1,0:T(8,128)(2,1)S(1)}, bf16[6,144,512]{2,1,0:T(8,128)(2,1)S(1)}, u32[]{:S(2)}, u32[]{:S(2)}) collective-permute-start(bf16[6,144,512]{2,1,0:T(8,128)(2,1)S(1)} %pad_maximum_fusion.refs_0_), channel_id=1, source_target_pairs={{0,12},{4,0},{8,4},{12,8},{1,13},{5,1},{9,5},{13,9},{2,14},{6,2},{... | collective-permute-start | bytes 2654216 | tf_op jit(solution)/shard_map/ppermute | solution.py:36
  32.7 0.8 copy-start.9
  33.5 0.8 copy-start.10
  34.4 1.5 %copy-start.1 = (bf16[256,256]{1,0:T(8,128)(2,1)S(1)}, bf16[256,256]{1,0:T(8,128)(2,1)}, u32[]{:S(2)}) copy-start(bf16[256,256]{1,0:T(8,128)(2,1)} %refs_7_.1) | copy-start | bytes 393220
  35.1 0.7 copy-start.15
  35.9 0.9 copy-start.4
  35.9 0.9 copy-start.5
  42.2 0.7 copy-start.12
  42.2 0.7 copy-start.13
  42.9 9.0 %copy-start.2 = (bf16[256,256]{0,1:T(8,128)(2,1)S(1)}, bf16[256,256]{0,1:T(8,128)(2,1)}, u32[]{:S(2)}) copy-start(bf16[256,256]{0,1:T(8,128)(2,1)} %copy.50) | copy-start | bytes 393220
  87.6 19.1 %collective-permute-start.6 = (f32[2,3,4,512]{3,2,1,0:T(4,128)S(1)}, f32[2,3,4,512]{3,2,1,0:T(4,128)S(1)}, u32[]{:S(2)}, u32[]{:S(2)}) collective-permute-start(f32[2,3,4,512]{3,2,1,0:T(4,128)S(1)} %bitcast.94), channel_id=1, source_target_pairs={{0,12},{4,0},{8,4},{12,8},{1,13},{5,1},{9,5},{13,9},{2,14},{6,2},{... | collective-permute-start | bytes 147464 | tf_op jit(solution)/shard_map/ppermute | solution.py:45
  87.7 19.3 %collective-permute-start.5 = (f32[2,3,4,512]{3,2,1,0:T(4,128)S(1)}, f32[2,3,4,512]{3,2,1,0:T(4,128)S(1)}, u32[]{:S(2)}, u32[]{:S(2)}) collective-permute-start(f32[2,3,4,512]{3,2,1,0:T(4,128)S(1)} %bitcast.93), channel_id=1, source_target_pairs={{0,4},{4,8},{8,12},{12,0},{1,5},{5,9},{9,13},{13,1},{2,6},{6,10},{... | collective-permute-start | bytes 147464 | tf_op jit(solution)/shard_map/ppermute | solution.py:43
  107.0 10.6 %collective-permute-start.7 = (f32[3,4,512]{2,1,0:T(4,128)S(1)}, f32[3,4,512]{2,1,0:T(4,128)S(1)}, u32[]{:S(2)}, u32[]{:S(2)}) collective-permute-start(f32[3,4,512]{2,1,0:T(4,128)S(1)} %slice_bitcast_fusion), channel_id=1, source_target_pairs={{0,16},{16,0},{1,17},{17,1},{2,18},{18,2},{3,19},{19,3},{4,20},{20... | collective-permute-start | bytes 73736 | tf_op jit(solution)/shard_map/ppermute | solution.py:43
  117.6 5.5 %collective-permute-start.8 = (f32[4,512]{1,0:T(4,128)S(1)}, f32[4,512]{1,0:T(4,128)S(1)}, u32[]{:S(2)}, u32[]{:S(2)}) collective-permute-start(f32[4,512]{1,0:T(4,128)S(1)} %get-tuple-element.22), channel_id=1, source_target_pairs={{0,1},{1,2},{2,3},{3,0},{4,5},{5,6},{6,7},{7,4},{8,9},{9,10},{10,1... | collective-permute-start | bytes 24584 | tf_op jit(solution)/shard_map/ppermute | solution.py:43
  117.7 5.4 %collective-permute-start.9 = (f32[4,512]{1,0:T(4,128)S(1)}, f32[4,512]{1,0:T(4,128)S(1)}, u32[]{:S(2)}, u32[]{:S(2)}) collective-permute-start(f32[4,512]{1,0:T(4,128)S(1)} %get-tuple-element.23), channel_id=1, source_target_pairs={{0,3},{1,0},{2,1},{3,2},{4,7},{5,4},{6,5},{7,6},{8,11},{9,8},{10,9... | collective-permute-start | bytes 24584 | tf_op jit(solution)/shard_map/ppermute | solution.py:45

commit v3 on v2

--- a/solution.py
+++ b/solution.py
@@ -62,10 +62,12 @@
 
 def pair_kernel(
     width,
+    stage,
     plan_ref,
     pairs_ref,
     *refs,
 ):
+    before_ref = refs[0] if stage else None
     (
         *table_refs,
         to_centre_ref,
@@ -84,7 +86,7 @@
         pick_i_ref,
         pick_j_ref,
         terms_ref,
-    ) = refs
+    ) = refs[1:] if stage else refs
     basis_count = radial_two_ref.shape[0] // 2
     atoms = centre_ref.shape[1]
     lanes = pairs_ref.shape[2]
@@ -127,7 +129,7 @@
 
     def begin_part(part):
         listed = pairs_ref[part]
-        least = plan_ref[2 * part + 1]
+        least = plan_ref[2 * part + 3]
         after = jnp.minimum(least + 1, image_ref.shape[0] - 1)
         pick_i = pick(atoms, listed[0:1])
         pick_j = pick(2 * width, listed[1:2] - least * width)
@@ -223,7 +225,7 @@
                 pre_ref[lane] += lower(image_ref[window], pick(width, entries))
                 return carry
 
-            lax.fori_loop(plan_ref[2 * part + 1] + 2, plan_ref[2 * part + 2] + 1, gather, 0)
+            lax.fori_loop(plan_ref[2 * part + 3] + 2, plan_ref[2 * part + 4] + 1, gather, 0)
 
         shapes = [geometry(part, lane) for lane, part in enumerate(parts)]
         ones = [first_layer(shape[-1]) for shape in shapes]
@@ -238,7 +240,7 @@
             back_basis = from_grad[:basis_count] + from_grad[basis_count:]
             terms_ref[lane] = pair_terms(part, lane, shapes[lane], back_basis, backs[lane][1])
         for lane, part in enumerate(parts):
-            least = plan_ref[2 * part + 1]
+            least = plan_ref[2 * part + 3]
             after = jnp.minimum(least + 1, image_ref.shape[0] - 1)
             terms = terms_ref[lane]
             sum_i_ref[...] += spill(terms, pick_i_ref[lane])
@@ -251,10 +253,10 @@
                 sum_j_ref[window] += spill(terms_ref[lane], pick(width, entries))
                 return carry
 
-            lax.fori_loop(plan_ref[2 * part + 1] + 2, plan_ref[2 * part + 2] + 1, scatter, 0)
+            lax.fori_loop(plan_ref[2 * part + 3] + 2, plan_ref[2 * part + 4] + 1, scatter, 0)
         return carry
 
-    lax.fori_loop(0, plan_ref[0], step, 0)
+    lax.fori_loop(plan_ref[stage], plan_ref[stage + 1], step, 0)
 
     def finish(index, carry):
         for cut in range(cuts):
@@ -264,6 +266,8 @@
 
     lax.fori_loop(0, out_ref.shape[0], finish, 0)
     out_ref[0] += sum_i_ref[0:4, :] + sum_i_ref[8:12, :]
+    if stage:
+        out_ref[: before_ref.shape[0]] += before_ref[...]
 
 
 def local(
@@ -299,7 +303,6 @@
 
     column = jnp.stack(widen(own, "gz"))
     plane = jnp.concatenate(widen(column, "gx"))
-    tables = widen(plane, "gy")
 
     entry = pair_second[0, 0, 0].reshape(-1)
     slot = entry // atoms
@@ -331,8 +334,10 @@
     listed = jnp.stack(rows, axis=1)
     window = jnp.minimum(second // width, bricks * atoms // width - 1)
     live = (valid + subs * lanes - 1) // (subs * lanes)
+    near = spans[0] * spans[2]
+    first_part = jnp.sum((second < near * atoms).astype(jnp.int32)) // (subs * lanes)
     plan = jnp.concatenate(
-        [live[None], jnp.stack([window[:, 0], jnp.max(window, axis=1)], axis=1).reshape(-1)]
+        [jnp.stack([jnp.zeros_like(live), first_part, live]), jnp.stack([window[:, 0], jnp.max(window, axis=1)], axis=1).reshape(-1)]
     ).astype(jnp.int32)
 
     carry_j = [[0.0] * part_rows for _ in range(part_rows)]
@@ -359,28 +364,41 @@
     radial_two = jnp.concatenate([radial_high, radial_low], axis=0).astype(jnp.bfloat16)
 
     vmem = pl.BlockSpec(memory_space=pltpu.VMEM)
-    operands = [listed, *tables]
-    operands += [with_parts(w_centre, carry_i), with_parts(w_neighbour, carry_j)]
-    operands += [radial_cat, radial_two, w_hidden, w_hidden.T, w_energy[:, None]]
-    windows = bricks * atoms // width
-    partial = pl.pallas_call(
-        functools.partial(pair_kernel, width),
-        out_shape=jax.ShapeDtypeStruct((bricks, 4, atoms), jnp.float32),
-        in_specs=[pl.BlockSpec(memory_space=pltpu.SMEM)] + [vmem] * len(operands),
-        out_specs=vmem,
-        scratch_shapes=[
-            pltpu.VMEM((hid + part_rows, atoms), jnp.bfloat16),
-            pltpu.VMEM((windows, hid + part_rows, width), jnp.bfloat16),
-            pltpu.VMEM((subs, hid + part_rows, lanes), jnp.float32),
-            pltpu.VMEM((16, atoms), jnp.float32),
-            pltpu.VMEM((windows, 16, width), jnp.float32),
-            pltpu.VMEM((subs, atoms, lanes), jnp.bfloat16),
-            pltpu.VMEM((subs, 2 * width, lanes), jnp.bfloat16),
-            pltpu.VMEM((subs, 16, lanes), jnp.bfloat16),
-        ],
-        compiler_params=pltpu.CompilerParams(vmem_limit_bytes=48 * 1024 * 1024),
-        name="pairs",
-    )(plan, *operands)
+    weights = [with_parts(w_centre, carry_i), with_parts(w_neighbour, carry_j)]
+    weights += [radial_cat, radial_two, w_hidden, w_hidden.T, w_energy[:, None]]
+    plane, listed, plan, *weights = lax.optimization_barrier((plane, listed, plan, *weights))
+    tables = widen(plane, "gy")
+
+    def run(stage, before, images, count):
+        operands = [listed, *before, *images, *weights]
+        windows = count * atoms // width
+        pairs = key.size // (2 - stage) // 2
+        return pl.pallas_call(
+            functools.partial(pair_kernel, width, stage),
+            out_shape=jax.ShapeDtypeStruct((count, 4, atoms), jnp.float32),
+            in_specs=[pl.BlockSpec(memory_space=pltpu.SMEM)] + [vmem] * len(operands),
+            out_specs=vmem,
+            scratch_shapes=[
+                pltpu.VMEM((hid + part_rows, atoms), jnp.bfloat16),
+                pltpu.VMEM((windows, hid + part_rows, width), jnp.bfloat16),
+                pltpu.VMEM((subs, hid + part_rows, lanes), jnp.float32),
+                pltpu.VMEM((16, atoms), jnp.float32),
+                pltpu.VMEM((windows, 16, width), jnp.float32),
+                pltpu.VMEM((subs, atoms, lanes), jnp.bfloat16),
+                pltpu.VMEM((subs, 2 * width, lanes), jnp.bfloat16),
+                pltpu.VMEM((subs, 16, lanes), jnp.bfloat16),
+            ],
+            compiler_params=pltpu.CompilerParams(vmem_limit_bytes=48 * 1024 * 1024),
+            cost_estimate=pl.CostEstimate(
+                flops=pairs * hid * (4 * hid + 2 * atoms + 4 * width),
+                bytes_accessed=count * atoms * 2 * feat,
+                transcendentals=pairs * 2 * hid,
+            ),
+            name="near_pairs" if stage == 0 else "far_pairs",
+        )(plan, *operands)
+
+    partial = run(0, [], tables[:1], near)
+    partial = run(1, [partial], tables, bricks)
     partial = partial.reshape(spans[1], spans[0], spans[2], 4, atoms)
     partial = fold(partial, "gy")
     partial = fold(partial, "gx")

time: 125 us -> 114 us (0.912)
  starting transfers between devices: 39.8 us -> 13.2 us
  Pallas kernels: 35.7 us -> 57.4 us
  local copies, waits for them, and re-layouts: 10.5 us -> 5.58 us
  other arithmetic: 13.8 us -> 10.9 us
  between operations: 2.99 us -> 5.69 us
    ppermute x3, starting transfers between devices: 27.3 us -> 0.63 us  [fold(): total = blocks[0] + lax.ppermute(blocks[1], axis, ring(axis, 1))]
    pallas_call x1 -> x2, Pallas kernels: 35.7 us -> 57.4 us  [run(): pl.pallas_call(functools.partial(pair_kernel, width, stage), out_shape=ja...]
    ppermute x2, waiting for transfers between devices: 7.1 us -> 1.06 us  [widen(): parts.append(lax.ppermute(block, axis, ring(axis, 1)))]
    ppermute x3, waiting for transfers between devices: 3.65 us -> 7.5 us  [fold(): total = blocks[0] + lax.ppermute(blocks[1], axis, ring(axis, 1))]
    unnamed x36 -> x30, local copies, waits for them, and re-layouts: 6.09 us -> 2.77 us
    another operation x2, local copies, waits for them, and re-layouts: 2.32 us -> 0.77 us  [local(): listed = jnp.stack(rows, axis=1)]
  transfers between devices with their start and end apart: 10 -> 10, of which waited for: 7 -> 7; matrix products, arithmetic and copies ran while one was open for 15% -> 10% of each run, Pallas kernels for 0% -> 15%
where the time goes in v3:
time: 114 us; the launch traced here: 113 us
  Pallas kernels  57.4 us (50%)
  waiting for transfers between devices  20.5 us (18%)
  starting transfers between devices  13.2 us (12%)
  other arithmetic  10.9 us (10%)
  between operations  5.69 us (5%)
  local copies, waits for them, and re-layouts  5.58 us (5%)
    pallas_call x2, Pallas kernels, run(): pl.pallas_call(functools.partial(pair_kernel, width, stage), out_shape=ja...  57.4 us
    ppermute x3, waiting for transfers between devices, widen(): parts = [block, lax.ppermute(block, axis, ring(axis, -1))]  10.7 us
    ppermute x3, waiting for transfers between devices, fold(): total = blocks[0] + lax.ppermute(blocks[1], axis, ring(axis, 1))  7.5 us
    sort x1, other arithmetic, local(): key = lax.sort(key, is_stable=False)  6.29 us
    ppermute x3, starting transfers between devices, widen(): parts = [block, lax.ppermute(block, axis, ring(axis, -1))]  5.54 us
    ppermute x2, starting transfers between devices, fold(): total = total + lax.ppermute(blocks[2], axis, ring(axis, -1))  3.87 us
    ppermute x2, starting transfers between devices, widen(): parts.append(lax.ppermute(block, axis, ring(axis, 1)))  3.13 us
    unnamed x30, local copies, waits for them, and re-layouts  2.77 us
  transfers between devices with their start and end apart: 10, of which 7 were waited for; matrix products, arithmetic and copies ran while one was open for 10% of the time, Pallas kernels for 15%

profile of v3, /device:TPU:0, one launch (start us, length us, event | category | flops | bytes accessed | tf_op | source)
XLA Modules:
  0.0 113.4 jit_solution(13595648884339930165)
XLA Ops:
  1.3 1.1 copy.48
  2.5 0.6 select_reduce_fusion
  3.9 0.6 copy-done.11
  4.6 0.2 concatenate.39
  4.8 3.1 %collective-permute-start.1 = (bf16[144,512]{1,0:T(8,128)(2,1)S(1)}, bf16[144,512]{1,0:T(8,128)(2,1)S(1)}, u32[]{:S(2)}, u32[]{:S(2)}) collective-permute-start(bf16[144,512]{1,0:T(8,128)(2,1)S(1)} %concatenate.39), channel_id=1, source_target_pairs={{0,1},{1,2},{2,3},{3,0},{4,5},{5,6},{6,7},{7,4},{8,9},{9,10},{10,1... | collective-permute-start | bytes 442376 | tf_op jit(solution)/shard_map/ppermute | solution.py:38
  7.8 2.1 %collective-permute-start = (bf16[144,512]{1,0:T(8,128)(2,1)S(1)}, bf16[144,512]{1,0:T(8,128)(2,1)S(1)}, u32[]{:S(2)}, u32[]{:S(2)}) collective-permute-start(bf16[144,512]{1,0:T(8,128)(2,1)S(1)} %concatenate.39), channel_id=1, source_target_pairs={{0,3},{1,0},{2,1},{3,2},{4,7},{5,4},{6,5},{7,6},{8,11},{9,8},{10,9... | collective-permute-start | bytes 442376 | tf_op jit(solution)/shard_map/ppermute | solution.py:36
  9.9 0.6 convert_reduce_fusion
  10.6 0.3 fusion.14
  10.8 6.3 %sort.7 = s32[16384]{0:T(1024)S(1)} sort(s32[16384]{0:T(1024)S(1)} %fusion.14), dimensions={0}, to_apply=%region_1.2 | sort | flops 229376 | bytes 131072 | tf_op jit(solution)/shard_map/sort | solution.py:317
  17.1 0.7 convert_reduce_fusion.1
  18.0 0.2 fusion.41
  18.2 0.7 fusion.24
  18.9 0.9 fusion.23
  19.9 0.2 compare_convert_fusion
  23.7 0.6 copy-done.1
  24.5 0.1 reshape.279
  24.8 0.7 stack.41.pairs_ref
  25.6 1.7 %collective-permute-start.2 = (bf16[3,144,512]{2,1,0:T(8,128)(2,1)S(1)}, bf16[3,144,512]{2,1,0:T(8,128)(2,1)S(1)}, u32[]{:S(2)}, u32[]{:S(2)}) collective-permute-start(bf16[3,144,512]{2,1,0:T(8,128)(2,1)S(1)} %pad_maximum_fusion.1), channel_id=1, source_target_pairs={{0,16},{16,0},{1,17},{17,1},{2,18},{18,2},{3,19},{19,3},{4,20},{20... | collective-permute-start | bytes 1327112 | tf_op jit(solution)/shard_map/ppermute | solution.py:36
  27.5 9.8 %collective-permute-done.2 = bf16[3,144,512]{2,1,0:T(8,128)(2,1)S(1)} collective-permute-done((bf16[3,144,512]{2,1,0:T(8,128)(2,1)S(1)}, bf16[3,144,512]{2,1,0:T(8,128)(2,1)S(1)}, u32[]{:S(2)}, u32[]{:S(2)}) %collective-permute-start.2) | collective-permute-done | bytes 442400 | tf_op jit(solution)/shard_map/ppermute | solution.py:36
  37.5 1.7 %collective-permute-start.3 = (bf16[6,144,512]{2,1,0:T(8,128)(2,1)S(1)}, bf16[6,144,512]{2,1,0:T(8,128)(2,1)}, u32[]{:S(2)}, u32[]{:S(2)}) collective-permute-start(bf16[6,144,512]{2,1,0:T(8,128)(2,1)S(1)} %pad_maximum_fusion.refs_0_.refs_1_), channel_id=1, source_target_pairs={{0,12},{4,0},{8,4},{12,8},{1,13},{5,1},{9,5},{13,9},{2,14},{6,2},{... | collective-permute-start | bytes 2654216 | tf_op jit(solution)/shard_map/ppermute | solution.py:36
  39.5 17.0 %near_pairs.1.refs_0_ = f32[6,4,512]{2,1,0:T(4,128)S(1)} custom-call(s32[131]{0:T(256)S(1)} %pad_add_fusion.1.plan_ref, s32[64,8,256]{2,1,0:T(8,128)S(1)} %stack.41.pairs_ref, bf16[6,144,512]{2,1,0:T(8,128)(2,1)S(1)} %pad_maximum_fusion.refs_0_.refs_1_, bf16[272,144]{1,0:T(8,128)(2,1)S(1)} %get-tuple-element.15.refs_1_.refs_4_, ...), custom_call_target="tpu_custom_call" | custom-call | flops 3221225472 | bytes 786432 | tf_op jit(solution)/shard_map/near_pairs/pallas_call | solution.py:376
  56.5 1.1 collective-permute-done.4.refs_3_
  57.5 0.9 collective-permute-done.3.refs_2_
  58.5 40.4 %far_pairs.1 = f32[18,4,512]{2,1,0:T(4,128)S(1)} custom-call(s32[131]{0:T(256)S(1)} %pad_add_fusion.1.plan_ref, s32[64,8,256]{2,1,0:T(8,128)S(1)} %stack.41.pairs_ref, f32[6,4,512]{2,1,0:T(4,128)S(1)} %near_pairs.1.refs_0_, bf16[6,144,512]{2,1,0:T(8,128)(2,1)S(1)} %pad_maximum_fusion.refs_0_.refs_1_, bf16[6,144,512]{2,1,0:T(8,128)(2,1)} %collective-permute-done.3.refs_2_, ...), custom_call_target="tpu_custom_call" | custom-call | flops 6442450944 | bytes 2359296 | tf_op jit(solution)/shard_map/far_pairs/pallas_call | solution.py:376
  99.0 0.5 collective-permute-start.5
  99.5 1.2 %collective-permute-done.6 = f32[2,3,4,512]{3,2,1,0:T(4,128)S(1)} collective-permute-done((f32[2,3,4,512]{3,2,1,0:T(4,128)S(1)}, f32[2,3,4,512]{3,2,1,0:T(4,128)S(1)}, u32[]{:S(2)}, u32[]{:S(2)}) %collective-permute-start.6) | collective-permute-done | bytes 49184 | tf_op jit(solution)/shard_map/ppermute | solution.py:45
  100.7 2.1 %collective-permute-done.5 = f32[2,3,4,512]{3,2,1,0:T(4,128)S(1)} collective-permute-done((f32[2,3,4,512]{3,2,1,0:T(4,128)S(1)}, f32[2,3,4,512]{3,2,1,0:T(4,128)S(1)}, u32[]{:S(2)}, u32[]{:S(2)}) %collective-permute-start.5) | collective-permute-done | bytes 49184 | tf_op jit(solution)/shard_map/ppermute | solution.py:43
  102.9 3.8 %collective-permute-done.7 = f32[3,4,512]{2,1,0:T(4,128)S(1)} collective-permute-done((f32[3,4,512]{2,1,0:T(4,128)S(1)}, f32[3,4,512]{2,1,0:T(4,128)S(1)}, u32[]{:S(2)}, u32[]{:S(2)}) %collective-permute-start.7) | collective-permute-done | bytes 24608 | tf_op jit(solution)/shard_map/ppermute | solution.py:43
  106.8 3.8 %collective-permute-start.9 = (f32[4,512]{1,0:T(4,128)S(1)}, f32[4,512]{1,0:T(4,128)S(1)}, u32[]{:S(2)}, u32[]{:S(2)}) collective-permute-start(f32[4,512]{1,0:T(4,128)S(1)} %get-tuple-element.44), channel_id=1, source_target_pairs={{0,3},{1,0},{2,1},{3,2},{4,7},{5,4},{6,5},{7,6},{8,11},{9,8},{10,9... | collective-permute-start | bytes 24584 | tf_op jit(solution)/shard_map/ppermute | solution.py:45
  110.6 1.6 %collective-permute-done.8 = f32[4,512]{1,0:T(4,128)S(1)} collective-permute-done((f32[4,512]{1,0:T(4,128)S(1)}, f32[4,512]{1,0:T(4,128)S(1)}, u32[]{:S(2)}, u32[]{:S(2)}) %collective-permute-start.8) | collective-permute-done | bytes 8224 | tf_op jit(solution)/shard_map/ppermute | solution.py:43
  112.3 0.6 slice_bitcast_fusion.5
  112.8 0.6 broadcast_in_dim.34
  (66 shorter events, 1.9 us)
Async XLA Ops:
  0.6 1.8 %copy-start = (bf16[128]{0:T(256)(128)(2,1)S(1)}, bf16[128]{0:T(256)(128)(2,1)}, u32[]{:S(2)}) copy-start(bf16[128]{0:T(256)(128)(2,1)} %param.22) | copy-start | bytes 772
  1.3 1.1 copy-start.2
  3.8 0.7 copy-start.11
  4.6 5.4 %copy-start.8 = (f32[8,256]{1,0:T(8,128)S(1)}, f32[8,256]{1,0:T(8,128)}, u32[]{:S(2)}) copy-start(f32[8,256]{1,0:T(8,128)} %param.23) | copy-start | bytes 24580
  4.6 5.4 %copy-start.3 = (s32[1,1,1,128,128]{4,3,2,1,0:T(8,128)S(1)}, s32[1,1,1,128,128]{4,3,2,1,0:T(8,128)}, u32[]{:S(2)}) copy-start(s32[1,1,1,128,128]{4,3,2,1,0:T(8,128)} %param.19) | copy-start | bytes 196612
  4.6 6.0 %copy-start.5 = (s32[1,1,1,128,128]{4,3,2,1,0:T(8,128)S(1)}, s32[1,1,1,128,128]{4,3,2,1,0:T(8,128)}, u32[]{:S(2)}) copy-start(s32[1,1,1,128,128]{4,3,2,1,0:T(8,128)} %param.18) | copy-start | bytes 196612
  4.8 5.8 %copy-start.4 = (s32[1,1,1,128,128]{4,3,2,1,0:T(8,128)S(1)}, s32[1,1,1,128,128]{4,3,2,1,0:T(8,128)}, u32[]{:S(2)}) copy-start(s32[1,1,1,128,128]{4,3,2,1,0:T(8,128)} %param.17) | copy-start | bytes 196612
  4.8 20.8 %collective-permute-start.1 = (bf16[144,512]{1,0:T(8,128)(2,1)S(1)}, bf16[144,512]{1,0:T(8,128)(2,1)S(1)}, u32[]{:S(2)}, u32[]{:S(2)}) collective-permute-start(bf16[144,512]{1,0:T(8,128)(2,1)S(1)} %concatenate.39), channel_id=1, source_target_pairs={{0,1},{1,2},{2,3},{3,0},{4,5},{5,6},{6,7},{7,4},{8,9},{9,10},{10,1... | collective-permute-start | bytes 442376 | tf_op jit(solution)/shard_map/ppermute | solution.py:38
  7.8 17.7 %collective-permute-start = (bf16[144,512]{1,0:T(8,128)(2,1)S(1)}, bf16[144,512]{1,0:T(8,128)(2,1)S(1)}, u32[]{:S(2)}, u32[]{:S(2)}) collective-permute-start(bf16[144,512]{1,0:T(8,128)(2,1)S(1)} %concatenate.39), channel_id=1, source_target_pairs={{0,3},{1,0},{2,1},{3,2},{4,7},{5,4},{6,5},{7,6},{8,11},{9,8},{10,9... | collective-permute-start | bytes 442376 | tf_op jit(solution)/shard_map/ppermute | solution.py:36
  20.1 3.4 %copy-start.6 = (bf16[128,256]{1,0:T(8,128)(2,1)S(1)}, bf16[128,256]{1,0:T(8,128)(2,1)}, u32[]{:S(2)}) copy-start(bf16[128,256]{1,0:T(8,128)(2,1)} %param.20) | copy-start | bytes 196612
  20.8 2.8 %copy-start.7 = (bf16[128,256]{1,0:T(8,128)(2,1)S(1)}, bf16[128,256]{1,0:T(8,128)(2,1)}, u32[]{:S(2)}) copy-start(bf16[128,256]{1,0:T(8,128)(2,1)} %param.21) | copy-start | bytes 196612
  23.5 0.9 copy-start.1
  25.5 1.9 %copy-start.10 = (bf16[16,144]{1,0:T(8,128)(2,1)S(1)}, bf16[16,144]{1,0:T(8,128)(2,1)}, u32[]{:S(2)}) copy-start(bf16[16,144]{1,0:T(8,128)(2,1)} %constant.176) | copy-start | bytes 13828
  25.6 1.8 %copy-start.9 = (bf16[16,144]{1,0:T(8,128)(2,1)S(1)}, bf16[16,144]{1,0:T(8,128)(2,1)}, u32[]{:S(2)}) copy-start(bf16[16,144]{1,0:T(8,128)(2,1)} %constant.177) | copy-start | bytes 13828
  25.6 11.7 %collective-permute-start.2 = (bf16[3,144,512]{2,1,0:T(8,128)(2,1)S(1)}, bf16[3,144,512]{2,1,0:T(8,128)(2,1)S(1)}, u32[]{:S(2)}, u32[]{:S(2)}) collective-permute-start(bf16[3,144,512]{2,1,0:T(8,128)(2,1)S(1)} %pad_maximum_fusion.1), channel_id=1, source_target_pairs={{0,16},{16,0},{1,17},{17,1},{2,18},{18,2},{3,19},{19,3},{4,20},{20... | collective-permute-start | bytes 1327112 | tf_op jit(solution)/shard_map/ppermute | solution.py:36
  37.4 1.9 %copy-start.12 = (f32[256]{0:T(256)S(1)}, f32[256]{0:T(256)}, u32[]{:S(2)}) copy-start(f32[256]{0:T(256)} %param.25) | copy-start | bytes 3076
  37.4 20.1 %collective-permute-start.4 = (bf16[6,144,512]{2,1,0:T(8,128)(2,1)S(1)}, bf16[6,144,512]{2,1,0:T(8,128)(2,1)S(1)}, u32[]{:S(2)}, u32[]{:S(2)}) collective-permute-start(bf16[6,144,512]{2,1,0:T(8,128)(2,1)S(1)} %pad_maximum_fusion.refs_0_.refs_1_), channel_id=1, source_target_pairs={{0,4},{4,8},{8,12},{12,0},{1,5},{5,9},{9,13},{13,1},{2,6},{6,10},{... | collective-permute-start | bytes 2654216 | tf_op jit(solution)/shard_map/ppermute | solution.py:38
  37.5 21.0 %collective-permute-start.3 = (bf16[6,144,512]{2,1,0:T(8,128)(2,1)S(1)}, bf16[6,144,512]{2,1,0:T(8,128)(2,1)}, u32[]{:S(2)}, u32[]{:S(2)}) collective-permute-start(bf16[6,144,512]{2,1,0:T(8,128)(2,1)S(1)} %pad_maximum_fusion.refs_0_.refs_1_), channel_id=1, source_target_pairs={{0,12},{4,0},{8,4},{12,8},{1,13},{5,1},{9,5},{13,9},{2,14},{6,2},{... | collective-permute-start | bytes 2654216 | tf_op jit(solution)/shard_map/ppermute | solution.py:36
  98.9 1.8 %collective-permute-start.6 = (f32[2,3,4,512]{3,2,1,0:T(4,128)S(1)}, f32[2,3,4,512]{3,2,1,0:T(4,128)S(1)}, u32[]{:S(2)}, u32[]{:S(2)}) collective-permute-start(f32[2,3,4,512]{3,2,1,0:T(4,128)S(1)} %bitcast.96), channel_id=1, source_target_pairs={{0,12},{4,0},{8,4},{12,8},{1,13},{5,1},{9,5},{13,9},{2,14},{6,2},{... | collective-permute-start | bytes 147464 | tf_op jit(solution)/shard_map/ppermute | solution.py:45
  99.0 3.8 %collective-permute-start.5 = (f32[2,3,4,512]{3,2,1,0:T(4,128)S(1)}, f32[2,3,4,512]{3,2,1,0:T(4,128)S(1)}, u32[]{:S(2)}, u32[]{:S(2)}) collective-permute-start(f32[2,3,4,512]{3,2,1,0:T(4,128)S(1)} %bitcast.95), channel_id=1, source_target_pairs={{0,4},{4,8},{8,12},{12,0},{1,5},{5,9},{9,13},{13,1},{2,6},{6,10},{... | collective-permute-start | bytes 147464 | tf_op jit(solution)/shard_map/ppermute | solution.py:43
  102.8 3.9 %collective-permute-start.7 = (f32[3,4,512]{2,1,0:T(4,128)S(1)}, f32[3,4,512]{2,1,0:T(4,128)S(1)}, u32[]{:S(2)}, u32[]{:S(2)}) collective-permute-start(f32[3,4,512]{2,1,0:T(4,128)S(1)} %slice_bitcast_fusion), channel_id=1, source_target_pairs={{0,16},{16,0},{1,17},{17,1},{2,18},{18,2},{3,19},{19,3},{4,20},{20... | collective-permute-start | bytes 73736 | tf_op jit(solution)/shard_map/ppermute | solution.py:43
  106.8 5.5 %collective-permute-start.8 = (f32[4,512]{1,0:T(4,128)S(1)}, f32[4,512]{1,0:T(4,128)S(1)}, u32[]{:S(2)}, u32[]{:S(2)}) collective-permute-start(f32[4,512]{1,0:T(4,128)S(1)} %get-tuple-element.43), channel_id=1, source_target_pairs={{0,1},{1,2},{2,3},{3,0},{4,5},{5,6},{6,7},{7,4},{8,9},{9,10},{10,1... | collective-permute-start | bytes 24584 | tf_op jit(solution)/shard_map/ppermute | solution.py:43
  106.8 5.4 %collective-permute-start.9 = (f32[4,512]{1,0:T(4,128)S(1)}, f32[4,512]{1,0:T(4,128)S(1)}, u32[]{:S(2)}, u32[]{:S(2)}) collective-permute-start(f32[4,512]{1,0:T(4,128)S(1)} %get-tuple-element.44), channel_id=1, source_target_pairs={{0,3},{1,0},{2,1},{3,2},{4,7},{5,4},{6,5},{7,6},{8,11},{9,8},{10,9... | collective-permute-start | bytes 24584 | tf_op jit(solution)/shard_map/ppermute | solution.py:45

commit v4 on v3

--- a/solution.py
+++ b/solution.py
@@ -61,7 +61,6 @@
 
 
 def pair_kernel(
-    width,
     stage,
     plan_ref,
     pairs_ref,
@@ -70,42 +69,45 @@
     before_ref = refs[0] if stage else None
     (
         *table_refs,
-        to_centre_ref,
-        to_image_ref,
+        project_ref,
         radial_cat_ref,
         radial_two_ref,
         hidden_ref,
         hidden_t_ref,
         energy_ref,
         out_ref,
-        centre_ref,
         image_ref,
-        pre_ref,
+        own_ref,
+        other_ref,
         sum_i_ref,
         sum_j_ref,
         pick_i_ref,
         pick_j_ref,
         terms_ref,
+        copied,
     ) = refs[1:] if stage else refs
     basis_count = radial_two_ref.shape[0] // 2
-    atoms = centre_ref.shape[1]
+    width = image_ref.shape[2]
+    feat = image_ref.shape[1] - part_rows
+    atoms = out_ref.shape[2]
     lanes = pairs_ref.shape[2]
-    hid = hidden_ref.shape[0]
     cuts = atoms // width
 
-    centre_ref[...] = lower(to_centre_ref[...], table_refs[0][0]).astype(jnp.bfloat16)
+    copies = []
     begin = 0
-    for table_ref in table_refs:
-        def project(index, carry, table_ref=table_ref, begin=begin):
-            image = lower(to_image_ref[...], table_ref[index]).astype(jnp.bfloat16)
-            for cut in range(cuts):
-                image_ref[(begin + index) * cuts + cut] = image[:, cut * width : (cut + 1) * width]
-            return carry
-
-        lax.fori_loop(0, table_ref.shape[0], project, 0)
+    for index, table_ref in enumerate(table_refs):
+        copies.append(
+            pltpu.make_async_copy(
+                table_ref, image_ref.at[begin : begin + table_ref.shape[0]], copied.at[index]
+            )
+        )
         begin += table_ref.shape[0]
+    for copy in copies:
+        copy.start()
     sum_i_ref[...] = jnp.zeros_like(sum_i_ref)
     sum_j_ref[...] = jnp.zeros_like(sum_j_ref)
+    for copy in copies:
+        copy.wait()
 
     chunk = 16
     ladder = lax.broadcasted_iota(jnp.int32, (chunk, lanes), 0).astype(jnp.int16)
@@ -127,24 +129,33 @@
     def spill(terms, picked):
         return lax.dot_general(terms, picked, across, preferred_element_type=jnp.float32)
 
-    def begin_part(part):
+    def begin_part(part, lane):
         listed = pairs_ref[part]
         least = plan_ref[2 * part + 3]
         after = jnp.minimum(least + 1, image_ref.shape[0] - 1)
         pick_i = pick(atoms, listed[0:1])
         pick_j = pick(2 * width, listed[1:2] - least * width)
-        pre = lower(centre_ref[...], pick_i)
-        pre += lower(image_ref[least], pick_j[:width])
-        pre += lower(image_ref[after], pick_j[width:])
-        return pre, pick_i, pick_j
+        own = lower(image_ref[0], pick_i[:width])
+        for cut in range(1, cuts):
+            own += lower(image_ref[cut], pick_i[cut * width : (cut + 1) * width])
+        other = lower(image_ref[least], pick_j[:width])
+        other += lower(image_ref[after], pick_j[width:])
+        own_ref[lane] = own
+        other_ref[lane] = other
+        pick_i_ref[lane] = pick_i
+        pick_j_ref[lane] = pick_j
+
+    def whole(ref, lane):
+        parts = ref[lane, feat:, :]
+        return (parts[0:4] + parts[4:8]) + parts[8:12]
 
     def geometry(part, lane):
-        listed = pairs_ref[part]
-        extra = pre_ref[lane, hid:, :]
-        sep_x = (extra[0:1] + extra[3:4]) + extra[6:7] + listed[2:3].astype(jnp.float32)
-        sep_y = (extra[1:2] + extra[4:5]) + extra[7:8] + listed[3:4].astype(jnp.float32)
-        sep_z = (extra[2:3] + extra[5:6]) + extra[8:9] + listed[4:5].astype(jnp.float32)
-        dist_sq = sep_x * sep_x + sep_y * sep_y + sep_z * sep_z + delta_sq
+        shift = pairs_ref[part][4:8].astype(jnp.float32)
+        at_i = whole(own_ref, lane)
+        at_j = whole(other_ref, lane)
+        sep = at_j - at_i + shift
+        square = sep * sep
+        dist_sq = square[0:1] + square[1:2] + square[2:3] + delta_sq
         distance = jnp.sqrt(dist_sq)
         order = lax.broadcasted_iota(jnp.int32, (basis_count, lanes), 0).astype(jnp.float32)
         offset = distance - (0.25 + 0.3 * order)
@@ -153,8 +164,10 @@
         basis_cat = jnp.concatenate(
             [basis_high, basis - basis_high, basis_high, jnp.zeros_like(basis)], axis=0
         ).astype(jnp.bfloat16)
-        pre_one = pre_ref[lane, :hid, :] + lower(radial_cat_ref[...], basis_cat)
-        return (sep_x, sep_y, sep_z), dist_sq, distance, offset, basis, pre_one
+        both = jnp.concatenate([own_ref[lane, :feat, :], other_ref[lane, :feat, :]], axis=0)
+        pre_one = lower(project_ref[...], both.astype(jnp.bfloat16))
+        pre_one += lower(radial_cat_ref[...], basis_cat)
+        return (at_i, at_j, sep), dist_sq, distance, offset, basis, pre_one
 
     def first_layer(pre_one):
         gate = 0.5 * jnp.tanh(0.5 * pre_one) + 0.5
@@ -171,11 +184,10 @@
         return back, readout * envelope
 
     def pair_terms(part, lane, shape, back_basis, readout):
-        (sep_x, sep_y, sep_z), dist_sq, distance, offset, basis, _ = shape
-        weight = pairs_ref[part][5:6].astype(jnp.float32)
-        extra = pre_ref[lane, hid:, :]
-        charge_i = extra[9:10] + extra[10:11] + extra[11:12]
-        charge_j = extra[12:13] + extra[13:14] + extra[14:15]
+        (at_i, at_j, sep), dist_sq, distance, offset, basis, _ = shape
+        weight = pairs_ref[part][2:3].astype(jnp.float32)
+        charge_i = at_i[3:4]
+        charge_j = at_j[3:4]
         inverse = 1.0 / distance
         slope_nn = (
             jnp.sum(
@@ -191,22 +203,11 @@
         potential = screened * inverse
         slope_coul = -(2.0 / root_pi) * jnp.exp(-dist_sq) * inverse - potential * inverse
         slope = weight * (slope_nn + coulomb * charge_i * charge_j * slope_coul) * inverse
-        push_x = slope * sep_x
-        push_y = slope * sep_y
-        push_z = slope * sep_z
+        push = slope * sep
         shared = weight * coulomb * potential
+        last = lax.broadcasted_iota(jnp.int32, push.shape, 0) == 3
         terms = jnp.concatenate(
-            [
-                push_x,
-                push_y,
-                push_z,
-                shared * charge_j,
-                -push_x,
-                -push_y,
-                -push_z,
-                shared * charge_i,
-            ],
-            axis=0,
+            [jnp.where(last, shared * at_j, push), jnp.where(last, shared * at_i, -push)], axis=0
         )
         terms_high = terms.astype(jnp.bfloat16).astype(jnp.float32)
         return jnp.concatenate([terms_high, terms - terms_high], axis=0).astype(jnp.bfloat16)
@@ -214,15 +215,12 @@
     def step(block, carry):
         parts = [block * subs + lane for lane in range(subs)]
         for lane, part in enumerate(parts):
-            pre, pick_i, pick_j = begin_part(part)
-            pre_ref[lane] = pre
-            pick_i_ref[lane] = pick_i
-            pick_j_ref[lane] = pick_j
+            begin_part(part, lane)
 
         for lane, part in enumerate(parts):
             def gather(window, carry, lane=lane, part=part):
                 entries = pairs_ref[part][1:2] - window * width
-                pre_ref[lane] += lower(image_ref[window], pick(width, entries))
+                other_ref[lane] += lower(image_ref[window], pick(width, entries))
                 return carry
 
             lax.fori_loop(plan_ref[2 * part + 3] + 2, plan_ref[2 * part + 4] + 1, gather, 0)
@@ -294,15 +292,14 @@
     average = jnp.sum(jnp.where(alive_slot, raw_charge, 0.0)) / filled.astype(jnp.float32)
     charges = jnp.where(alive_slot, raw_charge - average, 0.0)
     own = jnp.concatenate(
-        three_parts(positions[0, 0, 0])
-        + three_parts(charges[None, :])
+        three_parts(jnp.concatenate([positions[0, 0, 0], charges[None, :]], axis=0))
         + [jnp.zeros((part_rows - 12, atoms), jnp.float32)],
         axis=0,
     ).astype(jnp.bfloat16)
+    width = 256 if atoms % 256 == 0 else 128
     own = jnp.concatenate([own_feat.T, own], axis=0)
-
-    column = jnp.stack(widen(own, "gz"))
-    plane = jnp.concatenate(widen(column, "gx"))
+    own = jnp.stack(jnp.split(own, atoms // width, axis=1))
+    column = jnp.concatenate(widen(own, "gz"))
 
     entry = pair_second[0, 0, 0].reshape(-1)
     slot = entry // atoms
@@ -316,21 +313,27 @@
     key = jnp.where(mask, key, bricks * atoms * atoms * 27)
     key = lax.sort(key, is_stable=False)
     valid = jnp.sum(mask.astype(jnp.int32))
+
+    column, key, w_centre, w_neighbour, w_radial, w_hidden, w_energy = lax.optimization_barrier(
+        (column, key, w_centre, w_neighbour, w_radial, w_hidden, w_energy)
+    )
+    plane = jnp.concatenate(widen(column, "gx"))
     lanes = 256 if key.shape[0] % (256 * subs) == 0 else 128
-    width = 256 if atoms % 256 == 0 else 128
     blocks = key.shape[0] // lanes
     key = key.reshape(blocks, lanes)
     sign = key % 27
     second = key // (27 * atoms)
+    nothing = jnp.zeros_like(key)
     rows = [
         key // 27 % atoms,
         second,
+        (second < bricks * atoms).astype(jnp.int32),
+        nothing,
         sign // 9 - 1,
         sign // 3 % 3 - 1,
         sign % 3 - 1,
-        (second < bricks * atoms).astype(jnp.int32),
+        nothing,
     ]
-    rows = rows + [jnp.zeros_like(key)] * 2
     listed = jnp.stack(rows, axis=1)
     window = jnp.minimum(second // width, bricks * atoms // width - 1)
     live = (valid + subs * lanes - 1) // (subs * lanes)
@@ -340,22 +343,6 @@
         [jnp.stack([jnp.zeros_like(live), first_part, live]), jnp.stack([window[:, 0], jnp.max(window, axis=1)], axis=1).reshape(-1)]
     ).astype(jnp.int32)
 
-    carry_j = [[0.0] * part_rows for _ in range(part_rows)]
-    carry_i = [[0.0] * part_rows for _ in range(part_rows)]
-    for part in range(9):
-        carry_j[part][part] = 1.0
-        carry_i[part][part] = -1.0
-    for part in range(3):
-        carry_i[9 + part][9 + part] = 1.0
-        carry_j[12 + part][9 + part] = 1.0
-
-    def with_parts(weight, carried):
-        top = jnp.concatenate([weight.T, jnp.zeros((hid, part_rows), jnp.bfloat16)], axis=1)
-        bottom = jnp.concatenate(
-            [jnp.zeros((part_rows, feat), jnp.bfloat16), jnp.array(carried, jnp.bfloat16)], axis=1
-        )
-        return jnp.concatenate([top, bottom], axis=0)
-
     radial_high = rounded(w_radial)
     radial_low = w_radial - radial_high
     radial_cat = jnp.concatenate(
@@ -364,8 +351,8 @@
     radial_two = jnp.concatenate([radial_high, radial_low], axis=0).astype(jnp.bfloat16)
 
     vmem = pl.BlockSpec(memory_space=pltpu.VMEM)
-    weights = [with_parts(w_centre, carry_i), with_parts(w_neighbour, carry_j)]
-    weights += [radial_cat, radial_two, w_hidden, w_hidden.T, w_energy[:, None]]
+    weights = [jnp.concatenate([w_centre, w_neighbour], axis=0).T, radial_cat, radial_two]
+    weights += [w_hidden, w_hidden.T, w_energy[:, None]]
     plane, listed, plan, *weights = lax.optimization_barrier((plane, listed, plan, *weights))
     tables = widen(plane, "gy")
 
@@ -374,19 +361,23 @@
         windows = count * atoms // width
         pairs = key.size // (2 - stage) // 2
         return pl.pallas_call(
-            functools.partial(pair_kernel, width, stage),
+            functools.partial(pair_kernel, stage),
             out_shape=jax.ShapeDtypeStruct((count, 4, atoms), jnp.float32),
-            in_specs=[pl.BlockSpec(memory_space=pltpu.SMEM)] + [vmem] * len(operands),
+            in_specs=[pl.BlockSpec(memory_space=pltpu.SMEM)]
+            + [vmem] * (1 + len(before))
+            + [pl.BlockSpec(memory_space=pl.ANY)] * len(images)
+            + [vmem] * len(weights),
             out_specs=vmem,
             scratch_shapes=[
-                pltpu.VMEM((hid + part_rows, atoms), jnp.bfloat16),
-                pltpu.VMEM((windows, hid + part_rows, width), jnp.bfloat16),
-                pltpu.VMEM((subs, hid + part_rows, lanes), jnp.float32),
+                pltpu.VMEM((windows, feat + part_rows, width), jnp.bfloat16),
+                pltpu.VMEM((subs, feat + part_rows, lanes), jnp.float32),
+                pltpu.VMEM((subs, feat + part_rows, lanes), jnp.float32),
                 pltpu.VMEM((16, atoms), jnp.float32),
                 pltpu.VMEM((windows, 16, width), jnp.float32),
                 pltpu.VMEM((subs, atoms, lanes), jnp.bfloat16),
                 pltpu.VMEM((subs, 2 * width, lanes), jnp.bfloat16),
                 pltpu.VMEM((subs, 16, lanes), jnp.bfloat16),
+                pltpu.SemaphoreType.DMA((len(images),)),
             ],
             compiler_params=pltpu.CompilerParams(vmem_limit_bytes=48 * 1024 * 1024),
             cost_estimate=pl.CostEstimate(

time: 114 us -> 109 us (0.956)
  Pallas kernels: 57.4 us -> 45.3 us
  starting transfers between devices: 13.2 us -> 20.8 us
    pallas_call x2, Pallas kernels: 57.4 us -> 45.3 us  [run(): pl.pallas_call(functools.partial(pair_kernel, stage), out_shape=jax.Shape...]
    ppermute x3, starting transfers between devices: 0.63 us -> 6.29 us  [fold(): total = blocks[0] + lax.ppermute(blocks[1], axis, ring(axis, 1))]
    ppermute x2, waiting for transfers between devices: 1.06 us -> 4.12 us  [widen(): parts.append(lax.ppermute(block, axis, ring(axis, 1)))]
    ppermute x3, waiting for transfers between devices: 7.5 us -> 4.99 us  [fold(): total = blocks[0] + lax.ppermute(blocks[1], axis, ring(axis, 1))]
    ppermute x2, starting transfers between devices: 3.87 us -> 5.88 us  [fold(): total = total + lax.ppermute(blocks[2], axis, ring(axis, -1))]
    unnamed x30 -> x24, local copies, waits for them, and re-layouts: 2.77 us -> 2.33 us
  transfers between devices with their start and end apart: 10 -> 10, of which waited for: 7 -> 7; matrix products, arithmetic and copies ran while one was open for 10% -> 8% of each run, Pallas kernels for 15% -> 13%
where the time goes in v4:
time: 109 us
  Pallas kernels  45.3 us (42%)
  starting transfers between devices  20.8 us (19%)
  waiting for transfers between devices  20.2 us (19%)
  other arithmetic  10.9 us (10%)
  between operations  5.62 us (5%)
  local copies, waits for them, and re-layouts  5.47 us (5%)
    pallas_call x2, Pallas kernels, run(): pl.pallas_call(functools.partial(pair_kernel, stage), out_shape=jax.Shape...  45.3 us
    ppermute x3, waiting for transfers between devices, widen(): parts = [block, lax.ppermute(block, axis, ring(axis, -1))]  9.65 us
    ppermute x3, starting transfers between devices, fold(): total = blocks[0] + lax.ppermute(blocks[1], axis, ring(axis, 1))  6.29 us
    sort x1, other arithmetic, local(): key = lax.sort(key, is_stable=False)  6.28 us
    ppermute x2, starting transfers between devices, fold(): total = total + lax.ppermute(blocks[2], axis, ring(axis, -1))  5.88 us
    ppermute x3, starting transfers between devices, widen(): parts = [block, lax.ppermute(block, axis, ring(axis, -1))]  5.54 us
    ppermute x3, waiting for transfers between devices, fold(): total = blocks[0] + lax.ppermute(blocks[1], axis, ring(axis, 1))  4.99 us
    ppermute x2, waiting for transfers between devices, widen(): parts.append(lax.ppermute(block, axis, ring(axis, 1)))  4.12 us
  transfers between devices with their start and end apart: 10, of which 7 were waited for; matrix products, arithmetic and copies ran while one was open for 8% of the time, Pallas kernels for 13%

profile of v4, /device:TPU:0, one launch (start us, length us, event | category | flops | bytes accessed | tf_op | source)
XLA Modules:
  0.0 108.5 jit_solution(7331719569119260952)
XLA Ops:
  1.3 1.1 copy.46
  2.6 0.5 copy-done.9
  3.1 0.6 select_reduce_fusion
  4.5 3.1 %collective-permute-start.1 = (bf16[2,144,256]{2,1,0:T(8,128)(2,1)S(1)}, bf16[2,144,256]{2,1,0:T(8,128)(2,1)S(1)}, u32[]{:S(2)}, u32[]{:S(2)}) collective-permute-start(bf16[2,144,256]{2,1,0:T(8,128)(2,1)S(1)} %pad_maximum_fusion.2), channel_id=1, source_target_pairs={{0,1},{1,2},{2,3},{3,0},{4,5},{5,6},{6,7},{7,4},{8,9},{9,10},{10,1... | collective-permute-start | bytes 442376 | tf_op jit(solution)/shard_map/ppermute | solution.py:38
  7.6 2.1 %collective-permute-start = (bf16[2,144,256]{2,1,0:T(8,128)(2,1)S(1)}, bf16[2,144,256]{2,1,0:T(8,128)(2,1)S(1)}, u32[]{:S(2)}, u32[]{:S(2)}) collective-permute-start(bf16[2,144,256]{2,1,0:T(8,128)(2,1)S(1)} %pad_maximum_fusion.2), channel_id=1, source_target_pairs={{0,3},{1,0},{2,1},{3,2},{4,7},{5,4},{6,5},{7,6},{8,11},{9,8},{10,9... | collective-permute-start | bytes 442376 | tf_op jit(solution)/shard_map/ppermute | solution.py:36
  9.7 0.6 convert_reduce_fusion
  10.4 0.3 fusion.10
  11.3 6.3 %sort.7 = s32[16384]{0:T(1024)S(1)} sort(s32[16384]{0:T(1024)S(1)} %fusion.10), dimensions={0}, to_apply=%region_1.2 | sort | flops 229376 | bytes 131072 | tf_op jit(solution)/shard_map/sort | solution.py:314
  17.8 0.7 convert_reduce_fusion.1
  21.4 0.6 copy-done.1
  22.3 0.2 fusion.35
  22.7 0.7 fusion.20
  23.4 0.9 fusion.19
  24.4 1.7 %collective-permute-start.2 = (bf16[6,144,256]{2,1,0:T(8,128)(2,1)S(1)}, bf16[6,144,256]{2,1,0:T(8,128)(2,1)S(1)}, u32[]{:S(2)}, u32[]{:S(2)}) collective-permute-start(bf16[6,144,256]{2,1,0:T(8,128)(2,1)S(1)} %pad_maximum_fusion.1), channel_id=1, source_target_pairs={{0,16},{16,0},{1,17},{17,1},{2,18},{18,2},{3,19},{19,3},{4,20},{20... | collective-permute-start | bytes 1327112 | tf_op jit(solution)/shard_map/ppermute | solution.py:36
  26.1 0.2 compare_convert_fusion
  26.3 0.8 stack.33.pairs_ref
  27.3 8.7 %collective-permute-done.2 = bf16[6,144,256]{2,1,0:T(8,128)(2,1)S(1)} collective-permute-done((bf16[6,144,256]{2,1,0:T(8,128)(2,1)S(1)}, bf16[6,144,256]{2,1,0:T(8,128)(2,1)S(1)}, u32[]{:S(2)}, u32[]{:S(2)}) %collective-permute-start.2) | collective-permute-done | bytes 442400 | tf_op jit(solution)/shard_map/ppermute | solution.py:36
  36.2 1.7 %collective-permute-start.3 = (bf16[12,144,256]{2,1,0:T(8,128)(2,1)S(1)}, bf16[12,144,256]{2,1,0:T(8,128)(2,1)}, u32[]{:S(2)}, u32[]{:S(2)}) collective-permute-start(bf16[12,144,256]{2,1,0:T(8,128)(2,1)S(1)} %pad_maximum_fusion.refs_0_.refs_1_), channel_id=1, source_target_pairs={{0,12},{4,0},{8,4},{12,8},{1,13},{5,1},{9,5},{13,9},{2,14},{6,2},{... | collective-permute-start | bytes 2654216 | tf_op jit(solution)/shard_map/ppermute | solution.py:36
  38.2 13.9 %near_pairs.1.refs_0_ = f32[6,4,512]{2,1,0:T(4,128)S(1)} custom-call(s32[131]{0:T(256)S(1)} %pad_add_fusion.1.plan_ref, s32[64,8,256]{2,1,0:T(8,128)S(1)} %stack.33.pairs_ref, bf16[12,144,256]{2,1,0:T(8,128)(2,1)S(1)} %pad_maximum_fusion.refs_0_.refs_1_, bf16[256,256]{1,0:T(8,128)(2,1)S(1)} %maximum_bitcast_fusion.refs_1_.refs_4_, ...), custom_call_target="tpu_custom_call" | custom-call | flops 3221225472 | bytes 786432 | tf_op jit(solution)/shard_map/near_pairs/pallas_call | solution.py:363
  52.2 4.1 %collective-permute-done.4.refs_3_ = bf16[12,144,256]{2,1,0:T(8,128)(2,1)S(1)} collective-permute-done((bf16[12,144,256]{2,1,0:T(8,128)(2,1)S(1)}, bf16[12,144,256]{2,1,0:T(8,128)(2,1)S(1)}, u32[]{:S(2)}, u32[]{:S(2)}) %collective-permute-start.4) | collective-permute-done | bytes 884768 | tf_op jit(solution)/shard_map/ppermute | solution.py:38
  56.3 0.9 collective-permute-done.3.refs_2_
  57.2 31.4 %far_pairs.1 = f32[18,4,512]{2,1,0:T(4,128)S(1)} custom-call(s32[131]{0:T(256)S(1)} %pad_add_fusion.1.plan_ref, s32[64,8,256]{2,1,0:T(8,128)S(1)} %stack.33.pairs_ref, f32[6,4,512]{2,1,0:T(4,128)S(1)} %near_pairs.1.refs_0_, bf16[12,144,256]{2,1,0:T(8,128)(2,1)S(1)} %pad_maximum_fusion.refs_0_.refs_1_, bf16[12,144,256]{2,1,0:T(8,128)(2,1)} %collective-permute-done.3.refs_2_, ...), custom_call_target="tpu_custom_call" | custom-call | flops 6442450944 | bytes 2359296 | tf_op jit(solution)/shard_map/far_pairs/pallas_call | solution.py:363
  88.7 0.5 collective-permute-start.5
  89.2 1.4 %collective-permute-done.6 = f32[2,3,4,512]{3,2,1,0:T(4,128)S(1)} collective-permute-done((f32[2,3,4,512]{3,2,1,0:T(4,128)S(1)}, f32[2,3,4,512]{3,2,1,0:T(4,128)S(1)}, u32[]{:S(2)}, u32[]{:S(2)}) %collective-permute-start.6) | collective-permute-done | bytes 49184 | tf_op jit(solution)/shard_map/ppermute | solution.py:45
  90.7 1.6 %collective-permute-done.5 = f32[2,3,4,512]{3,2,1,0:T(4,128)S(1)} collective-permute-done((f32[2,3,4,512]{3,2,1,0:T(4,128)S(1)}, f32[2,3,4,512]{3,2,1,0:T(4,128)S(1)}, u32[]{:S(2)}, u32[]{:S(2)}) %collective-permute-start.5) | collective-permute-done | bytes 49184 | tf_op jit(solution)/shard_map/ppermute | solution.py:43
  92.3 2.3 %collective-permute-start.7 = (f32[3,4,512]{2,1,0:T(4,128)S(1)}, f32[3,4,512]{2,1,0:T(4,128)S(1)}, u32[]{:S(2)}, u32[]{:S(2)}) collective-permute-start(f32[3,4,512]{2,1,0:T(4,128)S(1)} %slice_bitcast_fusion.2), channel_id=1, source_target_pairs={{0,16},{16,0},{1,17},{17,1},{2,18},{18,2},{3,19},{19,3},{4,20},{20... | collective-permute-start | bytes 73736 | tf_op jit(solution)/shard_map/ppermute | solution.py:43
  94.6 1.8 %collective-permute-done.7 = f32[3,4,512]{2,1,0:T(4,128)S(1)} collective-permute-done((f32[3,4,512]{2,1,0:T(4,128)S(1)}, f32[3,4,512]{2,1,0:T(4,128)S(1)}, u32[]{:S(2)}, u32[]{:S(2)}) %collective-permute-start.7) | collective-permute-done | bytes 24608 | tf_op jit(solution)/shard_map/ppermute | solution.py:43
  96.4 3.5 %collective-permute-start.8 = (f32[4,512]{1,0:T(4,128)S(1)}, f32[4,512]{1,0:T(4,128)S(1)}, u32[]{:S(2)}, u32[]{:S(2)}) collective-permute-start(f32[4,512]{1,0:T(4,128)S(1)} %get-tuple-element.57), channel_id=1, source_target_pairs={{0,1},{1,2},{2,3},{3,0},{4,5},{5,6},{6,7},{7,4},{8,9},{9,10},{10,1... | collective-permute-start | bytes 24584 | tf_op jit(solution)/shard_map/ppermute | solution.py:43
  99.9 5.8 %collective-permute-start.9 = (f32[4,512]{1,0:T(4,128)S(1)}, f32[4,512]{1,0:T(4,128)S(1)}, u32[]{:S(2)}, u32[]{:S(2)}) collective-permute-start(f32[4,512]{1,0:T(4,128)S(1)} %get-tuple-element.58), channel_id=1, source_target_pairs={{0,3},{1,0},{2,1},{3,2},{4,7},{5,4},{6,5},{7,6},{8,11},{9,8},{10,9... | collective-permute-start | bytes 24584 | tf_op jit(solution)/shard_map/ppermute | solution.py:45
  105.8 1.6 %collective-permute-done.8 = f32[4,512]{1,0:T(4,128)S(1)} collective-permute-done((f32[4,512]{1,0:T(4,128)S(1)}, f32[4,512]{1,0:T(4,128)S(1)}, u32[]{:S(2)}, u32[]{:S(2)}) %collective-permute-start.8) | collective-permute-done | bytes 8224 | tf_op jit(solution)/shard_map/ppermute | solution.py:43
  107.3 0.6 slice_bitcast_fusion.7
  107.9 0.6 broadcast_in_dim.37
  (62 shorter events, 1.9 us)
Async XLA Ops:
  0.6 1.8 %copy-start = (bf16[128]{0:T(256)(128)(2,1)S(1)}, bf16[128]{0:T(256)(128)(2,1)}, u32[]{:S(2)}) copy-start(bf16[128]{0:T(256)(128)(2,1)} %param.20) | copy-start | bytes 772
  1.3 1.1 %copy-start.2 = (bf16[1,1,1,512,128]{4,3,2,1,0:T(8,128)(2,1)S(1)}, bf16[1,1,1,512,128]{4,3,2,1,0:T(8,128)(2,1)}, u32[]{:S(2)}) copy-start(bf16[1,1,1,512,128]{4,3,2,1,0:T(8,128)(2,1)} %param.12) | copy-start | bytes 393220
  2.4 0.7 copy-start.9
  4.5 5.2 %copy-start.3 = (s32[1,1,1,128,128]{4,3,2,1,0:T(8,128)S(1)}, s32[1,1,1,128,128]{4,3,2,1,0:T(8,128)}, u32[]{:S(2)}) copy-start(s32[1,1,1,128,128]{4,3,2,1,0:T(8,128)} %param.17) | copy-start | bytes 196612
  4.5 5.9 %copy-start.5 = (s32[1,1,1,128,128]{4,3,2,1,0:T(8,128)S(1)}, s32[1,1,1,128,128]{4,3,2,1,0:T(8,128)}, u32[]{:S(2)}) copy-start(s32[1,1,1,128,128]{4,3,2,1,0:T(8,128)} %param.16) | copy-start | bytes 196612
  4.5 5.8 %copy-start.4 = (s32[1,1,1,128,128]{4,3,2,1,0:T(8,128)S(1)}, s32[1,1,1,128,128]{4,3,2,1,0:T(8,128)}, u32[]{:S(2)}) copy-start(s32[1,1,1,128,128]{4,3,2,1,0:T(8,128)} %param.15) | copy-start | bytes 196612
  4.5 13.1 %collective-permute-start.1 = (bf16[2,144,256]{2,1,0:T(8,128)(2,1)S(1)}, bf16[2,144,256]{2,1,0:T(8,128)(2,1)S(1)}, u32[]{:S(2)}, u32[]{:S(2)}) collective-permute-start(bf16[2,144,256]{2,1,0:T(8,128)(2,1)S(1)} %pad_maximum_fusion.2), channel_id=1, source_target_pairs={{0,1},{1,2},{2,3},{3,0},{4,5},{5,6},{6,7},{7,4},{8,9},{9,10},{10,1... | collective-permute-start | bytes 442376 | tf_op jit(solution)/shard_map/ppermute | solution.py:38
  7.6 10.1 %collective-permute-start = (bf16[2,144,256]{2,1,0:T(8,128)(2,1)S(1)}, bf16[2,144,256]{2,1,0:T(8,128)(2,1)S(1)}, u32[]{:S(2)}, u32[]{:S(2)}) collective-permute-start(bf16[2,144,256]{2,1,0:T(8,128)(2,1)S(1)} %pad_maximum_fusion.2), channel_id=1, source_target_pairs={{0,3},{1,0},{2,1},{3,2},{4,7},{5,4},{6,5},{7,6},{8,11},{9,8},{10,9... | collective-permute-start | bytes 442376 | tf_op jit(solution)/shard_map/ppermute | solution.py:36
  17.7 3.4 %copy-start.6 = (bf16[128,256]{1,0:T(8,128)(2,1)S(1)}, bf16[128,256]{1,0:T(8,128)(2,1)}, u32[]{:S(2)}) copy-start(bf16[128,256]{1,0:T(8,128)(2,1)} %param.18) | copy-start | bytes 196612
  17.7 3.5 %copy-start.7 = (bf16[128,256]{1,0:T(8,128)(2,1)S(1)}, bf16[128,256]{1,0:T(8,128)(2,1)}, u32[]{:S(2)}) copy-start(bf16[128,256]{1,0:T(8,128)(2,1)} %param.19) | copy-start | bytes 196612
  18.5 2.6 %copy-start.8 = (f32[8,256]{1,0:T(8,128)S(1)}, f32[8,256]{1,0:T(8,128)}, u32[]{:S(2)}) copy-start(f32[8,256]{1,0:T(8,128)} %param.21) | copy-start | bytes 24580
  21.1 0.9 copy-start.1
  24.4 11.7 %collective-permute-start.2 = (bf16[6,144,256]{2,1,0:T(8,128)(2,1)S(1)}, bf16[6,144,256]{2,1,0:T(8,128)(2,1)S(1)}, u32[]{:S(2)}, u32[]{:S(2)}) collective-permute-start(bf16[6,144,256]{2,1,0:T(8,128)(2,1)S(1)} %pad_maximum_fusion.1), channel_id=1, source_target_pairs={{0,16},{16,0},{1,17},{17,1},{2,18},{18,2},{3,19},{19,3},{4,20},{20... | collective-permute-start | bytes 1327112 | tf_op jit(solution)/shard_map/ppermute | solution.py:36
  36.2 1.9 %copy-start.10 = (f32[256]{0:T(256)S(1)}, f32[256]{0:T(256)}, u32[]{:S(2)}) copy-start(f32[256]{0:T(256)} %param.23) | copy-start | bytes 3076
  36.2 20.1 %collective-permute-start.4 = (bf16[12,144,256]{2,1,0:T(8,128)(2,1)S(1)}, bf16[12,144,256]{2,1,0:T(8,128)(2,1)S(1)}, u32[]{:S(2)}, u32[]{:S(2)}) collective-permute-start(bf16[12,144,256]{2,1,0:T(8,128)(2,1)S(1)} %pad_maximum_fusion.refs_0_.refs_1_), channel_id=1, source_target_pairs={{0,4},{4,8},{8,12},{12,0},{1,5},{5,9},{9,13},{13,1},{2,6},{6,10},{... | collective-permute-start | bytes 2654216 | tf_op jit(solution)/shard_map/ppermute | solution.py:38
  36.2 21.0 %collective-permute-start.3 = (bf16[12,144,256]{2,1,0:T(8,128)(2,1)S(1)}, bf16[12,144,256]{2,1,0:T(8,128)(2,1)}, u32[]{:S(2)}, u32[]{:S(2)}) collective-permute-start(bf16[12,144,256]{2,1,0:T(8,128)(2,1)S(1)} %pad_maximum_fusion.refs_0_.refs_1_), channel_id=1, source_target_pairs={{0,12},{4,0},{8,4},{12,8},{1,13},{5,1},{9,5},{13,9},{2,14},{6,2},{... | collective-permute-start | bytes 2654216 | tf_op jit(solution)/shard_map/ppermute | solution.py:36
  88.6 2.0 %collective-permute-start.6 = (f32[2,3,4,512]{3,2,1,0:T(4,128)S(1)}, f32[2,3,4,512]{3,2,1,0:T(4,128)S(1)}, u32[]{:S(2)}, u32[]{:S(2)}) collective-permute-start(f32[2,3,4,512]{3,2,1,0:T(4,128)S(1)} %bitcast.86), channel_id=1, source_target_pairs={{0,12},{4,0},{8,4},{12,8},{1,13},{5,1},{9,5},{13,9},{2,14},{6,2},{... | collective-permute-start | bytes 147464 | tf_op jit(solution)/shard_map/ppermute | solution.py:45
  88.7 3.6 %collective-permute-start.5 = (f32[2,3,4,512]{3,2,1,0:T(4,128)S(1)}, f32[2,3,4,512]{3,2,1,0:T(4,128)S(1)}, u32[]{:S(2)}, u32[]{:S(2)}) collective-permute-start(f32[2,3,4,512]{3,2,1,0:T(4,128)S(1)} %bitcast.85), channel_id=1, source_target_pairs={{0,4},{4,8},{8,12},{12,0},{1,5},{5,9},{9,13},{13,1},{2,6},{6,10},{... | collective-permute-start | bytes 147464 | tf_op jit(solution)/shard_map/ppermute | solution.py:43
  92.3 4.1 %collective-permute-start.7 = (f32[3,4,512]{2,1,0:T(4,128)S(1)}, f32[3,4,512]{2,1,0:T(4,128)S(1)}, u32[]{:S(2)}, u32[]{:S(2)}) collective-permute-start(f32[3,4,512]{2,1,0:T(4,128)S(1)} %slice_bitcast_fusion.2), channel_id=1, source_target_pairs={{0,16},{16,0},{1,17},{17,1},{2,18},{18,2},{3,19},{19,3},{4,20},{20... | collective-permute-start | bytes 73736 | tf_op jit(solution)/shard_map/ppermute | solution.py:43
  96.4 10.9 %collective-permute-start.8 = (f32[4,512]{1,0:T(4,128)S(1)}, f32[4,512]{1,0:T(4,128)S(1)}, u32[]{:S(2)}, u32[]{:S(2)}) collective-permute-start(f32[4,512]{1,0:T(4,128)S(1)} %get-tuple-element.57), channel_id=1, source_target_pairs={{0,1},{1,2},{2,3},{3,0},{4,5},{5,6},{6,7},{7,4},{8,9},{9,10},{10,1... | collective-permute-start | bytes 24584 | tf_op jit(solution)/shard_map/ppermute | solution.py:43
  99.9 7.4 %collective-permute-start.9 = (f32[4,512]{1,0:T(4,128)S(1)}, f32[4,512]{1,0:T(4,128)S(1)}, u32[]{:S(2)}, u32[]{:S(2)}) collective-permute-start(f32[4,512]{1,0:T(4,128)S(1)} %get-tuple-element.58), channel_id=1, source_target_pairs={{0,3},{1,0},{2,1},{3,2},{4,7},{5,4},{6,5},{7,6},{8,11},{9,8},{10,9... | collective-permute-start | bytes 24584 | tf_op jit(solution)/shard_map/ppermute | solution.py:45

commit v5 on v4

--- a/solution.py
+++ b/solution.py
@@ -81,8 +81,6 @@
         other_ref,
         sum_i_ref,
         sum_j_ref,
-        pick_i_ref,
-        pick_j_ref,
         terms_ref,
         copied,
     ) = refs[1:] if stage else refs
@@ -129,21 +127,52 @@
     def spill(terms, picked):
         return lax.dot_general(terms, picked, across, preferred_element_type=jnp.float32)
 
+    last_window = image_ref.shape[0] - 4
+
+    def near_entries(part, turn):
+        second = pairs_ref[part][1:2]
+        start = plan_ref[2 * part + 3] + 4 * turn
+        base = jnp.minimum(start, last_window)
+        inside = (second >= start * width) & (second < (start + 4) * width)
+        return base, jnp.where(inside, second - base * width, -1)
+
+    def select(base, groups, entries):
+        low = jnp.where(entries < 0, -1, entries & (2 * width - 1))
+        picked = pick(2 * width, low)
+        total = None
+        for group in range(groups):
+            table = jnp.concatenate(
+                [image_ref[base + 2 * group], image_ref[base + 2 * group + 1]], axis=1
+            )
+            found = lower(table, picked)
+            total = found if total is None else jnp.where(
+                entries >= 2 * width * group, found, total
+            )
+        return total
+
+    def spread_terms(terms, groups, entries):
+        low = jnp.where(entries < 0, -1, entries & (width - 1))
+        rows = jnp.concatenate(
+            [
+                jnp.where(
+                    (entries >= width * group) & (entries < width * (group + 1)), terms, 0.0
+                )
+                for group in range(groups)
+            ],
+            axis=0,
+        ).astype(jnp.bfloat16)
+        return spill(rows, pick(width, low))
+
+    def add_other(lane, part, turn):
+        base, entries = near_entries(part, turn)
+        moved = spread_terms(terms_ref[lane, 8:16, :], 4, entries)
+        for group in range(4):
+            sum_j_ref[base + group] += moved[8 * group : 8 * group + 8]
+
     def begin_part(part, lane):
-        listed = pairs_ref[part]
-        least = plan_ref[2 * part + 3]
-        after = jnp.minimum(least + 1, image_ref.shape[0] - 1)
-        pick_i = pick(atoms, listed[0:1])
-        pick_j = pick(2 * width, listed[1:2] - least * width)
-        own = lower(image_ref[0], pick_i[:width])
-        for cut in range(1, cuts):
-            own += lower(image_ref[cut], pick_i[cut * width : (cut + 1) * width])
-        other = lower(image_ref[least], pick_j[:width])
-        other += lower(image_ref[after], pick_j[width:])
-        own_ref[lane] = own
-        other_ref[lane] = other
-        pick_i_ref[lane] = pick_i
-        pick_j_ref[lane] = pick_j
+        own_ref[lane] = select(0, cuts // 2, pairs_ref[part][0:1])
+        base, entries = near_entries(part, 0)
+        other_ref[lane] = select(base, 2, entries)
 
     def whole(ref, lane):
         parts = ref[lane, feat:, :]
@@ -206,11 +235,11 @@
         push = slope * sep
         shared = weight * coulomb * potential
         last = lax.broadcasted_iota(jnp.int32, push.shape, 0) == 3
-        terms = jnp.concatenate(
-            [jnp.where(last, shared * at_j, push), jnp.where(last, shared * at_i, -push)], axis=0
-        )
-        terms_high = terms.astype(jnp.bfloat16).astype(jnp.float32)
-        return jnp.concatenate([terms_high, terms - terms_high], axis=0).astype(jnp.bfloat16)
+        for_i = jnp.where(last, shared * at_j, push)
+        for_j = jnp.where(last, shared * at_i, -push)
+        high_i = for_i.astype(jnp.bfloat16).astype(jnp.float32)
+        high_j = for_j.astype(jnp.bfloat16).astype(jnp.float32)
+        return jnp.concatenate([high_i, for_i - high_i, high_j, for_j - high_j], axis=0)
 
     def step(block, carry):
         parts = [block * subs + lane for lane in range(subs)]
@@ -218,12 +247,12 @@
             begin_part(part, lane)
 
         for lane, part in enumerate(parts):
-            def gather(window, carry, lane=lane, part=part):
-                entries = pairs_ref[part][1:2] - window * width
-                other_ref[lane] += lower(image_ref[window], pick(width, entries))
+            def gather(turn, carry, lane=lane, part=part):
+                base, entries = near_entries(part, turn)
+                other_ref[lane] += select(base, 2, entries)
                 return carry
 
-            lax.fori_loop(plan_ref[2 * part + 3] + 2, plan_ref[2 * part + 4] + 1, gather, 0)
+            lax.fori_loop(1, plan_ref[2 * part + 4], gather, 0)
 
         shapes = [geometry(part, lane) for lane, part in enumerate(parts)]
         ones = [first_layer(shape[-1]) for shape in shapes]
@@ -238,20 +267,15 @@
             back_basis = from_grad[:basis_count] + from_grad[basis_count:]
             terms_ref[lane] = pair_terms(part, lane, shapes[lane], back_basis, backs[lane][1])
         for lane, part in enumerate(parts):
-            least = plan_ref[2 * part + 3]
-            after = jnp.minimum(least + 1, image_ref.shape[0] - 1)
-            terms = terms_ref[lane]
-            sum_i_ref[...] += spill(terms, pick_i_ref[lane])
-            sum_j_ref[least] += spill(terms, pick_j_ref[lane, :width])
-            sum_j_ref[after] += spill(terms, pick_j_ref[lane, width:])
+            sum_i_ref[...] += spread_terms(terms_ref[lane, 0:8, :], cuts, pairs_ref[part][0:1])
+            add_other(lane, part, 0)
 
         for lane, part in enumerate(parts):
-            def scatter(window, carry, lane=lane, part=part):
-                entries = pairs_ref[part][1:2] - window * width
-                sum_j_ref[window] += spill(terms_ref[lane], pick(width, entries))
+            def scatter(turn, carry, lane=lane, part=part):
+                add_other(lane, part, turn)
                 return carry
 
-            lax.fori_loop(plan_ref[2 * part + 3] + 2, plan_ref[2 * part + 4] + 1, scatter, 0)
+            lax.fori_loop(1, plan_ref[2 * part + 4], scatter, 0)
         return carry
 
     lax.fori_loop(plan_ref[stage], plan_ref[stage + 1], step, 0)
@@ -259,11 +283,13 @@
     def finish(index, carry):
         for cut in range(cuts):
             total = sum_j_ref[index * cuts + cut]
-            out_ref[index, :, cut * width : (cut + 1) * width] = total[4:8] + total[12:16]
+            out_ref[index, :, cut * width : (cut + 1) * width] = total[0:4] + total[4:8]
         return carry
 
     lax.fori_loop(0, out_ref.shape[0], finish, 0)
-    out_ref[0] += sum_i_ref[0:4, :] + sum_i_ref[8:12, :]
+    for cut in range(cuts):
+        total = sum_i_ref[8 * cut : 8 * cut + 8]
+        out_ref[0, :, cut * width : (cut + 1) * width] += total[0:4] + total[4:8]
     if stage:
         out_ref[: before_ref.shape[0]] += before_ref[...]
 
@@ -296,7 +322,7 @@
         + [jnp.zeros((part_rows - 12, atoms), jnp.float32)],
         axis=0,
     ).astype(jnp.bfloat16)
-    width = 256 if atoms % 256 == 0 else 128
+    width = 128
     own = jnp.concatenate([own_feat.T, own], axis=0)
     own = jnp.stack(jnp.split(own, atoms // width, axis=1))
     column = jnp.concatenate(widen(own, "gz"))
@@ -336,11 +362,17 @@
     ]
     listed = jnp.stack(rows, axis=1)
     window = jnp.minimum(second // width, bricks * atoms // width - 1)
+    near = spans[0] * spans[2]
+    in_near = (second < near * atoms).astype(jnp.int32)
     live = (valid + subs * lanes - 1) // (subs * lanes)
-    near = spans[0] * spans[2]
-    first_part = jnp.sum((second < near * atoms).astype(jnp.int32)) // (subs * lanes)
+    first_part = jnp.sum(in_near) // (subs * lanes)
+    near_part = (jnp.arange(blocks) // subs) < first_part
+    least = jnp.minimum(
+        window[:, 0], jnp.where(near_part, near, bricks) * atoms // width - 4
+    )
+    turns = (jnp.max(window, axis=1) - least) // 4 + 1
     plan = jnp.concatenate(
-        [jnp.stack([jnp.zeros_like(live), first_part, live]), jnp.stack([window[:, 0], jnp.max(window, axis=1)], axis=1).reshape(-1)]
+        [jnp.stack([jnp.zeros_like(live), first_part, live]), jnp.stack([least, turns], axis=1).reshape(-1)]
     ).astype(jnp.int32)
 
     radial_high = rounded(w_radial)
@@ -372,11 +404,9 @@
                 pltpu.VMEM((windows, feat + part_rows, width), jnp.bfloat16),
                 pltpu.VMEM((subs, feat + part_rows, lanes), jnp.float32),
                 pltpu.VMEM((subs, feat + part_rows, lanes), jnp.float32),
-                pltpu.VMEM((16, atoms), jnp.float32),
-                pltpu.VMEM((windows, 16, width), jnp.float32),
-                pltpu.VMEM((subs, atoms, lanes), jnp.bfloat16),
-                pltpu.VMEM((subs, 2 * width, lanes), jnp.bfloat16),
-                pltpu.VMEM((subs, 16, lanes), jnp.bfloat16),
+                pltpu.VMEM((8 * atoms // width, width), jnp.float32),
+                pltpu.VMEM((windows, 8, width), jnp.float32),
+                pltpu.VMEM((subs, 16, lanes), jnp.float32),
                 pltpu.SemaphoreType.DMA((len(images),)),
             ],
             compiler_params=pltpu.CompilerParams(vmem_limit_bytes=48 * 1024 * 1024),

time: 109 us -> 107 us (0.982)
  Pallas kernels: 45.3 us -> 26.3 us
  starting transfers between devices: 20.8 us -> 29.5 us
  waiting for transfers between devices: 20.2 us -> 28.6 us
    pallas_call x2, Pallas kernels: 45.3 us -> 26.3 us  [run(): pl.pallas_call(functools.partial(pair_kernel, stage), out_shape=jax.Shape...]
    ppermute x2, starting transfers between devices: 5.88 us -> 20.7 us  [fold(): total = total + lax.ppermute(blocks[2], axis, ring(axis, -1))]
    ppermute x3, starting transfers between devices: 6.29 us -> 0.13 us  [fold(): total = blocks[0] + lax.ppermute(blocks[1], axis, ring(axis, 1))]
    ppermute x2, waiting for transfers between devices: 4.12 us -> 9.97 us  [widen(): parts.append(lax.ppermute(block, axis, ring(axis, 1)))]
    ppermute x3, waiting for transfers between devices: 4.99 us -> 7.2 us  [fold(): total = blocks[0] + lax.ppermute(blocks[1], axis, ring(axis, 1))]
    unnamed x24 -> x29, local copies, waits for them, and re-layouts: 2.33 us -> 3.23 us
  transfers between devices with their start and end apart: 10 -> 10, of which waited for: 7 -> 7; matrix products, arithmetic and copies ran while one was open for 8% -> 8% of each run, Pallas kernels for 13% -> 8%
where the time goes in v5:
time: 107 us
  starting transfers between devices  29.5 us (28%)
  waiting for transfers between devices  28.6 us (27%)
  Pallas kernels  26.3 us (25%)
  other arithmetic  10.9 us (10%)
  local copies, waits for them, and re-layouts  6.4 us (6%)
  between operations  5.63 us (5%)
    pallas_call x2, Pallas kernels, run(): pl.pallas_call(functools.partial(pair_kernel, stage), out_shape=jax.Shape...  26.3 us
    ppermute x2, starting transfers between devices, fold(): total = total + lax.ppermute(blocks[2], axis, ring(axis, -1))  20.7 us
    ppermute x2, waiting for transfers between devices, widen(): parts.append(lax.ppermute(block, axis, ring(axis, 1)))  9.97 us
    ppermute x3, waiting for transfers between devices, widen(): parts = [block, lax.ppermute(block, axis, ring(axis, -1))]  9.65 us
    ppermute x3, waiting for transfers between devices, fold(): total = blocks[0] + lax.ppermute(blocks[1], axis, ring(axis, 1))  7.2 us
    sort x1, other arithmetic, local(): key = lax.sort(key, is_stable=False)  6.28 us
    ppermute x3, starting transfers between devices, widen(): parts = [block, lax.ppermute(block, axis, ring(axis, -1))]  5.54 us
    unnamed x29, local copies, waits for them, and re-layouts  3.23 us
  transfers between devices with their start and end apart: 10, of which 7 were waited for; matrix products, arithmetic and copies ran while one was open for 8% of the time, Pallas kernels for 8%

profile of v5, /device:TPU:0, one launch (start us, length us, event | category | flops | bytes accessed | tf_op | source)
XLA Modules:
  0.0 107.5 jit_solution(10543857769455798116)
XLA Ops:
  1.3 1.1 copy.48
  2.6 0.5 copy-done.9
  3.1 0.6 select_reduce_fusion
  4.5 3.1 %collective-permute-start.1 = (bf16[4,144,128]{2,1,0:T(8,128)(2,1)S(1)}, bf16[4,144,128]{2,1,0:T(8,128)(2,1)S(1)}, u32[]{:S(2)}, u32[]{:S(2)}) collective-permute-start(bf16[4,144,128]{2,1,0:T(8,128)(2,1)S(1)} %pad_maximum_fusion.1), channel_id=1, source_target_pairs={{0,1},{1,2},{2,3},{3,0},{4,5},{5,6},{6,7},{7,4},{8,9},{9,10},{10,1... | collective-permute-start | bytes 442376 | tf_op jit(solution)/shard_map/ppermute | solution.py:38
  7.6 2.1 %collective-permute-start = (bf16[4,144,128]{2,1,0:T(8,128)(2,1)S(1)}, bf16[4,144,128]{2,1,0:T(8,128)(2,1)S(1)}, u32[]{:S(2)}, u32[]{:S(2)}) collective-permute-start(bf16[4,144,128]{2,1,0:T(8,128)(2,1)S(1)} %pad_maximum_fusion.1), channel_id=1, source_target_pairs={{0,3},{1,0},{2,1},{3,2},{4,7},{5,4},{6,5},{7,6},{8,11},{9,8},{10,9... | collective-permute-start | bytes 442376 | tf_op jit(solution)/shard_map/ppermute | solution.py:36
  9.7 0.6 convert_reduce_fusion
  10.4 0.8 copy-done.4
  11.2 0.3 fusion.10
  12.2 6.3 %sort.7 = s32[16384]{0:T(1024)S(1)} sort(s32[16384]{0:T(1024)S(1)} %fusion.10), dimensions={0}, to_apply=%region_1.2 | sort | flops 229376 | bytes 131072 | tf_op jit(solution)/shard_map/sort | solution.py:340
  18.6 0.7 convert_reduce_fusion.1
  22.2 0.6 copy-done.1
  23.2 0.2 fusion.48
  23.5 0.1 reshape.364
  23.7 0.7 fusion.20
  24.4 0.9 fusion.19
  25.3 1.7 %collective-permute-start.2 = (bf16[12,144,128]{2,1,0:T(8,128)(2,1)S(1)}, bf16[12,144,128]{2,1,0:T(8,128)(2,1)S(1)}, u32[]{:S(2)}, u32[]{:S(2)}) collective-permute-start(bf16[12,144,128]{2,1,0:T(8,128)(2,1)S(1)} %constant_dynamic-update-slice_fusion), channel_id=1, source_target_pairs={{0,16},{16,0},{1,17},{17,1},{2,18},{18,2},{3,19},{19,3},{4,20},{20... | collective-permute-start | bytes 1327112 | tf_op jit(solution)/shard_map/ppermute | solution.py:36
  27.0 0.2 compare_convert_fusion
  27.3 0.8 stack.40.pairs_ref
  28.3 8.7 %collective-permute-done.2 = bf16[12,144,128]{2,1,0:T(8,128)(2,1)S(1)} collective-permute-done((bf16[12,144,128]{2,1,0:T(8,128)(2,1)S(1)}, bf16[12,144,128]{2,1,0:T(8,128)(2,1)S(1)}, u32[]{:S(2)}, u32[]{:S(2)}) %collective-permute-start.2) | collective-permute-done | bytes 442400 | tf_op jit(solution)/shard_map/ppermute | solution.py:36
  37.2 1.7 %collective-permute-start.3 = (bf16[24,144,128]{2,1,0:T(8,128)(2,1)S(1)}, bf16[24,144,128]{2,1,0:T(8,128)(2,1)}, u32[]{:S(2)}, u32[]{:S(2)}) collective-permute-start(bf16[24,144,128]{2,1,0:T(8,128)(2,1)S(1)} %pad_maximum_fusion.refs_0_.refs_1_), channel_id=1, source_target_pairs={{0,12},{4,0},{8,4},{12,8},{1,13},{5,1},{9,5},{13,9},{2,14},{6,2},{... | collective-permute-start | bytes 2654216 | tf_op jit(solution)/shard_map/ppermute | solution.py:36
  39.2 8.1 %near_pairs.1.refs_0_ = f32[6,4,512]{2,1,0:T(4,128)S(1)} custom-call(s32[131]{0:T(256)S(1)} %pad_add_fusion.1.plan_ref, s32[64,8,256]{2,1,0:T(8,128)S(1)} %stack.40.pairs_ref, bf16[24,144,128]{2,1,0:T(8,128)(2,1)S(1)} %pad_maximum_fusion.refs_0_.refs_1_, bf16[256,256]{1,0:T(8,128)(2,1)S(1)} %maximum_bitcast_fusion.refs_1_.refs_4_, ...), custom_call_target="tpu_custom_call" | custom-call | flops 2684354560 | bytes 786432 | tf_op jit(solution)/shard_map/near_pairs/pallas_call | solution.py:395
  47.3 10.0 %collective-permute-done.4.refs_3_ = bf16[24,144,128]{2,1,0:T(8,128)(2,1)S(1)} collective-permute-done((bf16[24,144,128]{2,1,0:T(8,128)(2,1)S(1)}, bf16[24,144,128]{2,1,0:T(8,128)(2,1)S(1)}, u32[]{:S(2)}, u32[]{:S(2)}) %collective-permute-start.4) | collective-permute-done | bytes 884768 | tf_op jit(solution)/shard_map/ppermute | solution.py:38
  57.2 0.9 collective-permute-done.3.refs_2_
  58.2 18.2 %far_pairs.1 = f32[18,4,512]{2,1,0:T(4,128)S(1)} custom-call(s32[131]{0:T(256)S(1)} %pad_add_fusion.1.plan_ref, s32[64,8,256]{2,1,0:T(8,128)S(1)} %stack.40.pairs_ref, f32[6,4,512]{2,1,0:T(4,128)S(1)} %near_pairs.1.refs_0_, bf16[24,144,128]{2,1,0:T(8,128)(2,1)S(1)} %pad_maximum_fusion.refs_0_.refs_1_, bf16[24,144,128]{2,1,0:T(8,128)(2,1)} %collective-permute-done.3.refs_2_, ...), custom_call_target="tpu_custom_call" | custom-call | flops 5368709120 | bytes 2359296 | tf_op jit(solution)/shard_map/far_pairs/pallas_call | solution.py:395
  76.4 16.9 %collective-permute-start.6 = (f32[2,3,4,512]{3,2,1,0:T(4,128)S(1)}, f32[2,3,4,512]{3,2,1,0:T(4,128)S(1)}, u32[]{:S(2)}, u32[]{:S(2)}) collective-permute-start(f32[2,3,4,512]{3,2,1,0:T(4,128)S(1)} %bitcast.98), channel_id=1, source_target_pairs={{0,12},{4,0},{8,4},{12,8},{1,13},{5,1},{9,5},{13,9},{2,14},{6,2},{... | collective-permute-start | bytes 147464 | tf_op jit(solution)/shard_map/ppermute | solution.py:45
  93.3 1.7 %collective-permute-done.6 = f32[2,3,4,512]{3,2,1,0:T(4,128)S(1)} collective-permute-done((f32[2,3,4,512]{3,2,1,0:T(4,128)S(1)}, f32[2,3,4,512]{3,2,1,0:T(4,128)S(1)}, u32[]{:S(2)}, u32[]{:S(2)}) %collective-permute-start.6) | collective-permute-done | bytes 49184 | tf_op jit(solution)/shard_map/ppermute | solution.py:45
  95.1 1.8 %collective-permute-done.5 = f32[2,3,4,512]{3,2,1,0:T(4,128)S(1)} collective-permute-done((f32[2,3,4,512]{3,2,1,0:T(4,128)S(1)}, f32[2,3,4,512]{3,2,1,0:T(4,128)S(1)}, u32[]{:S(2)}, u32[]{:S(2)}) %collective-permute-start.5) | collective-permute-done | bytes 49184 | tf_op jit(solution)/shard_map/ppermute | solution.py:43
  96.9 3.8 %collective-permute-done.7 = f32[3,4,512]{2,1,0:T(4,128)S(1)} collective-permute-done((f32[3,4,512]{2,1,0:T(4,128)S(1)}, f32[3,4,512]{2,1,0:T(4,128)S(1)}, u32[]{:S(2)}, u32[]{:S(2)}) %collective-permute-start.7) | collective-permute-done | bytes 24608 | tf_op jit(solution)/shard_map/ppermute | solution.py:43
  100.8 3.8 %collective-permute-start.9 = (f32[4,512]{1,0:T(4,128)S(1)}, f32[4,512]{1,0:T(4,128)S(1)}, u32[]{:S(2)}, u32[]{:S(2)}) collective-permute-start(f32[4,512]{1,0:T(4,128)S(1)} %get-tuple-element.62), channel_id=1, source_target_pairs={{0,3},{1,0},{2,1},{3,2},{4,7},{5,4},{6,5},{7,6},{8,11},{9,8},{10,9... | collective-permute-start | bytes 24584 | tf_op jit(solution)/shard_map/ppermute | solution.py:45
  104.7 1.6 %collective-permute-done.8 = f32[4,512]{1,0:T(4,128)S(1)} collective-permute-done((f32[4,512]{1,0:T(4,128)S(1)}, f32[4,512]{1,0:T(4,128)S(1)}, u32[]{:S(2)}, u32[]{:S(2)}) %collective-permute-start.8) | collective-permute-done | bytes 8224 | tf_op jit(solution)/shard_map/ppermute | solution.py:43
  106.3 0.6 slice_bitcast_fusion.9
  106.9 0.6 broadcast_in_dim.47
  (67 shorter events, 2.0 us)
Async XLA Ops:
  0.6 1.8 %copy-start = (bf16[128]{0:T(256)(128)(2,1)S(1)}, bf16[128]{0:T(256)(128)(2,1)}, u32[]{:S(2)}) copy-start(bf16[128]{0:T(256)(128)(2,1)} %param.20) | copy-start | bytes 772
  1.3 1.1 %copy-start.2 = (bf16[1,1,1,512,128]{4,3,2,1,0:T(8,128)(2,1)S(1)}, bf16[1,1,1,512,128]{4,3,2,1,0:T(8,128)(2,1)}, u32[]{:S(2)}) copy-start(bf16[1,1,1,512,128]{4,3,2,1,0:T(8,128)(2,1)} %param.12) | copy-start | bytes 393220
  2.4 0.7 copy-start.9
  4.5 5.2 %copy-start.3 = (s32[1,1,1,128,128]{4,3,2,1,0:T(8,128)S(1)}, s32[1,1,1,128,128]{4,3,2,1,0:T(8,128)}, u32[]{:S(2)}) copy-start(s32[1,1,1,128,128]{4,3,2,1,0:T(8,128)} %param.17) | copy-start | bytes 196612
  4.5 14.0 %collective-permute-start.1 = (bf16[4,144,128]{2,1,0:T(8,128)(2,1)S(1)}, bf16[4,144,128]{2,1,0:T(8,128)(2,1)S(1)}, u32[]{:S(2)}, u32[]{:S(2)}) collective-permute-start(bf16[4,144,128]{2,1,0:T(8,128)(2,1)S(1)} %pad_maximum_fusion.1), channel_id=1, source_target_pairs={{0,1},{1,2},{2,3},{3,0},{4,5},{5,6},{6,7},{7,4},{8,9},{9,10},{10,1... | collective-permute-start | bytes 442376 | tf_op jit(solution)/shard_map/ppermute | solution.py:38
  7.6 10.9 %collective-permute-start = (bf16[4,144,128]{2,1,0:T(8,128)(2,1)S(1)}, bf16[4,144,128]{2,1,0:T(8,128)(2,1)S(1)}, u32[]{:S(2)}, u32[]{:S(2)}) collective-permute-start(bf16[4,144,128]{2,1,0:T(8,128)(2,1)S(1)} %pad_maximum_fusion.1), channel_id=1, source_target_pairs={{0,3},{1,0},{2,1},{3,2},{4,7},{5,4},{6,5},{7,6},{8,11},{9,8},{10,9... | collective-permute-start | bytes 442376 | tf_op jit(solution)/shard_map/ppermute | solution.py:36
  10.4 0.8 copy-start.4
  10.4 0.9 copy-start.5
  18.6 3.4 %copy-start.6 = (bf16[128,256]{1,0:T(8,128)(2,1)S(1)}, bf16[128,256]{1,0:T(8,128)(2,1)}, u32[]{:S(2)}) copy-start(bf16[128,256]{1,0:T(8,128)(2,1)} %param.18) | copy-start | bytes 196612
  18.6 3.5 %copy-start.7 = (bf16[128,256]{1,0:T(8,128)(2,1)S(1)}, bf16[128,256]{1,0:T(8,128)(2,1)}, u32[]{:S(2)}) copy-start(bf16[128,256]{1,0:T(8,128)(2,1)} %param.19) | copy-start | bytes 196612
  19.3 2.6 %copy-start.8 = (f32[8,256]{1,0:T(8,128)S(1)}, f32[8,256]{1,0:T(8,128)}, u32[]{:S(2)}) copy-start(f32[8,256]{1,0:T(8,128)} %param.21) | copy-start | bytes 24580
  22.0 0.9 copy-start.1
  25.3 11.7 %collective-permute-start.2 = (bf16[12,144,128]{2,1,0:T(8,128)(2,1)S(1)}, bf16[12,144,128]{2,1,0:T(8,128)(2,1)S(1)}, u32[]{:S(2)}, u32[]{:S(2)}) collective-permute-start(bf16[12,144,128]{2,1,0:T(8,128)(2,1)S(1)} %constant_dynamic-update-slice_fusion), channel_id=1, source_target_pairs={{0,16},{16,0},{1,17},{17,1},{2,18},{18,2},{3,19},{19,3},{4,20},{20... | collective-permute-start | bytes 1327112 | tf_op jit(solution)/shard_map/ppermute | solution.py:36
  37.1 1.9 %copy-start.10 = (f32[256]{0:T(256)S(1)}, f32[256]{0:T(256)}, u32[]{:S(2)}) copy-start(f32[256]{0:T(256)} %param.23) | copy-start | bytes 3076
  37.1 20.1 %collective-permute-start.4 = (bf16[24,144,128]{2,1,0:T(8,128)(2,1)S(1)}, bf16[24,144,128]{2,1,0:T(8,128)(2,1)S(1)}, u32[]{:S(2)}, u32[]{:S(2)}) collective-permute-start(bf16[24,144,128]{2,1,0:T(8,128)(2,1)S(1)} %pad_maximum_fusion.refs_0_.refs_1_), channel_id=1, source_target_pairs={{0,4},{4,8},{8,12},{12,0},{1,5},{5,9},{9,13},{13,1},{2,6},{6,10},{... | collective-permute-start | bytes 2654216 | tf_op jit(solution)/shard_map/ppermute | solution.py:38
  37.2 21.0 %collective-permute-start.3 = (bf16[24,144,128]{2,1,0:T(8,128)(2,1)S(1)}, bf16[24,144,128]{2,1,0:T(8,128)(2,1)}, u32[]{:S(2)}, u32[]{:S(2)}) collective-permute-start(bf16[24,144,128]{2,1,0:T(8,128)(2,1)S(1)} %pad_maximum_fusion.refs_0_.refs_1_), channel_id=1, source_target_pairs={{0,12},{4,0},{8,4},{12,8},{1,13},{5,1},{9,5},{13,9},{2,14},{6,2},{... | collective-permute-start | bytes 2654216 | tf_op jit(solution)/shard_map/ppermute | solution.py:36
  76.4 18.7 %collective-permute-start.6 = (f32[2,3,4,512]{3,2,1,0:T(4,128)S(1)}, f32[2,3,4,512]{3,2,1,0:T(4,128)S(1)}, u32[]{:S(2)}, u32[]{:S(2)}) collective-permute-start(f32[2,3,4,512]{3,2,1,0:T(4,128)S(1)} %bitcast.98), channel_id=1, source_target_pairs={{0,12},{4,0},{8,4},{12,8},{1,13},{5,1},{9,5},{13,9},{2,14},{6,2},{... | collective-permute-start | bytes 147464 | tf_op jit(solution)/shard_map/ppermute | solution.py:45
  93.3 3.5 %collective-permute-start.5 = (f32[2,3,4,512]{3,2,1,0:T(4,128)S(1)}, f32[2,3,4,512]{3,2,1,0:T(4,128)S(1)}, u32[]{:S(2)}, u32[]{:S(2)}) collective-permute-start(f32[2,3,4,512]{3,2,1,0:T(4,128)S(1)} %bitcast.97), channel_id=1, source_target_pairs={{0,4},{4,8},{8,12},{12,0},{1,5},{5,9},{9,13},{13,1},{2,6},{6,10},{... | collective-permute-start | bytes 147464 | tf_op jit(solution)/shard_map/ppermute | solution.py:43
  96.9 3.9 %collective-permute-start.7 = (f32[3,4,512]{2,1,0:T(4,128)S(1)}, f32[3,4,512]{2,1,0:T(4,128)S(1)}, u32[]{:S(2)}, u32[]{:S(2)}) collective-permute-start(f32[3,4,512]{2,1,0:T(4,128)S(1)} %slice_bitcast_fusion.4), channel_id=1, source_target_pairs={{0,16},{16,0},{1,17},{17,1},{2,18},{18,2},{3,19},{19,3},{4,20},{20... | collective-permute-start | bytes 73736 | tf_op jit(solution)/shard_map/ppermute | solution.py:43
  100.8 5.5 %collective-permute-start.8 = (f32[4,512]{1,0:T(4,128)S(1)}, f32[4,512]{1,0:T(4,128)S(1)}, u32[]{:S(2)}, u32[]{:S(2)}) collective-permute-start(f32[4,512]{1,0:T(4,128)S(1)} %get-tuple-element.61), channel_id=1, source_target_pairs={{0,1},{1,2},{2,3},{3,0},{4,5},{5,6},{6,7},{7,4},{8,9},{9,10},{10,1... | collective-permute-start | bytes 24584 | tf_op jit(solution)/shard_map/ppermute | solution.py:43
  100.8 5.4 %collective-permute-start.9 = (f32[4,512]{1,0:T(4,128)S(1)}, f32[4,512]{1,0:T(4,128)S(1)}, u32[]{:S(2)}, u32[]{:S(2)}) collective-permute-start(f32[4,512]{1,0:T(4,128)S(1)} %get-tuple-element.62), channel_id=1, source_target_pairs={{0,3},{1,0},{2,1},{3,2},{4,7},{5,4},{6,5},{7,6},{8,11},{9,8},{10,9... | collective-permute-start | bytes 24584 | tf_op jit(solution)/shard_map/ppermute | solution.py:45

commit v6 on v5

--- a/solution.py
+++ b/solution.py
@@ -12,7 +12,7 @@
 coulomb = 0.2
 root_pi = 1.7724538509055159
 part_rows = 16
-subs = 2
+subs = 4
 erfc_terms = (
     0.17087277,
     -0.82215223,
@@ -199,17 +199,18 @@
         return (at_i, at_j, sep), dist_sq, distance, offset, basis, pre_one
 
     def first_layer(pre_one):
-        gate = 0.5 * jnp.tanh(0.5 * pre_one) + 0.5
-        act = pre_one * gate
-        return act.astype(jnp.bfloat16), gate + act * (1.0 - gate)
+        wave = jnp.tanh(pre_one)
+        rise = 1.0 + wave
+        act = pre_one * rise
+        return act.astype(jnp.bfloat16), rise + act * (1.0 - wave)
 
     def second_layer(pre_two, dist_sq):
-        gate = 0.5 * jnp.tanh(0.5 * pre_two) + 0.5
-        scaled = energy_ref[...] * gate
+        wave = jnp.tanh(pre_two)
+        scaled = energy_ref[...] * (1.0 + wave)
         scaled_act = pre_two * scaled
         readout = jnp.sum(scaled_act, axis=0, keepdims=True)
         envelope = jnp.exp(-0.5 * dist_sq)
-        back = (envelope * (scaled + scaled_act * (1.0 - gate))).astype(jnp.bfloat16)
+        back = (envelope * (scaled + scaled_act * (1.0 - wave))).astype(jnp.bfloat16)
         return back, readout * envelope
 
     def pair_terms(part, lane, shape, back_basis, readout):
@@ -339,10 +340,6 @@
     key = jnp.where(mask, key, bricks * atoms * atoms * 27)
     key = lax.sort(key, is_stable=False)
     valid = jnp.sum(mask.astype(jnp.int32))
-
-    column, key, w_centre, w_neighbour, w_radial, w_hidden, w_energy = lax.optimization_barrier(
-        (column, key, w_centre, w_neighbour, w_radial, w_hidden, w_energy)
-    )
     plane = jnp.concatenate(widen(column, "gx"))
     lanes = 256 if key.shape[0] % (256 * subs) == 0 else 128
     blocks = key.shape[0] // lanes
@@ -361,11 +358,15 @@
         nothing,
     ]
     listed = jnp.stack(rows, axis=1)
+
+    def whole_blocks(pairs):
+        return (pairs.astype(jnp.uint32) // (subs * lanes)).astype(jnp.int32)
+
     window = jnp.minimum(second // width, bricks * atoms // width - 1)
     near = spans[0] * spans[2]
     in_near = (second < near * atoms).astype(jnp.int32)
-    live = (valid + subs * lanes - 1) // (subs * lanes)
-    first_part = jnp.sum(in_near) // (subs * lanes)
+    live = whole_blocks(valid + subs * lanes - 1)
+    first_part = whole_blocks(jnp.sum(in_near))
     near_part = (jnp.arange(blocks) // subs) < first_part
     least = jnp.minimum(
         window[:, 0], jnp.where(near_part, near, bricks) * atoms // width - 4
@@ -383,9 +384,11 @@
     radial_two = jnp.concatenate([radial_high, radial_low], axis=0).astype(jnp.bfloat16)
 
     vmem = pl.BlockSpec(memory_space=pltpu.VMEM)
-    weights = [jnp.concatenate([w_centre, w_neighbour], axis=0).T, radial_cat, radial_two]
-    weights += [w_hidden, w_hidden.T, w_energy[:, None]]
-    plane, listed, plan, *weights = lax.optimization_barrier((plane, listed, plan, *weights))
+    half = jnp.bfloat16(0.5)
+    quarter = jnp.bfloat16(0.25)
+    weights = [jnp.concatenate([w_centre, w_neighbour], axis=0).T * half]
+    weights += [radial_cat * half, radial_two]
+    weights += [w_hidden * quarter, w_hidden.T * half, w_energy[:, None]]
     tables = widen(plane, "gy")
 
     def run(stage, before, images, count):

time: 107 us -> 90.9 us (0.85)
  starting transfers between devices: 29.5 us -> 15.8 us
  waiting for transfers between devices: 28.6 us -> 20.3 us
  local copies, waits for them, and re-layouts: 6.4 us -> 9.49 us
  other arithmetic: 10.9 us -> 13.8 us
  between operations: 5.63 us -> 3.63 us
  Pallas kernels: 26.3 us -> 28 us
    ppermute x2, starting transfers between devices: 20.7 us -> 4.77 us  [fold(): total = total + lax.ppermute(blocks[2], axis, ring(axis, -1))]
    ppermute x2, waiting for transfers between devices: 9.97 us -> 2.97 us  [widen(): parts.append(lax.ppermute(block, axis, ring(axis, 1)))]
    ppermute x3, starting transfers between devices: 0.13 us -> 3.86 us  [fold(): total = blocks[0] + lax.ppermute(blocks[1], axis, ring(axis, 1))]
    ppermute x2, starting transfers between devices: 3.13 us -> 0.5 us  [widen(): parts.append(lax.ppermute(block, axis, ring(axis, 1)))]
    unnamed x29 -> x38, local copies, waits for them, and re-layouts: 3.23 us -> 5.77 us
    ppermute x3, waiting for transfers between devices: 9.65 us -> 12.1 us  [widen(): parts = [block, lax.ppermute(block, axis, ring(axis, -1))]]
    ppermute x3, waiting for transfers between devices: 7.2 us -> 5.27 us  [fold(): total = blocks[0] + lax.ppermute(blocks[1], axis, ring(axis, 1))]
    ppermute x2, waiting for transfers between devices: 1.75 us -> 0.01 us  [fold(): total = total + lax.ppermute(blocks[2], axis, ring(axis, -1))]
  transfers between devices with their start and end apart: 10 -> 10, of which waited for: 7 -> 6; matrix products, arithmetic and copies ran while one was open for 8% -> 19% of each run, Pallas kernels for 8% -> 9%
where the time goes in v6:
time: 90.9 us; the launch traced here: 91.2 us
  Pallas kernels  28 us (31%)
  waiting for transfers between devices  20.3 us (22%)
  starting transfers between devices  15.8 us (17%)
  other arithmetic  13.8 us (15%)
  local copies, waits for them, and re-layouts  9.49 us (10%)
  between operations  3.63 us (4%)
    pallas_call x2, Pallas kernels, run(): pl.pallas_call(functools.partial(pair_kernel, stage), out_shape=jax.Shape...  28 us
    ppermute x3, waiting for transfers between devices, widen(): parts = [block, lax.ppermute(block, axis, ring(axis, -1))]  12.1 us
    ppermute x3, starting transfers between devices, widen(): parts = [block, lax.ppermute(block, axis, ring(axis, -1))]  6.72 us
    sort x1, other arithmetic, local(): key = lax.sort(key, is_stable=False)  6.29 us
    unnamed x38, local copies, waits for them, and re-layouts  5.77 us
    ppermute x3, waiting for transfers between devices, fold(): total = blocks[0] + lax.ppermute(blocks[1], axis, ring(axis, 1))  5.27 us
    ppermute x2, starting transfers between devices, fold(): total = total + lax.ppermute(blocks[2], axis, ring(axis, -1))  4.77 us
    ppermute x3, starting transfers between devices, fold(): total = blocks[0] + lax.ppermute(blocks[1], axis, ring(axis, 1))  3.86 us
  transfers between devices with their start and end apart: 10, of which 6 were waited for; matrix products, arithmetic and copies ran while one was open for 19% of the time, Pallas kernels for 9%

profile of v6, /device:TPU:0, one launch (start us, length us, event | category | flops | bytes accessed | tf_op | source)
XLA Modules:
  0.0 91.2 jit_solution(12253830794581525212)
XLA Ops:
  1.3 1.1 %copy.52 = bf16[1,1,1,512,128]{3,4,2,1,0:T(8,128)(2,1)S(1)} copy(bf16[1,1,1,512,128]{4,3,2,1,0:T(8,128)(2,1)} %param.12) | data formatting | bytes 262144 | tf_op args[0]
  2.6 0.5 copy-done.12
  3.1 0.6 select_reduce_fusion
  4.6 5.1 %collective-permute-start = (bf16[4,144,128]{2,1,0:T(8,128)(2,1)S(1)}, bf16[4,144,128]{2,1,0:T(8,128)(2,1)S(1)}, u32[]{:S(2)}, u32[]{:S(2)}) collective-permute-start(bf16[4,144,128]{2,1,0:T(8,128)(2,1)S(1)} %pad_maximum_fusion), channel_id=1, source_target_pairs={{0,3},{1,0},{2,1},{3,2},{4,7},{5,4},{6,5},{7,6},{8,11},{9,8},{10,9... | collective-permute-start | bytes 442376 | tf_op jit(solution)/shard_map/ppermute | solution.py:36
  9.7 0.6 convert_reduce_fusion
  10.8 6.3 %sort.7 = s32[16384]{0:T(1024)S(1)} sort(s32[16384]{0:T(1024)S(1)} %fusion.11), dimensions={0}, to_apply=%region_0.1 | sort | flops 229376 | bytes 131072 | tf_op jit(solution)/shard_map/sort | solution.py:341
  17.1 0.7 broadcast_remainder_fusion
  18.9 1.3 %fusion.21 = (s32[64,1,256]{2,1,0:T(1,128)}, s32[64,1,256]{2,1,0:T(1,128)S(1)}, s32[64,1,256]{2,1,0:T(1,128)}) fusion(s32[64,1,256]{2,1,0:T(1,128)S(1)} %bitcast.101, s32[64,1,256]{2,1,0:T(1,128)S(1)} %bitcast.102, pred[64,1,256]{2,1,0:T(4,128)(4,1)S(1)} %ne.354), kind=kLoop, calls=%fused_computation.53 | loop fusion | flops 425984 | bytes 344064 | tf_op jit(solution)/shard_map/sub | solution.py:357
  20.2 0.8 compare_convert_fusion
  21.1 0.6 copy-done.11
  22.8 1.6 %collective-permute-start.2 = (bf16[12,144,128]{2,1,0:T(8,128)(2,1)S(1)}, bf16[12,144,128]{2,1,0:T(8,128)(2,1)S(1)}, u32[]{:S(2)}, u32[]{:S(2)}) collective-permute-start(bf16[12,144,128]{2,1,0:T(8,128)(2,1)S(1)} %get-tuple-element.19), channel_id=1, source_target_pairs={{0,16},{16,0},{1,17},{17,1},{2,18},{18,2},{3,19},{19,3},{4,20},{20... | collective-permute-start | bytes 1327112 | tf_op jit(solution)/shard_map/ppermute | solution.py:36
  24.5 1.6 %fusion.20 = (s32[64,1,256]{2,1,0:T(1,128)}, s32[64,1,256]{2,1,0:T(1,128)}) fusion(s32[64,1,256]{2,1,0:T(1,128)S(1)} %get-tuple-element.3), kind=kLoop, calls=%fused_computation.52 | loop fusion | flops 360448 | bytes 196608 | tf_op jit(solution)/shard_map/sub | solution.py:356
  26.1 8.5 %collective-permute-done.2 = bf16[12,144,128]{2,1,0:T(8,128)(2,1)S(1)} collective-permute-done((bf16[12,144,128]{2,1,0:T(8,128)(2,1)S(1)}, bf16[12,144,128]{2,1,0:T(8,128)(2,1)S(1)}, u32[]{:S(2)}, u32[]{:S(2)}) %collective-permute-start.2) | collective-permute-done | bytes 442400 | tf_op jit(solution)/shard_map/ppermute | solution.py:36
  35.4 0.8 copy.55
  36.3 0.7 copy.53
  37.1 0.7 copy.54
  37.9 0.7 copy-done.13
  38.7 1.6 %stack.38.pairs_ref = s32[64,8,256]{2,1,0:T(8,128)S(1)} concatenate(s32[64,1,256]{2,1,0:T(1,128)} %get-tuple-element.37, s32[64,1,256]{2,1,0:T(1,128)} %get-tuple-element.5, s32[64,1,256]{2,1,0:T(1,128)S(1)} %get-tuple-element.4, s32[64,1,256]{2,1,0:T(1,128)S(1)} %ne.344, s32[64,1,256]{2,1,0:T(1,128)} %get-tuple-element.36, s32[64,1,256]{2,1,0:T(1,128)} %get-tuple-element.35, ...), dimensions={1} | concatenate | bytes 1048576 | tf_op jit(solution)/shard_map/stack | solution.py:360
  40.4 1.0 %broadcast_multiply_fusion.refs_4_.refs_7_ = bf16[256,256]{1,0:T(8,128)(2,1)S(1)} fusion(bf16[256,256]{1,0:T(8,128)(2,1)} %param.22), kind=kLoop, calls=%fused_computation.58 | loop fusion | flops 65536 | bytes 262144 | tf_op jit(solution)/shard_map/mul | solution.py:391
  41.4 8.6 %near_pairs.1.refs_0_ = f32[6,4,512]{2,1,0:T(4,128)S(1)} custom-call(s32[131]{0:T(256)S(1)} %pad_add_fusion.1.plan_ref, s32[64,8,256]{2,1,0:T(8,128)S(1)} %stack.38.pairs_ref, bf16[24,144,128]{2,1,0:T(8,128)(2,1)S(1)} %constant_dynamic-update-slice_fusion.6.refs_0_.refs_1_, bf16[256,256]{1,0:T(8,128)(2,1)S(1)} %get-tuple-element.52.refs_1_.refs_4_, ...), custom_call_target="tpu_custom_call" | custom-call | flops 2684354560 | bytes 786432 | tf_op jit(solution)/shard_map/near_pairs/pallas_call | solution.py:398
  50.1 3.6 %collective-permute-done.3.refs_2_ = bf16[24,144,128]{2,1,0:T(8,128)(2,1)S(1)} collective-permute-done((bf16[24,144,128]{2,1,0:T(8,128)(2,1)S(1)}, bf16[24,144,128]{2,1,0:T(8,128)(2,1)S(1)}, u32[]{:S(2)}, u32[]{:S(2)}) %collective-permute-start.3) | collective-permute-done | bytes 884768 | tf_op jit(solution)/shard_map/ppermute | solution.py:36
  53.7 3.0 %collective-permute-done.4.refs_3_ = bf16[24,144,128]{2,1,0:T(8,128)(2,1)S(1)} collective-permute-done((bf16[24,144,128]{2,1,0:T(8,128)(2,1)S(1)}, bf16[24,144,128]{2,1,0:T(8,128)(2,1)S(1)}, u32[]{:S(2)}, u32[]{:S(2)}) %collective-permute-start.4) | collective-permute-done | bytes 884768 | tf_op jit(solution)/shard_map/ppermute | solution.py:38
  56.7 19.3 %far_pairs.1 = f32[18,4,512]{2,1,0:T(4,128)S(1)} custom-call(s32[131]{0:T(256)S(1)} %pad_add_fusion.1.plan_ref, s32[64,8,256]{2,1,0:T(8,128)S(1)} %stack.38.pairs_ref, f32[6,4,512]{2,1,0:T(4,128)S(1)} %near_pairs.1.refs_0_, bf16[24,144,128]{2,1,0:T(8,128)(2,1)S(1)} %constant_dynamic-update-slice_fusion.6.refs_0_.refs_1_, ...), custom_call_target="tpu_custom_call" | custom-call | flops 5368709120 | bytes 2359296 | tf_op jit(solution)/shard_map/far_pairs/pallas_call | solution.py:398
  76.1 1.7 %collective-permute-start.6 = (f32[2,3,4,512]{3,2,1,0:T(4,128)S(1)}, f32[2,3,4,512]{3,2,1,0:T(4,128)S(1)}, u32[]{:S(2)}, u32[]{:S(2)}) collective-permute-start(f32[2,3,4,512]{3,2,1,0:T(4,128)S(1)} %bitcast.104), channel_id=1, source_target_pairs={{0,12},{4,0},{8,4},{12,8},{1,13},{5,1},{9,5},{13,9},{2,14},{6,2},{... | collective-permute-start | bytes 147464 | tf_op jit(solution)/shard_map/ppermute | solution.py:45
  77.8 1.8 %collective-permute-done.5 = f32[2,3,4,512]{3,2,1,0:T(4,128)S(1)} collective-permute-done((f32[2,3,4,512]{3,2,1,0:T(4,128)S(1)}, f32[2,3,4,512]{3,2,1,0:T(4,128)S(1)}, u32[]{:S(2)}, u32[]{:S(2)}) %collective-permute-start.5) | collective-permute-done | bytes 49184 | tf_op jit(solution)/shard_map/ppermute | solution.py:43
  79.6 3.0 %collective-permute-start.7 = (f32[3,4,512]{2,1,0:T(4,128)S(1)}, f32[3,4,512]{2,1,0:T(4,128)S(1)}, u32[]{:S(2)}, u32[]{:S(2)}) collective-permute-start(f32[3,4,512]{2,1,0:T(4,128)S(1)} %slice_bitcast_fusion.4), channel_id=1, source_target_pairs={{0,16},{16,0},{1,17},{17,1},{2,18},{18,2},{3,19},{19,3},{4,20},{20... | collective-permute-start | bytes 73736 | tf_op jit(solution)/shard_map/ppermute | solution.py:43
  82.6 1.8 %collective-permute-done.7 = f32[3,4,512]{2,1,0:T(4,128)S(1)} collective-permute-done((f32[3,4,512]{2,1,0:T(4,128)S(1)}, f32[3,4,512]{2,1,0:T(4,128)S(1)}, u32[]{:S(2)}, u32[]{:S(2)}) %collective-permute-start.7) | collective-permute-done | bytes 24608 | tf_op jit(solution)/shard_map/ppermute | solution.py:43
  84.4 0.8 collective-permute-start.8
  85.2 3.0 %collective-permute-start.9 = (f32[4,512]{1,0:T(4,128)S(1)}, f32[4,512]{1,0:T(4,128)S(1)}, u32[]{:S(2)}, u32[]{:S(2)}) collective-permute-start(f32[4,512]{1,0:T(4,128)S(1)} %get-tuple-element.46), channel_id=1, source_target_pairs={{0,3},{1,0},{2,1},{3,2},{4,7},{5,4},{6,5},{7,6},{8,11},{9,8},{10,9... | collective-permute-start | bytes 24584 | tf_op jit(solution)/shard_map/ppermute | solution.py:45
  88.3 1.7 %collective-permute-done.8 = f32[4,512]{1,0:T(4,128)S(1)} collective-permute-done((f32[4,512]{1,0:T(4,128)S(1)}, f32[4,512]{1,0:T(4,128)S(1)}, u32[]{:S(2)}, u32[]{:S(2)}) %collective-permute-start.8) | collective-permute-done | bytes 8224 | tf_op jit(solution)/shard_map/ppermute | solution.py:43
  90.0 0.6 slice_bitcast_fusion.9
  90.6 0.6 broadcast_in_dim.47
  (74 shorter events, 3.1 us)
Async XLA Ops:
  0.6 1.8 %copy-start = (bf16[128]{0:T(256)(128)(2,1)S(1)}, bf16[128]{0:T(256)(128)(2,1)}, u32[]{:S(2)}) copy-start(bf16[128]{0:T(256)(128)(2,1)} %param.20) | copy-start | bytes 772
  1.3 1.1 %copy-start.1 = (bf16[1,1,1,512,128]{4,3,2,1,0:T(8,128)(2,1)S(1)}, bf16[1,1,1,512,128]{4,3,2,1,0:T(8,128)(2,1)}, u32[]{:S(2)}) copy-start(bf16[1,1,1,512,128]{4,3,2,1,0:T(8,128)(2,1)} %param.12) | copy-start | bytes 393220
  2.4 0.7 copy-start.12
  4.5 5.8 %copy-start.8 = (s32[1,1,1,128,128]{4,3,2,1,0:T(8,128)S(1)}, s32[1,1,1,128,128]{4,3,2,1,0:T(8,128)}, u32[]{:S(2)}) copy-start(s32[1,1,1,128,128]{4,3,2,1,0:T(8,128)} %param.16) | copy-start | bytes 196612
  4.5 5.1 %copy-start.6 = (s32[1,1,1,128,128]{4,3,2,1,0:T(8,128)S(1)}, s32[1,1,1,128,128]{4,3,2,1,0:T(8,128)}, u32[]{:S(2)}) copy-start(s32[1,1,1,128,128]{4,3,2,1,0:T(8,128)} %param.17) | copy-start | bytes 196612
  4.6 18.1 %collective-permute-start = (bf16[4,144,128]{2,1,0:T(8,128)(2,1)S(1)}, bf16[4,144,128]{2,1,0:T(8,128)(2,1)S(1)}, u32[]{:S(2)}, u32[]{:S(2)}) collective-permute-start(bf16[4,144,128]{2,1,0:T(8,128)(2,1)S(1)} %pad_maximum_fusion), channel_id=1, source_target_pairs={{0,3},{1,0},{2,1},{3,2},{4,7},{5,4},{6,5},{7,6},{8,11},{9,8},{10,9... | collective-permute-start | bytes 442376 | tf_op jit(solution)/shard_map/ppermute | solution.py:36
  9.7 13.1 %collective-permute-start.1 = (bf16[4,144,128]{2,1,0:T(8,128)(2,1)S(1)}, bf16[4,144,128]{2,1,0:T(8,128)(2,1)S(1)}, u32[]{:S(2)}, u32[]{:S(2)}) collective-permute-start(bf16[4,144,128]{2,1,0:T(8,128)(2,1)S(1)} %pad_maximum_fusion), channel_id=1, source_target_pairs={{0,1},{1,2},{2,3},{3,0},{4,5},{5,6},{6,7},{7,4},{8,9},{9,10},{10,1... | collective-permute-start | bytes 442376 | tf_op jit(solution)/shard_map/ppermute | solution.py:38
  9.7 0.8 copy-start.7
  21.0 0.7 copy-start.11
  22.8 11.7 %collective-permute-start.2 = (bf16[12,144,128]{2,1,0:T(8,128)(2,1)S(1)}, bf16[12,144,128]{2,1,0:T(8,128)(2,1)S(1)}, u32[]{:S(2)}, u32[]{:S(2)}) collective-permute-start(bf16[12,144,128]{2,1,0:T(8,128)(2,1)S(1)} %get-tuple-element.19), channel_id=1, source_target_pairs={{0,16},{16,0},{1,17},{17,1},{2,18},{18,2},{3,19},{19,3},{4,20},{20... | collective-permute-start | bytes 1327112 | tf_op jit(solution)/shard_map/ppermute | solution.py:36
  34.5 0.9 copy-start.2
  34.6 19.1 %collective-permute-start.3 = (bf16[24,144,128]{2,1,0:T(8,128)(2,1)S(1)}, bf16[24,144,128]{2,1,0:T(8,128)(2,1)S(1)}, u32[]{:S(2)}, u32[]{:S(2)}) collective-permute-start(bf16[24,144,128]{2,1,0:T(8,128)(2,1)S(1)} %constant_dynamic-update-slice_fusion.6.refs_0_.refs_1_), channel_id=1, source_target_pairs={{0,12},{4,0},{8,4},{12,8},{1,13},{5,1},{9,5},{13,9},{2,14},{6,2},{... | collective-permute-start | bytes 2654216 | tf_op jit(solution)/shard_map/ppermute | solution.py:36
  34.7 22.0 %collective-permute-start.4 = (bf16[24,144,128]{2,1,0:T(8,128)(2,1)S(1)}, bf16[24,144,128]{2,1,0:T(8,128)(2,1)S(1)}, u32[]{:S(2)}, u32[]{:S(2)}) collective-permute-start(bf16[24,144,128]{2,1,0:T(8,128)(2,1)S(1)} %constant_dynamic-update-slice_fusion.6.refs_0_.refs_1_), channel_id=1, source_target_pairs={{0,4},{4,8},{8,12},{12,0},{1,5},{5,9},{9,13},{13,1},{2,6},{6,10},{... | collective-permute-start | bytes 2654216 | tf_op jit(solution)/shard_map/ppermute | solution.py:38
  35.4 0.8 copy-start.9
  36.3 0.8 copy-start.10
  37.9 0.7 copy-start.13
  40.3 1.0 %copy-start.3 = (bf16[256,256]{0,1:T(8,128)(2,1)S(1)}, bf16[256,256]{0,1:T(8,128)(2,1)}, u32[]{:S(2)}) copy-start(bf16[256,256]{0,1:T(8,128)(2,1)} %copy.55) | copy-start | bytes 393220
  40.3 1.0 %copy-start.4 = (bf16[128,256]{0,1:T(8,128)(2,1)S(1)}, bf16[128,256]{0,1:T(8,128)(2,1)}, u32[]{:S(2)}) copy-start(bf16[128,256]{0,1:T(8,128)(2,1)} %copy.53) | copy-start | bytes 196612
  40.4 1.0 %copy-start.5 = (bf16[128,256]{0,1:T(8,128)(2,1)S(1)}, bf16[128,256]{0,1:T(8,128)(2,1)}, u32[]{:S(2)}) copy-start(bf16[128,256]{0,1:T(8,128)(2,1)} %copy.54) | copy-start | bytes 196612
  76.0 3.6 %collective-permute-start.5 = (f32[2,3,4,512]{3,2,1,0:T(4,128)S(1)}, f32[2,3,4,512]{3,2,1,0:T(4,128)S(1)}, u32[]{:S(2)}, u32[]{:S(2)}) collective-permute-start(f32[2,3,4,512]{3,2,1,0:T(4,128)S(1)} %bitcast.105), channel_id=1, source_target_pairs={{0,4},{4,8},{8,12},{12,0},{1,5},{5,9},{9,13},{13,1},{2,6},{6,10},{... | collective-permute-start | bytes 147464 | tf_op jit(solution)/shard_map/ppermute | solution.py:43
  76.1 3.5 %collective-permute-start.6 = (f32[2,3,4,512]{3,2,1,0:T(4,128)S(1)}, f32[2,3,4,512]{3,2,1,0:T(4,128)S(1)}, u32[]{:S(2)}, u32[]{:S(2)}) collective-permute-start(f32[2,3,4,512]{3,2,1,0:T(4,128)S(1)} %bitcast.104), channel_id=1, source_target_pairs={{0,12},{4,0},{8,4},{12,8},{1,13},{5,1},{9,5},{13,9},{2,14},{6,2},{... | collective-permute-start | bytes 147464 | tf_op jit(solution)/shard_map/ppermute | solution.py:45
  79.6 4.8 %collective-permute-start.7 = (f32[3,4,512]{2,1,0:T(4,128)S(1)}, f32[3,4,512]{2,1,0:T(4,128)S(1)}, u32[]{:S(2)}, u32[]{:S(2)}) collective-permute-start(f32[3,4,512]{2,1,0:T(4,128)S(1)} %slice_bitcast_fusion.4), channel_id=1, source_target_pairs={{0,16},{16,0},{1,17},{17,1},{2,18},{18,2},{3,19},{19,3},{4,20},{20... | collective-permute-start | bytes 73736 | tf_op jit(solution)/shard_map/ppermute | solution.py:43
  84.4 5.6 %collective-permute-start.8 = (f32[4,512]{1,0:T(4,128)S(1)}, f32[4,512]{1,0:T(4,128)S(1)}, u32[]{:S(2)}, u32[]{:S(2)}) collective-permute-start(f32[4,512]{1,0:T(4,128)S(1)} %get-tuple-element.45), channel_id=1, source_target_pairs={{0,1},{1,2},{2,3},{3,0},{4,5},{5,6},{6,7},{7,4},{8,9},{9,10},{10,1... | collective-permute-start | bytes 24584 | tf_op jit(solution)/shard_map/ppermute | solution.py:43
  85.2 4.7 %collective-permute-start.9 = (f32[4,512]{1,0:T(4,128)S(1)}, f32[4,512]{1,0:T(4,128)S(1)}, u32[]{:S(2)}, u32[]{:S(2)}) collective-permute-start(f32[4,512]{1,0:T(4,128)S(1)} %get-tuple-element.46), channel_id=1, source_target_pairs={{0,3},{1,0},{2,1},{3,2},{4,7},{5,4},{6,5},{7,6},{8,11},{9,8},{10,9... | collective-permute-start | bytes 24584 | tf_op jit(solution)/shard_map/ppermute | solution.py:45

commit v7 on v6

--- a/solution.py
+++ b/solution.py
@@ -340,7 +340,10 @@
     key = jnp.where(mask, key, bricks * atoms * atoms * 27)
     key = lax.sort(key, is_stable=False)
     valid = jnp.sum(mask.astype(jnp.int32))
-    plane = jnp.concatenate(widen(column, "gx"))
+    side_x = widen(column, "gx")[1:]
+    side_x = jnp.concatenate(side_x) if len(side_x) > 1 else side_x[0]
+    columns = widen(column, "gy")
+    side_x, key = lax.optimization_barrier((side_x, key))
     lanes = 256 if key.shape[0] % (256 * subs) == 0 else 128
     blocks = key.shape[0] // lanes
     key = key.reshape(blocks, lanes)
@@ -389,7 +392,8 @@
     weights = [jnp.concatenate([w_centre, w_neighbour], axis=0).T * half]
     weights += [radial_cat * half, radial_two]
     weights += [w_hidden * quarter, w_hidden.T * half, w_energy[:, None]]
-    tables = widen(plane, "gy")
+    sides = widen(side_x, "gy")
+    tables = [table for pair in zip(columns, sides) for table in pair]
 
     def run(stage, before, images, count):
         operands = [listed, *before, *images, *weights]
@@ -421,7 +425,7 @@
             name="near_pairs" if stage == 0 else "far_pairs",
         )(plan, *operands)
 
-    partial = run(0, [], tables[:1], near)
+    partial = run(0, [], tables[:2], near)
     partial = run(1, [partial], tables, bricks)
     partial = partial.reshape(spans[1], spans[0], spans[2], 4, atoms)
     partial = fold(partial, "gy")

time: 90.9 us -> 86.7 us (0.954); the launches traced: 91.2 us -> 86 us
  starting transfers between devices: 15.8 us -> 24.9 us
  Pallas kernels: 28 us -> 20.2 us
  waiting for transfers between devices: 20.3 us -> 17.1 us
  local copies, waits for them, and re-layouts: 9.49 us -> 7.79 us
  other arithmetic: 13.8 us -> 12.2 us
    ppermute x3, starting transfers between devices: 3.86 us -> 12.3 us  [fold(): total = blocks[0] + lax.ppermute(blocks[1], axis, ring(axis, 1))]
    pallas_call x2, Pallas kernels: 28 us -> 20.2 us  [run(): pl.pallas_call(functools.partial(pair_kernel, stage), out_shape=jax.Shape...]
    ppermute x3 -> x4, waiting for transfers between devices: 12.1 us -> 8.11 us  [widen(): parts = [block, lax.ppermute(block, axis, ring(axis, -1))]]
    ppermute x2, waiting for transfers between devices: 0.01 us -> 3.85 us  [fold(): total = total + lax.ppermute(blocks[2], axis, ring(axis, -1))]
    ppermute x2 -> x3, waiting for transfers between devices: 2.97 us -> 0.01 us  [widen(): parts.append(lax.ppermute(block, axis, ring(axis, 1)))]
    ppermute x2 -> x3, starting transfers between devices: 0.5 us -> 3.14 us  [widen(): parts.append(lax.ppermute(block, axis, ring(axis, 1)))]
    ppermute x2, starting transfers between devices: 4.77 us -> 2.18 us  [fold(): total = total + lax.ppermute(blocks[2], axis, ring(axis, -1))]
    unnamed x38 -> x32, local copies, waits for them, and re-layouts: 5.77 us -> 4.18 us
  transfers between devices with their start and end apart: 10 -> 12, of which waited for: 6 -> 6; matrix products, arithmetic and copies ran while one was open for 19% -> 17% of each run, Pallas kernels for 9% -> 5%
where the time goes in v7:
time: 86.7 us; the launch traced here: 86 us
  starting transfers between devices  24.9 us (29%)
  Pallas kernels  20.2 us (23%)
  waiting for transfers between devices  17.1 us (20%)
  other arithmetic  12.2 us (14%)
  local copies, waits for them, and re-layouts  7.79 us (9%)
  between operations  3.67 us (4%)
    pallas_call x2, Pallas kernels, run(): pl.pallas_call(functools.partial(pair_kernel, stage), out_shape=jax.Shape...  20.2 us
    ppermute x3, starting transfers between devices, fold(): total = blocks[0] + lax.ppermute(blocks[1], axis, ring(axis, 1))  12.3 us
    ppermute x4, waiting for transfers between devices, widen(): parts = [block, lax.ppermute(block, axis, ring(axis, -1))]  8.11 us
    ppermute x4, starting transfers between devices, widen(): parts = [block, lax.ppermute(block, axis, ring(axis, -1))]  7.28 us
    sort x1, other arithmetic, local(): key = lax.sort(key, is_stable=False)  6.28 us
    ppermute x3, waiting for transfers between devices, fold(): total = blocks[0] + lax.ppermute(blocks[1], axis, ring(axis, 1))  5.12 us
    unnamed x32, local copies, waits for them, and re-layouts  4.18 us
    ppermute x2, waiting for transfers between devices, fold(): total = total + lax.ppermute(blocks[2], axis, ring(axis, -1))  3.85 us
  transfers between devices with their start and end apart: 12, of which 6 were waited for; matrix products, arithmetic and copies ran while one was open for 17% of the time, Pallas kernels for 5%

profile of v7, /device:TPU:0, one launch (start us, length us, event | category | flops | bytes accessed | tf_op | source)
XLA Modules:
  0.0 86.0 jit_solution(9307289008245522392)
XLA Ops:
  1.3 1.1 %copy.48 = bf16[1,1,1,512,128]{3,4,2,1,0:T(8,128)(2,1)S(1)} copy(bf16[1,1,1,512,128]{4,3,2,1,0:T(8,128)(2,1)} %param.12) | data formatting | bytes 262144 | tf_op args[0]
  2.6 0.5 copy-done.9
  3.1 0.6 select_reduce_fusion
  4.6 3.1 %collective-permute-start.1 = (bf16[4,144,128]{2,1,0:T(8,128)(2,1)S(1)}, bf16[4,144,128]{2,1,0:T(8,128)(2,1)S(1)}, u32[]{:S(2)}, u32[]{:S(2)}) collective-permute-start(bf16[4,144,128]{2,1,0:T(8,128)(2,1)S(1)} %pad_maximum_fusion), channel_id=1, source_target_pairs={{0,1},{1,2},{2,3},{3,0},{4,5},{5,6},{6,7},{7,4},{8,9},{9,10},{10,1... | collective-permute-start | bytes 442376 | tf_op jit(solution)/shard_map/ppermute | solution.py:38
  7.6 2.1 %collective-permute-start = (bf16[4,144,128]{2,1,0:T(8,128)(2,1)S(1)}, bf16[4,144,128]{2,1,0:T(8,128)(2,1)S(1)}, u32[]{:S(2)}, u32[]{:S(2)}) collective-permute-start(bf16[4,144,128]{2,1,0:T(8,128)(2,1)S(1)} %pad_maximum_fusion), channel_id=1, source_target_pairs={{0,3},{1,0},{2,1},{3,2},{4,7},{5,4},{6,5},{7,6},{8,11},{9,8},{10,9... | collective-permute-start | bytes 442376 | tf_op jit(solution)/shard_map/ppermute | solution.py:36
  9.8 0.6 convert_reduce_fusion
  10.6 0.7 copy-done.4
  11.3 0.3 fusion.11
  12.4 6.3 %sort.7 = s32[16384]{0:T(1024)S(1)} sort(s32[16384]{0:T(1024)S(1)} %fusion.11), dimensions={0}, to_apply=%region_1.2 | sort | flops 229376 | bytes 131072 | tf_op jit(solution)/shard_map/sort | solution.py:341
  18.8 0.7 copy-done.7
  19.7 0.7 copy-done.10
  20.7 1.7 %collective-permute-start.2 = (bf16[12,144,128]{2,1,0:T(8,128)(2,1)S(1)}, bf16[12,144,128]{2,1,0:T(8,128)(2,1)S(1)}, u32[]{:S(2)}, u32[]{:S(2)}) collective-permute-start(bf16[12,144,128]{2,1,0:T(8,128)(2,1)S(1)} %constant_dynamic-update-slice_fusion.refs_0_.refs_1_), channel_id=1, source_target_pairs={{0,16},{16,0},{1,17},{17,1},{2,18},{18,2},{3,19},{19,3},{4,20},{20... | collective-permute-start | bytes 1327112 | tf_op jit(solution)/shard_map/ppermute | solution.py:36
  22.6 1.7 %collective-permute-start.3 = (bf16[12,144,128]{2,1,0:T(8,128)(2,1)S(1)}, bf16[12,144,128]{2,1,0:T(8,128)(2,1)S(1)}, u32[]{:S(2)}, u32[]{:S(2)}) collective-permute-start(bf16[12,144,128]{2,1,0:T(8,128)(2,1)S(1)} %constant_dynamic-update-slice_fusion.refs_0_.refs_1_), channel_id=1, source_target_pairs={{0,12},{4,0},{8,4},{12,8},{1,13},{5,1},{9,5},{13,9},{2,14},{6,2},{... | collective-permute-start | bytes 1327112 | tf_op jit(solution)/shard_map/ppermute | solution.py:36
  24.3 8.1 %collective-permute-done.2.refs_1_.refs_2_ = bf16[12,144,128]{2,1,0:T(8,128)(2,1)S(1)} collective-permute-done((bf16[12,144,128]{2,1,0:T(8,128)(2,1)S(1)}, bf16[12,144,128]{2,1,0:T(8,128)(2,1)S(1)}, u32[]{:S(2)}, u32[]{:S(2)}) %collective-permute-start.2) | collective-permute-done | bytes 442400 | tf_op jit(solution)/shard_map/ppermute | solution.py:36
  32.4 1.7 %collective-permute-start.4 = (bf16[12,144,128]{2,1,0:T(8,128)(2,1)S(1)}, bf16[12,144,128]{2,1,0:T(8,128)(2,1)}, u32[]{:S(2)}, u32[]{:S(2)}) collective-permute-start(bf16[12,144,128]{2,1,0:T(8,128)(2,1)S(1)} %collective-permute-done.2.refs_1_.refs_2_), channel_id=1, source_target_pairs={{0,12},{4,0},{8,4},{12,8},{1,13},{5,1},{9,5},{13,9},{2,14},{6,2},{... | collective-permute-start | bytes 1327112 | tf_op jit(solution)/shard_map/ppermute | solution.py:36
  34.1 0.7 broadcast_remainder_fusion
  35.9 1.4 %fusion.21 = (s32[64,1,256]{2,1,0:T(1,128)}, s32[64,1,256]{2,1,0:T(1,128)S(1)}, s32[64,1,256]{2,1,0:T(1,128)}) fusion(s32[64,1,256]{2,1,0:T(1,128)S(1)} %bitcast.93, s32[64,1,256]{2,1,0:T(1,128)S(1)} %bitcast.94, pred[64,1,256]{2,1,0:T(4,128)(4,1)S(1)} %ne.354), kind=kLoop, calls=%fused_computation.53 | loop fusion | flops 425984 | bytes 344064 | tf_op jit(solution)/shard_map/sub | solution.py:360
  37.2 0.9 %fusion.20 = (s32[64,1,256]{2,1,0:T(1,128)S(1)}, s32[64,1,256]{2,1,0:T(1,128)S(1)}) fusion(s32[64,1,256]{2,1,0:T(1,128)S(1)} %get-tuple-element.7), kind=kLoop, calls=%fused_computation.52 | loop fusion | flops 360448 | bytes 196608 | tf_op jit(solution)/shard_map/sub | solution.py:359
  38.2 0.8 compare_convert_fusion
  39.3 1.6 %stack.43.pairs_ref = s32[64,8,256]{2,1,0:T(8,128)S(1)} concatenate(s32[64,1,256]{2,1,0:T(1,128)} %get-tuple-element.29, s32[64,1,256]{2,1,0:T(1,128)} %get-tuple-element.9, s32[64,1,256]{2,1,0:T(1,128)} %get-tuple-element.8, s32[64,1,256]{2,1,0:T(1,128)S(1)} %ne.344, s32[64,1,256]{2,1,0:T(1,128)S(1)} %get-tuple-element.28, s32[64,1,256]{2,1,0:T(1,128)S(1)} %get-tuple-element.27, ...), dimensions={1} | concatenate | bytes 1048576 | tf_op jit(solution)/shard_map/stack | solution.py:363
  41.0 4.2 %near_pairs.1.refs_0_ = f32[6,4,512]{2,1,0:T(4,128)S(1)} custom-call(s32[131]{0:T(256)S(1)} %pad_add_fusion.1.plan_ref, s32[64,8,256]{2,1,0:T(8,128)S(1)} %stack.43.pairs_ref, bf16[12,144,128]{2,1,0:T(8,128)(2,1)S(1)} %constant_dynamic-update-slice_fusion.refs_0_.refs_1_, bf16[12,144,128]{2,1,0:T(8,128)(2,1)S(1)} %collective-permute-done.2.refs_1_.refs_2_, ...), custom_call_target="tpu_custom_call" | custom-call | flops 2684354560 | bytes 786432 | tf_op jit(solution)/shard_map/near_pairs/pallas_call | solution.py:402
  45.2 16.1 %far_pairs.1 = f32[18,4,512]{2,1,0:T(4,128)S(1)} custom-call(s32[131]{0:T(256)S(1)} %pad_add_fusion.1.plan_ref, s32[64,8,256]{2,1,0:T(8,128)S(1)} %stack.43.pairs_ref, f32[6,4,512]{2,1,0:T(4,128)S(1)} %near_pairs.1.refs_0_, bf16[12,144,128]{2,1,0:T(8,128)(2,1)S(1)} %constant_dynamic-update-slice_fusion.refs_0_.refs_1_, ...), custom_call_target="tpu_custom_call" | custom-call | flops 5368709120 | bytes 2359296 | tf_op jit(solution)/shard_map/far_pairs/pallas_call | solution.py:402
  61.3 2.2 %collective-permute-start.8 = (f32[2,3,4,512]{3,2,1,0:T(4,128)S(1)}, f32[2,3,4,512]{3,2,1,0:T(4,128)S(1)}, u32[]{:S(2)}, u32[]{:S(2)}) collective-permute-start(f32[2,3,4,512]{3,2,1,0:T(4,128)S(1)} %bitcast.97), channel_id=1, source_target_pairs={{0,12},{4,0},{8,4},{12,8},{1,13},{5,1},{9,5},{13,9},{2,14},{6,2},{... | collective-permute-start | bytes 147464 | tf_op jit(solution)/shard_map/ppermute | solution.py:45
  63.5 1.7 %collective-permute-done.8 = f32[2,3,4,512]{3,2,1,0:T(4,128)S(1)} collective-permute-done((f32[2,3,4,512]{3,2,1,0:T(4,128)S(1)}, f32[2,3,4,512]{3,2,1,0:T(4,128)S(1)}, u32[]{:S(2)}, u32[]{:S(2)}) %collective-permute-start.8) | collective-permute-done | bytes 49184 | tf_op jit(solution)/shard_map/ppermute | solution.py:45
  65.3 1.8 %collective-permute-done.7 = f32[2,3,4,512]{3,2,1,0:T(4,128)S(1)} collective-permute-done((f32[2,3,4,512]{3,2,1,0:T(4,128)S(1)}, f32[2,3,4,512]{3,2,1,0:T(4,128)S(1)}, u32[]{:S(2)}, u32[]{:S(2)}) %collective-permute-start.7) | collective-permute-done | bytes 49184 | tf_op jit(solution)/shard_map/ppermute | solution.py:43
  67.1 8.4 %collective-permute-start.9 = (f32[3,4,512]{2,1,0:T(4,128)S(1)}, f32[3,4,512]{2,1,0:T(4,128)S(1)}, u32[]{:S(2)}, u32[]{:S(2)}) collective-permute-start(f32[3,4,512]{2,1,0:T(4,128)S(1)} %slice_bitcast_fusion.4), channel_id=1, source_target_pairs={{0,16},{16,0},{1,17},{17,1},{2,18},{18,2},{3,19},{19,3},{4,20},{20... | collective-permute-start | bytes 73736 | tf_op jit(solution)/shard_map/ppermute | solution.py:43
  75.4 1.8 %collective-permute-done.9 = f32[3,4,512]{2,1,0:T(4,128)S(1)} collective-permute-done((f32[3,4,512]{2,1,0:T(4,128)S(1)}, f32[3,4,512]{2,1,0:T(4,128)S(1)}, u32[]{:S(2)}, u32[]{:S(2)}) %collective-permute-start.9) | collective-permute-done | bytes 24608 | tf_op jit(solution)/shard_map/ppermute | solution.py:43
  77.2 3.9 %collective-permute-start.10 = (f32[4,512]{1,0:T(4,128)S(1)}, f32[4,512]{1,0:T(4,128)S(1)}, u32[]{:S(2)}, u32[]{:S(2)}) collective-permute-start(f32[4,512]{1,0:T(4,128)S(1)} %get-tuple-element.37), channel_id=1, source_target_pairs={{0,1},{1,2},{2,3},{3,0},{4,5},{5,6},{6,7},{7,4},{8,9},{9,10},{10,1... | collective-permute-start | bytes 24584 | tf_op jit(solution)/shard_map/ppermute | solution.py:43
  81.2 1.6 %collective-permute-done.10 = f32[4,512]{1,0:T(4,128)S(1)} collective-permute-done((f32[4,512]{1,0:T(4,128)S(1)}, f32[4,512]{1,0:T(4,128)S(1)}, u32[]{:S(2)}, u32[]{:S(2)}) %collective-permute-start.10) | collective-permute-done | bytes 8224 | tf_op jit(solution)/shard_map/ppermute | solution.py:43
  82.7 2.1 %collective-permute-done.11 = f32[4,512]{1,0:T(4,128)S(1)} collective-permute-done((f32[4,512]{1,0:T(4,128)S(1)}, f32[4,512]{1,0:T(4,128)S(1)}, u32[]{:S(2)}, u32[]{:S(2)}) %collective-permute-start.11) | collective-permute-done | bytes 8224 | tf_op jit(solution)/shard_map/ppermute | solution.py:45
  84.8 0.6 slice_bitcast_fusion.9
  85.4 0.6 broadcast_in_dim.47
  (71 shorter events, 2.1 us)
Async XLA Ops:
  0.6 1.8 %copy-start = (bf16[128]{0:T(256)(128)(2,1)S(1)}, bf16[128]{0:T(256)(128)(2,1)}, u32[]{:S(2)}) copy-start(bf16[128]{0:T(256)(128)(2,1)} %param.20) | copy-start | bytes 772
  1.3 1.1 %copy-start.1 = (bf16[1,1,1,512,128]{4,3,2,1,0:T(8,128)(2,1)S(1)}, bf16[1,1,1,512,128]{4,3,2,1,0:T(8,128)(2,1)}, u32[]{:S(2)}) copy-start(bf16[1,1,1,512,128]{4,3,2,1,0:T(8,128)(2,1)} %param.12) | copy-start | bytes 393220
  2.4 0.7 copy-start.9
  4.5 5.2 %copy-start.8 = (f32[8,256]{1,0:T(8,128)S(1)}, f32[8,256]{1,0:T(8,128)}, u32[]{:S(2)}) copy-start(f32[8,256]{1,0:T(8,128)} %param.21) | copy-start | bytes 24580
  4.5 5.2 %copy-start.3 = (s32[1,1,1,128,128]{4,3,2,1,0:T(8,128)S(1)}, s32[1,1,1,128,128]{4,3,2,1,0:T(8,128)}, u32[]{:S(2)}) copy-start(s32[1,1,1,128,128]{4,3,2,1,0:T(8,128)} %param.17) | copy-start | bytes 196612
  4.6 16.1 %collective-permute-start.1 = (bf16[4,144,128]{2,1,0:T(8,128)(2,1)S(1)}, bf16[4,144,128]{2,1,0:T(8,128)(2,1)S(1)}, u32[]{:S(2)}, u32[]{:S(2)}) collective-permute-start(bf16[4,144,128]{2,1,0:T(8,128)(2,1)S(1)} %pad_maximum_fusion), channel_id=1, source_target_pairs={{0,1},{1,2},{2,3},{3,0},{4,5},{5,6},{6,7},{7,4},{8,9},{9,10},{10,1... | collective-permute-start | bytes 442376 | tf_op jit(solution)/shard_map/ppermute | solution.py:38
  7.6 13.0 %collective-permute-start = (bf16[4,144,128]{2,1,0:T(8,128)(2,1)S(1)}, bf16[4,144,128]{2,1,0:T(8,128)(2,1)S(1)}, u32[]{:S(2)}, u32[]{:S(2)}) collective-permute-start(bf16[4,144,128]{2,1,0:T(8,128)(2,1)S(1)} %pad_maximum_fusion), channel_id=1, source_target_pairs={{0,3},{1,0},{2,1},{3,2},{4,7},{5,4},{6,5},{7,6},{8,11},{9,8},{10,9... | collective-permute-start | bytes 442376 | tf_op jit(solution)/shard_map/ppermute | solution.py:36
  10.4 0.8 copy-start.4
  10.4 0.9 %copy-start.5 = (s32[1,1,1,128,128]{4,3,2,1,0:T(8,128)S(1)}, s32[1,1,1,128,128]{4,3,2,1,0:T(8,128)}, u32[]{:S(2)}) copy-start(s32[1,1,1,128,128]{4,3,2,1,0:T(8,128)} %param.16) | copy-start | bytes 196612
  12.4 6.3 %copy-start.6 = (bf16[128,256]{1,0:T(8,128)(2,1)S(1)}, bf16[128,256]{1,0:T(8,128)(2,1)}, u32[]{:S(2)}) copy-start(bf16[128,256]{1,0:T(8,128)(2,1)} %param.18) | copy-start | bytes 196612
  18.7 0.8 copy-start.7
  19.6 0.9 %copy-start.2 = (bf16[256,256]{1,0:T(8,128)(2,1)S(1)}, bf16[256,256]{1,0:T(8,128)(2,1)}, u32[]{:S(2)}) copy-start(bf16[256,256]{1,0:T(8,128)(2,1)} %param.22) | copy-start | bytes 393220
  19.7 0.7 copy-start.10
  20.7 11.7 %collective-permute-start.2 = (bf16[12,144,128]{2,1,0:T(8,128)(2,1)S(1)}, bf16[12,144,128]{2,1,0:T(8,128)(2,1)S(1)}, u32[]{:S(2)}, u32[]{:S(2)}) collective-permute-start(bf16[12,144,128]{2,1,0:T(8,128)(2,1)S(1)} %constant_dynamic-update-slice_fusion.refs_0_.refs_1_), channel_id=1, source_target_pairs={{0,16},{16,0},{1,17},{17,1},{2,18},{18,2},{3,19},{19,3},{4,20},{20... | collective-permute-start | bytes 1327112 | tf_op jit(solution)/shard_map/ppermute | solution.py:36
  22.5 22.7 %collective-permute-start.5 = (bf16[12,144,128]{2,1,0:T(8,128)(2,1)S(1)}, bf16[12,144,128]{2,1,0:T(8,128)(2,1)S(1)}, u32[]{:S(2)}, u32[]{:S(2)}) collective-permute-start(bf16[12,144,128]{2,1,0:T(8,128)(2,1)S(1)} %constant_dynamic-update-slice_fusion.refs_0_.refs_1_), channel_id=1, source_target_pairs={{0,4},{4,8},{8,12},{12,0},{1,5},{5,9},{9,13},{13,1},{2,6},{6,10},{... | collective-permute-start | bytes 1327112 | tf_op jit(solution)/shard_map/ppermute | solution.py:38
  22.6 22.6 %collective-permute-start.3 = (bf16[12,144,128]{2,1,0:T(8,128)(2,1)S(1)}, bf16[12,144,128]{2,1,0:T(8,128)(2,1)S(1)}, u32[]{:S(2)}, u32[]{:S(2)}) collective-permute-start(bf16[12,144,128]{2,1,0:T(8,128)(2,1)S(1)} %constant_dynamic-update-slice_fusion.refs_0_.refs_1_), channel_id=1, source_target_pairs={{0,12},{4,0},{8,4},{12,8},{1,13},{5,1},{9,5},{13,9},{2,14},{6,2},{... | collective-permute-start | bytes 1327112 | tf_op jit(solution)/shard_map/ppermute | solution.py:36
  32.4 12.8 %collective-permute-start.6 = (bf16[12,144,128]{2,1,0:T(8,128)(2,1)S(1)}, bf16[12,144,128]{2,1,0:T(8,128)(2,1)S(1)}, u32[]{:S(2)}, u32[]{:S(2)}) collective-permute-start(bf16[12,144,128]{2,1,0:T(8,128)(2,1)S(1)} %collective-permute-done.2.refs_1_.refs_2_), channel_id=1, source_target_pairs={{0,4},{4,8},{8,12},{12,0},{1,5},{5,9},{9,13},{13,1},{2,6},{6,10},{... | collective-permute-start | bytes 1327112 | tf_op jit(solution)/shard_map/ppermute | solution.py:38
  32.4 12.8 %collective-permute-start.4 = (bf16[12,144,128]{2,1,0:T(8,128)(2,1)S(1)}, bf16[12,144,128]{2,1,0:T(8,128)(2,1)}, u32[]{:S(2)}, u32[]{:S(2)}) collective-permute-start(bf16[12,144,128]{2,1,0:T(8,128)(2,1)S(1)} %collective-permute-done.2.refs_1_.refs_2_), channel_id=1, source_target_pairs={{0,12},{4,0},{8,4},{12,8},{1,13},{5,1},{9,5},{13,9},{2,14},{6,2},{... | collective-permute-start | bytes 1327112 | tf_op jit(solution)/shard_map/ppermute | solution.py:36
  61.3 3.9 %collective-permute-start.8 = (f32[2,3,4,512]{3,2,1,0:T(4,128)S(1)}, f32[2,3,4,512]{3,2,1,0:T(4,128)S(1)}, u32[]{:S(2)}, u32[]{:S(2)}) collective-permute-start(f32[2,3,4,512]{3,2,1,0:T(4,128)S(1)} %bitcast.97), channel_id=1, source_target_pairs={{0,12},{4,0},{8,4},{12,8},{1,13},{5,1},{9,5},{13,9},{2,14},{6,2},{... | collective-permute-start | bytes 147464 | tf_op jit(solution)/shard_map/ppermute | solution.py:45
  63.5 3.5 %collective-permute-start.7 = (f32[2,3,4,512]{3,2,1,0:T(4,128)S(1)}, f32[2,3,4,512]{3,2,1,0:T(4,128)S(1)}, u32[]{:S(2)}, u32[]{:S(2)}) collective-permute-start(f32[2,3,4,512]{3,2,1,0:T(4,128)S(1)} %bitcast.96), channel_id=1, source_target_pairs={{0,4},{4,8},{8,12},{12,0},{1,5},{5,9},{9,13},{13,1},{2,6},{6,10},{... | collective-permute-start | bytes 147464 | tf_op jit(solution)/shard_map/ppermute | solution.py:43
  67.1 10.2 %collective-permute-start.9 = (f32[3,4,512]{2,1,0:T(4,128)S(1)}, f32[3,4,512]{2,1,0:T(4,128)S(1)}, u32[]{:S(2)}, u32[]{:S(2)}) collective-permute-start(f32[3,4,512]{2,1,0:T(4,128)S(1)} %slice_bitcast_fusion.4), channel_id=1, source_target_pairs={{0,16},{16,0},{1,17},{17,1},{2,18},{18,2},{3,19},{19,3},{4,20},{20... | collective-permute-start | bytes 73736 | tf_op jit(solution)/shard_map/ppermute | solution.py:43
  77.2 5.5 %collective-permute-start.10 = (f32[4,512]{1,0:T(4,128)S(1)}, f32[4,512]{1,0:T(4,128)S(1)}, u32[]{:S(2)}, u32[]{:S(2)}) collective-permute-start(f32[4,512]{1,0:T(4,128)S(1)} %get-tuple-element.37), channel_id=1, source_target_pairs={{0,1},{1,2},{2,3},{3,0},{4,5},{5,6},{6,7},{7,4},{8,9},{9,10},{10,1... | collective-permute-start | bytes 24584 | tf_op jit(solution)/shard_map/ppermute | solution.py:43
  81.2 3.7 %collective-permute-start.11 = (f32[4,512]{1,0:T(4,128)S(1)}, f32[4,512]{1,0:T(4,128)S(1)}, u32[]{:S(2)}, u32[]{:S(2)}) collective-permute-start(f32[4,512]{1,0:T(4,128)S(1)} %get-tuple-element.38), channel_id=1, source_target_pairs={{0,3},{1,0},{2,1},{3,2},{4,7},{5,4},{6,5},{7,6},{8,11},{9,8},{10,9... | collective-permute-start | bytes 24584 | tf_op jit(solution)/shard_map/ppermute | solution.py:45
